TPU v7x, 128 devices: a whole 4x4x4 slice. The times are simulated.
128 devices in a mesh: half: 2 (over z_hi), row: 8 (over x, core), col: 8 (over z_lo, y).
Axes of the slice: x: 4, y: 4, z: 4 (z_hi: 2, z_lo: 2; z = z_hi * 2 + z_lo), core: 2. Of those that a mesh axis runs over, the one named last changes fastest.
Arguments:
- front: bfloat16 [2, 16384, 16384], P('half', 'row', 'col'), may hold values from -6 to 6, as said below
- panel: bfloat16 [2, 16384, 1024], P('half', 'row', 'col'), may hold values from -2.5 to 2.5
- inverse_block: bfloat16 [2, 1024, 1024], P('half', None, 'col'), as said below
- child_maps: int32 [2, 16384], replicated, may hold values from 0 to 16383, as said below
- root_front: bfloat16 [16384, 16384], P(('half', 'row'), 'col'), may hold values from -6 to 6, as said below
Outputs:
- root_sum: float32 [16384, 16384], P(('half', 'row'), 'col')
Inputs may be any that keep to these rules, and one draw needn't show every extreme that they name: `child_maps`: each row is a permutation of the 16384 root indices. For each child, in every aligned block of 2048 positions, the k-th aligned run of 128 positions maps into the k-th aligned block of 1024 root indices. `inverse_block`: each matrix is lower triangular with a positive diagonal. `front`: each child's matrix is symmetric. `root_front`: the matrix is symmetric.
All inputs are finite; a program needn't handle non-finite values.
Results may differ from a plain program's by a relative error of at most 0.0041.
Values may be sent and summed in bfloat16 or wider, within the bound.
No kernel may reach another device: no remote copies, remote signals or barrier semaphores. Data moves between devices by JAX's collectives and lax.ppermute only.
A program may use at most 128 MiB of HBM per device.

v0:
```python
import jax
import jax.numpy as jnp
from jax import lax
from jax.experimental import pallas as pl
from jax.experimental.pallas import tpu as pltpu
from jax.sharding import PartitionSpec as P

ALL = ("half", "row", "col")
BF16 = jnp.bfloat16
F32 = jnp.float32
VMEM_LIMIT = 58 * 1024 * 1024
ROWS_AXIS = (((1,), (1,)), ((), ()))


def shift(array, move):
    pairs = []
    for half in range(2):
        for row in range(8):
            for col in range(8):
                h, r, c = move(half, row, col)
                pairs.append(((half * 8 + row) * 8 + col, (h * 8 + r) * 8 + c))
    return lax.ppermute(array, ALL, pairs)


LOWER_STEPS = 4
LOWER_ROWS = 512


def schur_kernel(
    place_ref,
    rows_ref,
    mine_ref,
    other_ref,
    inverse_mine_ref,
    inverse_other_ref,
    front_ref,
    out_ref,
    inverse_ref,
    wide_ref,
    left_ref,
    right_ref,
):
    step = pl.program_id(0)
    x, core = place_ref[0], place_ref[1]

    @pl.when(step == 0)
    def _():
        for ref, part in ((inverse_mine_ref, core), (inverse_other_ref, 1 - core)):
            for chunk in range(8):
                inverse_ref[
                    pl.ds(pl.multiple_of(part * 512, 512), 512),
                    chunk * 128 : (chunk + 1) * 128,
                ] = ref[chunk]

    def lower(out):
        for n in range(4):
            reach = (n + 1) * 256
            out(
                n,
                lax.dot_general(
                    wide_ref[:, :reach],
                    inverse_ref[n * 256 : reach, :reach],
                    ROWS_AXIS,
                    preferred_element_type=F32,
                ).astype(BF16),
            )

    @pl.when(step < LOWER_STEPS)
    def _():
        span = pl.ds(pl.multiple_of(step * LOWER_ROWS, LOWER_ROWS), LOWER_ROWS)

        def to_left(n, value):
            left_ref[span, n * 256 : (n + 1) * 256] = value

        def to_right(n, value):
            right_ref[span, n * 256 : (n + 1) * 256] = value

        for chunk in range(8):
            wide_ref[:, chunk * 128 : (chunk + 1) * 128] = rows_ref[chunk]
        lower(to_left)
        for ref, part in ((mine_ref, core), (other_ref, 1 - core)):
            for index, away in enumerate((0, 3, 1, 2)):
                chunk = ((x + away) % 4) * 2 + part
                wide_ref[:, pl.ds(pl.multiple_of(chunk * 128, 128), 128)] = ref[index]
        lower(to_right)

    @pl.when(step >= LOWER_STEPS)
    def _():
        at = step - LOWER_STEPS
        block = right_ref[pl.ds(pl.multiple_of(at * 256, 256), 256), :]
        for part in range(4):
            rows = slice(part * 512, (part + 1) * 512)
            product = lax.dot_general(
                left_ref[rows, :], block, ROWS_AXIS, preferred_element_type=F32
            )
            schur = (front_ref[rows, :].astype(F32) - product).astype(BF16)
            for k in range(4):
                out_ref[part * 4 + k, 0] = schur[k * 128 : (k + 1) * 128]


def schur_parcels(place, rows, mine, other, inverse_mine, inverse_other, front):
    def early(step, place):
        return jnp.minimum(step, LOWER_STEPS - 1)

    def late(step, place):
        return jnp.maximum(step - LOWER_STEPS, 0)

    grid_spec = pltpu.PrefetchScalarGridSpec(
        num_scalar_prefetch=1,
        grid=(LOWER_STEPS + 8,),
        in_specs=[
            pl.BlockSpec((8, LOWER_ROWS, 128), lambda i, s: (0, early(i, s), 0)),
            pl.BlockSpec((4, LOWER_ROWS, 128), lambda i, s: (0, early(i, s), 0)),
            pl.BlockSpec((4, LOWER_ROWS, 128), lambda i, s: (0, early(i, s), 0)),
            pl.BlockSpec((8, 512, 128), lambda i, s: (0, 0, 0)),
            pl.BlockSpec((8, 512, 128), lambda i, s: (0, 0, 0)),
            pl.BlockSpec((2048, 256), lambda i, s: (0, late(i, s))),
        ],
        out_specs=pl.BlockSpec((16, 1, 128, 256), lambda i, s: (0, late(i, s), 0, 0)),
        scratch_shapes=[
            pltpu.VMEM((1024, 1024), BF16),
            pltpu.VMEM((LOWER_ROWS, 1024), BF16),
            pltpu.VMEM((2048, 1024), BF16),
            pltpu.VMEM((2048, 1024), BF16),
        ],
    )
    return pl.pallas_call(
        schur_kernel,
        grid_spec=grid_spec,
        out_shape=jax.ShapeDtypeStruct((16, 8, 128, 256), BF16),
        compiler_params=pltpu.CompilerParams(vmem_limit_bytes=VMEM_LIMIT),
        cost_estimate=pl.CostEstimate(
            flops=14 << 30, bytes_accessed=26 << 20, transcendentals=0
        ),
        name="schur",
    )(place, rows, mine, other, inverse_mine, inverse_other, front)


def place_kernel(
    place_ref, schur_in_ref, row_map_ref, col_map_ref, base_ref, out_ref, schur_ref
):
    b, child = pl.program_id(0), pl.program_id(1)
    for r in range(8):
        for c in range(8):
            schur_ref[r * 128 : (r + 1) * 128, c * 128 : (c + 1) * 128] = schur_in_ref[
                r * 8 + c
            ]
    row_ids = lax.broadcasted_iota(jnp.int32, (1024, 1024), 0)
    col_ids = lax.broadcasted_iota(jnp.int32, (1024, 1024), 1)
    row_pick = jnp.where(row_map_ref[0] == row_ids, 1.0, 0.0).astype(BF16)
    col_pick = jnp.where(col_map_ref[0, 0] == col_ids, 1.0, 0.0).astype(BF16)
    rowed = jnp.dot(row_pick, schur_ref[...], preferred_element_type=F32).astype(BF16)
    placed = jnp.dot(rowed, col_pick, preferred_element_type=F32)

    @pl.when(child == 0)
    def _():
        out_ref[...] = base_ref[...].astype(F32) + placed

    @pl.when(child == 1)
    def _():
        rows = row_ids + place_ref[2] * 1024
        cols = col_ids + (place_ref[3] * 2048 + b * 1024)
        out_ref[...] = jnp.where(rows >= cols, out_ref[...] + placed, 0.0)


def place_children(place, arrived, row_maps, col_maps, base):
    grid_spec = pltpu.PrefetchScalarGridSpec(
        num_scalar_prefetch=1,
        grid=(2, 2),
        in_specs=[
            pl.BlockSpec((64, 128, 128), lambda b, c, s: (c, 0, b)),
            pl.BlockSpec((1, 1, 1024), lambda b, c, s: (c, 0, 0)),
            pl.BlockSpec((1, 1, 1024, 1), lambda b, c, s: (c, b, 0, 0)),
            pl.BlockSpec((1024, 1024), lambda b, c, s: (0, b)),
        ],
        out_specs=pl.BlockSpec((1024, 1024), lambda b, c, s: (0, b)),
        scratch_shapes=[pltpu.VMEM((1024, 1024), BF16)],
    )
    return pl.pallas_call(
        place_kernel,
        grid_spec=grid_spec,
        out_shape=jax.ShapeDtypeStruct((1024, 2048), F32),
        compiler_params=pltpu.CompilerParams(vmem_limit_bytes=VMEM_LIMIT),
        cost_estimate=pl.CostEstimate(
            flops=16 << 30, bytes_accessed=20 << 20, transcendentals=0
        ),
        name="place",
    )(place, arrived, row_maps, col_maps, base)


def body(front, panel, inverse_block, child_maps, root_front):
    half = lax.axis_index("half")
    row = lax.axis_index("row")
    col = lax.axis_index("col")
    x, core = row // 2, row % 2
    target = half * 8 + row
    place = jnp.stack([x, core, target, col]).astype(jnp.int32)

    rows = lax.all_gather(panel[0], "col", axis=0)
    turned = shift(panel[0], lambda h, r, c: (h, c, r))
    inverse_share = lax.dynamic_slice_in_dim(inverse_block[0], core * 512, 512, 0)
    inverse_mine = lax.all_to_all(
        jnp.broadcast_to(inverse_share, (8, 512, 128)), "col", 0, 0, tiled=True
    )
    turned, inverse_mine = lax.optimization_barrier((turned, inverse_mine))
    inverse_other = shift(inverse_mine, lambda h, r, c: (h, r ^ 1, c))
    mine = jnp.stack(
        [
            turned,
            shift(turned, lambda h, r, c: (h, (r + 2) % 8, c)),
            shift(turned, lambda h, r, c: (h, (r + 6) % 8, c)),
            shift(turned, lambda h, r, c: (h, (r + 4) % 8, c)),
        ]
    )
    other = shift(mine, lambda h, r, c: (h, r ^ 1, c))

    parcels = schur_parcels(
        place, rows, mine, other, inverse_mine, inverse_other, front[0]
    )
    arrived = lax.all_to_all(
        parcels.reshape(128, 128, 256), ALL, split_axis=0, concat_axis=0, tiled=True
    )

    maps = child_maps.reshape(2, 8, 16, 128)
    row_maps = (
        lax.dynamic_index_in_dim(maps, target, 2, keepdims=False).reshape(2, 1, 1024)
        - target * 1024
    )
    col_maps = lax.dynamic_slice_in_dim(maps, 2 * col, 2, 2).transpose(0, 2, 1, 3)
    col_maps = col_maps - (2 * col + jnp.arange(2, dtype=jnp.int32))[None, :, None, None] * 1024
    return place_children(
        place, arrived, row_maps, col_maps.reshape(2, 2, 1024, 1), root_front
    )


def solution(mesh):
    return jax.shard_map(
        body,
        mesh=mesh,
        in_specs=(
            P("half", "row", "col"),
            P("half", "row", "col"),
            P("half", None, "col"),
            P(),
            P(("half", "row"), "col"),
        ),
        out_specs=P(("half", "row"), "col"),
        check_vma=False,
    )
```

profile of v0, /device:TPU:1, one launch (start us, length us, event | category | flops | bytes accessed | tf_op | source)
XLA Modules:
  0.0 269.0 jit_solution(14705340565243735217)
XLA Ops:
  6.5 0.0 copy-start
  6.5 0.0 copy-start.3
  6.5 0.0 all-gather.2.cloned.1.call-start
  6.5 0.7 all-gather.2.cloned.1.call-update
  7.3 0.2 copy-done
  7.5 1.1 broadcast_in_dim.4
  8.6 6.4 %all-to-all-start = ((bf16[8,512,128]{2,1,0:T(8,128)(2,1)}), bf16[8,512,128]{2,1,0:T(8,128)(2,1)S(1)}, u32[]{:S(2)}, u32[]{:S(2)}) async-start(bf16[8,512,128]{2,1,0:T(8,128)(2,1)} %broadcast_in_dim.4), calls=%async_computation | async-start | bytes 2097152 | tf_op jit(solution)/shard_map/all_to_all | solution.py:202
  15.0 0.0 copy-done.3
  15.0 4.5 %collective-permute-start = (bf16[2048,128]{1,0:T(8,128)(2,1)S(1)}, bf16[2048,128]{1,0:T(8,128)(2,1)}, u32[]{:S(2)}, u32[]{:S(2)}) collective-permute-start(bf16[2048,128]{1,0:T(8,128)(2,1)S(1)} %bitcast.23), channel_id=1, source_target_pairs={{0,0},{1,8},{2,16},{3,24},{4,32},{5,40},{6,48},{7,56},{8,1},{9,9},... | collective-permute-start | bytes 1572872 | tf_op jit(solution)/shard_map/ppermute | solution.py:22
  19.5 60.3 %collective-permute-done = bf16[2048,128]{1,0:T(8,128)(2,1)} collective-permute-done((bf16[2048,128]{1,0:T(8,128)(2,1)S(1)}, bf16[2048,128]{1,0:T(8,128)(2,1)}, u32[]{:S(2)}, u32[]{:S(2)}) %collective-permute-start) | collective-permute-done | bytes 524320 | tf_op jit(solution)/shard_map/ppermute | solution.py:22
  79.7 0.0 all-to-all-done.inverse_mine_ref
  79.7 0.0 copy-start.2
  79.7 0.0 collective-permute-start.1
  79.7 2.7 collective-permute-start.2
  82.4 0.0 collective-permute-start.3
  82.4 12.8 %collective-permute-done.1 = bf16[2048,128]{1,0:T(8,128)(2,1)S(1)} collective-permute-done((bf16[2048,128]{1,0:T(8,128)(2,1)}, bf16[2048,128]{1,0:T(8,128)(2,1)S(1)}, u32[]{:S(2)}, u32[]{:S(2)}) %collective-permute-start.1) | collective-permute-done | bytes 524320 | tf_op jit(solution)/shard_map/ppermute | solution.py:22
  95.2 0.0 collective-permute-done.2
  95.2 0.0 collective-permute-done.3
  95.2 1.3 pad_maximum_fusion.mine_ref
  96.5 0.0 copy-start.1
  96.5 0.1 collective-permute-start.4
  96.6 0.0 copy-done.2
  96.6 0.5 collective-permute-start.5
  97.1 0.6 pad_add_fusion.place_ref
  97.8 4.6 %collective-permute-done.5.inverse_other_ref = bf16[8,512,128]{2,1,0:T(8,128)(2,1)} collective-permute-done((bf16[8,512,128]{2,1,0:T(8,128)(2,1)S(1)}, bf16[8,512,128]{2,1,0:T(8,128)(2,1)}, u32[]{:S(2)}, u32[]{:S(2)}) %collective-permute-start.5) | collective-permute-done | bytes 1048608 | tf_op jit(solution)/shard_map/ppermute | solution.py:22
  102.4 0.0 collective-permute-done.4.other_ref
  102.4 0.0 all-gather.2.cloned.1.call-done.rows_ref
  102.4 0.0 copy-done.1
  102.4 24.4 %schur.1 = bf16[16,8,128,256]{3,2,1,0:T(8,128)(2,1)} custom-call(s32[4]{0:T(128)} %pad_add_fusion.place_ref, bf16[8,2048,128]{2,1,0:T(8,128)(2,1)} %all-gather.2.cloned.1.call-done.rows_ref, bf16[4,2048,128]{2,1,0:T(8,128)(2,1)} %copy-done.1, bf16[4,2048,128]{2,1,0:T(8,128)(2,1)} %collective-permute-done.4.other_ref, bf16[8,512,128]{2,1,0:T(8,128)(2,1)} %copy-done.2, ...), custom_call_target="tpu_custom_call" | custom-call | flops 15032385536 | bytes 27262976 | tf_op jit(solution)/shard_map/schur/pallas_call | solution.py:127
  126.8 0.0 copy-start.4
  126.8 7.8 %all-to-all-start.1 = ((bf16[128,128,256]{2,1,0:T(8,128)(2,1)}), bf16[128,128,256]{2,1,0:T(8,128)(2,1)}, u32[]{:S(2)}, u32[]{:S(2)}) async-start(bf16[128,128,256]{2,1,0:T(8,128)(2,1)} %bitcast.22), calls=%async_computation.1 | async-start | bytes 16777216 | tf_op jit(solution)/shard_map/all_to_all | solution.py:220
  134.6 0.0 copy-done.4
  134.7 0.1 fusion
  134.8 3.3 %reshape.35.col_map_ref = s32[2,2,1024,1]{3,2,1,0:T(8,128)} reshape(s32[2,2,8,128]{3,2,1,0:T(8,128)S(1)} %fusion) | data formatting | bytes 32768 | tf_op jit(solution)/shard_map/reshape | solution.py:232
  138.1 0.6 broadcast_subtract_fusion
  138.7 97.7 %all-to-all-done.1.schur_in_ref = bf16[128,128,256]{2,1,0:T(8,128)(2,1)} async-done(((bf16[128,128,256]{2,1,0:T(8,128)(2,1)}), bf16[128,128,256]{2,1,0:T(8,128)(2,1)}, u32[]{:S(2)}, u32[]{:S(2)}) %all-to-all-start.1) | async-done | bytes 8388640 | tf_op jit(solution)/shard_map/all_to_all | solution.py:220
  236.4 25.7 %place.1 = f32[1024,2048]{1,0:T(8,128)} custom-call(s32[4]{0:T(128)} %pad_add_fusion.place_ref, bf16[128,128,256]{2,1,0:T(8,128)(2,1)} %all-to-all-done.1.schur_in_ref, s32[2,1,1024]{2,1,0:T(1,128)} %bitcast.31, s32[2,2,1024,1]{3,2,1,0:T(8,128)} %reshape.35.col_map_ref, bf16[1024,2048]{1,0:T(8,128)(2,1)} %base_ref.1), custom_call_target="tpu_custom_call" | custom-call | flops 17179869184 | bytes 20971520 | tf_op jit(solution)/shard_map/place/pallas_call | solution.py:179
  (5 shorter events, 0.1 us)
Async XLA Ops:
  6.5 1.0 copy-start
  6.5 8.4 %copy-start.3 = (bf16[1,2048,128]{2,1,0:T(8,128)(2,1)S(1)}, bf16[1,2048,128]{2,1,0:T(8,128)(2,1)}, u32[]{:S(2)}) copy-start(bf16[1,2048,128]{2,1,0:T(8,128)(2,1)} %param.6) | copy-start | bytes 1572868
  6.5 95.9 %all-gather.2.cloned.1.call-start = ((), (), s32[]{:S(2)}) async-start(), calls=%async_computation.2 | async-start | bytes 4718592 | tf_op jit(solution)/shard_map/all_gather | solution.py:199
  8.6 71.1 %all-to-all-start = ((bf16[8,512,128]{2,1,0:T(8,128)(2,1)}), bf16[8,512,128]{2,1,0:T(8,128)(2,1)S(1)}, u32[]{:S(2)}, u32[]{:S(2)}) async-start(bf16[8,512,128]{2,1,0:T(8,128)(2,1)} %broadcast_in_dim.4), calls=%async_computation | async-start | bytes 2097152 | tf_op jit(solution)/shard_map/all_to_all | solution.py:202
  15.0 64.7 %collective-permute-start = (bf16[2048,128]{1,0:T(8,128)(2,1)S(1)}, bf16[2048,128]{1,0:T(8,128)(2,1)}, u32[]{:S(2)}, u32[]{:S(2)}) collective-permute-start(bf16[2048,128]{1,0:T(8,128)(2,1)S(1)} %bitcast.23), channel_id=1, source_target_pairs={{0,0},{1,8},{2,16},{3,24},{4,32},{5,40},{6,48},{7,56},{8,1},{9,9},... | collective-permute-start | bytes 1572872 | tf_op jit(solution)/shard_map/ppermute | solution.py:22
  79.7 16.9 %copy-start.2 = (bf16[8,512,128]{2,1,0:T(8,128)(2,1)}, bf16[8,512,128]{2,1,0:T(8,128)(2,1)S(1)}, u32[]{:S(2)}) copy-start(bf16[8,512,128]{2,1,0:T(8,128)(2,1)S(1)} %all-to-all-done.inverse_mine_ref) | copy-start | bytes 3145732
  79.7 15.5 %collective-permute-start.1 = (bf16[2048,128]{1,0:T(8,128)(2,1)}, bf16[2048,128]{1,0:T(8,128)(2,1)S(1)}, u32[]{:S(2)}, u32[]{:S(2)}) collective-permute-start(bf16[2048,128]{1,0:T(8,128)(2,1)} %collective-permute-done), channel_id=1, source_target_pairs={{0,16},{1,17},{2,18},{3,19},{4,20},{5,21},{6,22},{7,23},{8,24},{9,... | collective-permute-start | bytes 1572872 | tf_op jit(solution)/shard_map/ppermute | solution.py:22
  79.7 15.5 %collective-permute-start.2 = (bf16[2048,128]{1,0:T(8,128)(2,1)}, bf16[2048,128]{1,0:T(8,128)(2,1)S(1)}, u32[]{:S(2)}, u32[]{:S(2)}) collective-permute-start(bf16[2048,128]{1,0:T(8,128)(2,1)} %collective-permute-done), channel_id=1, source_target_pairs={{0,48},{1,49},{2,50},{3,51},{4,52},{5,53},{6,54},{7,55},{8,56},{9,... | collective-permute-start | bytes 1572872 | tf_op jit(solution)/shard_map/ppermute | solution.py:22
  82.4 12.8 %collective-permute-start.3 = (bf16[2048,128]{1,0:T(8,128)(2,1)}, bf16[2048,128]{1,0:T(8,128)(2,1)S(1)}, u32[]{:S(2)}, u32[]{:S(2)}) collective-permute-start(bf16[2048,128]{1,0:T(8,128)(2,1)} %collective-permute-done), channel_id=1, source_target_pairs={{0,32},{1,33},{2,34},{3,35},{4,36},{5,37},{6,38},{7,39},{8,40},{9,... | collective-permute-start | bytes 1572872 | tf_op jit(solution)/shard_map/ppermute | solution.py:22
  96.5 5.9 %copy-start.1 = (bf16[4,2048,128]{2,1,0:T(8,128)(2,1)}, bf16[4,2048,128]{2,1,0:T(8,128)(2,1)S(1)}, u32[]{:S(2)}) copy-start(bf16[4,2048,128]{2,1,0:T(8,128)(2,1)S(1)} %pad_maximum_fusion.mine_ref) | copy-start | bytes 6291460
  96.5 5.9 %collective-permute-start.4 = (bf16[4,2048,128]{2,1,0:T(8,128)(2,1)S(1)}, bf16[4,2048,128]{2,1,0:T(8,128)(2,1)}, u32[]{:S(2)}, u32[]{:S(2)}) collective-permute-start(bf16[4,2048,128]{2,1,0:T(8,128)(2,1)S(1)} %pad_maximum_fusion.mine_ref), channel_id=1, source_target_pairs={{0,8},{1,9},{2,10},{3,11},{4,12},{5,13},{6,14},{7,15},{8,0},{9,1},... | collective-permute-start | bytes 6291464 | tf_op jit(solution)/shard_map/ppermute | solution.py:22
  96.6 5.8 %collective-permute-start.5 = (bf16[8,512,128]{2,1,0:T(8,128)(2,1)S(1)}, bf16[8,512,128]{2,1,0:T(8,128)(2,1)}, u32[]{:S(2)}, u32[]{:S(2)}) collective-permute-start(bf16[8,512,128]{2,1,0:T(8,128)(2,1)S(1)} %all-to-all-done.inverse_mine_ref), channel_id=1, source_target_pairs={{0,8},{1,9},{2,10},{3,11},{4,12},{5,13},{6,14},{7,15},{8,0},{9,1},... | collective-permute-start | bytes 3145736 | tf_op jit(solution)/shard_map/ppermute | solution.py:22
  126.8 7.8 %copy-start.4 = (s32[2,16384]{1,0:T(2,128)S(1)}, s32[2,16384]{1,0:T(2,128)}, u32[]{:S(2)}) copy-start(s32[2,16384]{1,0:T(2,128)} %param.8) | copy-start | bytes 393220
  126.8 109.6 %all-to-all-start.1 = ((bf16[128,128,256]{2,1,0:T(8,128)(2,1)}), bf16[128,128,256]{2,1,0:T(8,128)(2,1)}, u32[]{:S(2)}, u32[]{:S(2)}) async-start(bf16[128,128,256]{2,1,0:T(8,128)(2,1)} %bitcast.22), calls=%async_computation.1 | async-start | bytes 16777216 | tf_op jit(solution)/shard_map/all_to_all | solution.py:220
Sparse Core Ops, SparseCore 0:
  9.0 91.3 all-gather.1
where the time goes:
time: 272 us; the launch traced here: 269 us
  waiting for transfers between devices  176 us (65%)
  Pallas kernels  50.2 us (18%)
  starting transfers between devices  21.9 us (8%)
  between operations  13.5 us (5%)
  local copies, waits for them, and re-layouts  4.71 us (2%)
    all_to_all x1, waiting for transfers between devices, body(): lax.all_to_all(parcels.reshape(128, 128, 256), ALL, split_axis=0, concat_...  97.7 us
    ppermute x6, waiting for transfers between devices, shift(): return lax.ppermute(array, ALL, pairs)  77.7 us
    pallas_call x1, Pallas kernels, place_children(): pl.pallas_call(place_kernel, grid_spec=grid_spec, out_shape=jax.ShapeDtyp...  25.7 us
    pallas_call x1, Pallas kernels, schur_parcels(): pl.pallas_call(schur_kernel, grid_spec=grid_spec, out_shape=jax.ShapeDtyp...  24.4 us
    all_to_all x1, starting transfers between devices, body(): lax.all_to_all(parcels.reshape(128, 128, 256), ALL, split_axis=0, concat_...  7.8 us
    ppermute x6, starting transfers between devices, shift(): return lax.ppermute(array, ALL, pairs)  7.73 us
    all_to_all x1, starting transfers between devices, body(): lax.all_to_all(jnp.broadcast_to(inverse_share, (8, 512, 128)), 'col', 0,...  6.37 us
  transfers between devices with their start and end apart: 9, of which 4 were waited for; matrix products, arithmetic and copies ran while one was open for 3% of the time, Pallas kernels for 0%

commit v1 on v0

v1 whole, which is shorter than its diff:
```python
import functools

import jax
import jax.numpy as jnp
from jax import lax
from jax.experimental import pallas as pl
from jax.experimental.pallas import tpu as pltpu
from jax.sharding import PartitionSpec as P

ALL = ("half", "row", "col")
BF16 = jnp.bfloat16
F32 = jnp.float32
VMEM_LIMIT = 58 * 1024 * 1024
ROWS_AXIS = (((1,), (1,)), ((), ()))


def shift(array, move):
    pairs = []
    for half in range(2):
        for row in range(8):
            for col in range(8):
                h, r, c = move(half, row, col)
                pairs.append(((half * 8 + row) * 8 + col, (h * 8 + r) * 8 + c))
    return lax.ppermute(array, ALL, pairs)


LOWER_ROWS = 512


def lower_kernel(
    place_ref,
    rows_ref,
    mine_ref,
    other_ref,
    inverse_mine_ref,
    inverse_other_ref,
    left_ref,
    right_ref,
    inverse_ref,
    wide_ref,
):
    x, core = place_ref[0], place_ref[1]

    @pl.when(pl.program_id(0) == 0)
    def _():
        for ref, part in ((inverse_mine_ref, core), (inverse_other_ref, 1 - core)):
            for chunk in range(8):
                inverse_ref[
                    pl.ds(pl.multiple_of(part * 512, 512), 512),
                    chunk * 128 : (chunk + 1) * 128,
                ] = ref[chunk]

    def lower(out_ref):
        for n in range(4):
            reach = (n + 1) * 256
            out_ref[:, n * 256 : reach] = lax.dot_general(
                wide_ref[:, :reach],
                inverse_ref[n * 256 : reach, :reach],
                ROWS_AXIS,
                preferred_element_type=F32,
            ).astype(BF16)

    for chunk in range(8):
        wide_ref[:, chunk * 128 : (chunk + 1) * 128] = rows_ref[chunk]
    lower(left_ref)
    for ref, part in ((mine_ref, core), (other_ref, 1 - core)):
        for index, away in enumerate((0, 3, 1, 2)):
            chunk = ((x + away) % 4) * 2 + part
            wide_ref[:, pl.ds(pl.multiple_of(chunk * 128, 128), 128)] = ref[index]
    lower(right_ref)


def lower_rows(place, packet, mine, other, inverse_other):
    out = jax.ShapeDtypeStruct((2048, 1024), BF16)
    grid_spec = pltpu.PrefetchScalarGridSpec(
        num_scalar_prefetch=1,
        grid=(2048 // LOWER_ROWS,),
        in_specs=[
            pl.BlockSpec((8, LOWER_ROWS, 128), lambda i, s: (0, i, 0)),
            pl.BlockSpec((4, LOWER_ROWS, 128), lambda i, s: (0, i, 0)),
            pl.BlockSpec((4, LOWER_ROWS, 128), lambda i, s: (0, i, 0)),
            pl.BlockSpec((8, 512, 128), lambda i, s: (0, 4, 0)),
            pl.BlockSpec((8, 512, 128), lambda i, s: (0, 0, 0)),
        ],
        out_specs=[pl.BlockSpec((LOWER_ROWS, 1024), lambda i, s: (i, 0))] * 2,
        scratch_shapes=[
            pltpu.VMEM((1024, 1024), BF16),
            pltpu.VMEM((LOWER_ROWS, 1024), BF16),
        ],
    )
    return pl.pallas_call(
        lower_kernel,
        grid_spec=grid_spec,
        out_shape=[out, out],
        compiler_params=pltpu.CompilerParams(vmem_limit_bytes=VMEM_LIMIT),
        cost_estimate=pl.CostEstimate(
            flops=5 << 30, bytes_accessed=18 << 20, transcendentals=0
        ),
        name="lower",
    )(place, packet, mine, other, packet, inverse_other)


def schur_kernel(left_ref, right_ref, front_even_ref, front_odd_ref, out_ref):
    block = right_ref[...].reshape(256, 1024)
    for part in range(4):
        rows = slice(part * 512, (part + 1) * 512)
        product = lax.dot_general(
            left_ref[rows, :], block, ROWS_AXIS, preferred_element_type=F32
        )
        for which, front_ref in enumerate((front_even_ref, front_odd_ref)):
            lanes = slice(which * 128, (which + 1) * 128)
            schur = (front_ref[rows, :].astype(F32) - product[:, lanes]).astype(BF16)
            for k in range(4):
                out_ref[part * 4 + k, which] = schur[k * 128 : (k + 1) * 128]


def schur_parcels(b, left, right, front):
    return pl.pallas_call(
        schur_kernel,
        grid=(4,),
        in_specs=[
            pl.BlockSpec((2048, 1024), lambda i: (0, 0)),
            pl.BlockSpec((2, 1, 128, 1024), lambda i: (i, b, 0, 0)),
            pl.BlockSpec((2048, 128), lambda i: (0, 4 * i + b)),
            pl.BlockSpec((2048, 128), lambda i: (0, 4 * i + 2 + b)),
        ],
        out_specs=pl.BlockSpec((16, 2, 128, 128), lambda i: (0, i, 0, 0)),
        out_shape=jax.ShapeDtypeStruct((16, 8, 128, 128), BF16),
        compiler_params=pltpu.CompilerParams(vmem_limit_bytes=VMEM_LIMIT),
        cost_estimate=pl.CostEstimate(
            flops=4 << 30, bytes_accessed=14 << 20, transcendentals=0
        ),
        name="schur",
    )(left, right.reshape(8, 2, 128, 1024), front, front)


def place_kernel(
    b, place_ref, schur_in_ref, row_map_ref, col_map_ref, base_ref, *refs
):
    out_ref, schur_ref = refs[-2:]
    child = pl.program_id(0)
    for r in range(8):
        for c in range(8):
            schur_ref[r * 128 : (r + 1) * 128, c * 128 : (c + 1) * 128] = schur_in_ref[
                r * 8 + c
            ]
    row_ids = lax.broadcasted_iota(jnp.int32, (1024, 1024), 0)
    col_ids = lax.broadcasted_iota(jnp.int32, (1024, 1024), 1)
    row_pick = jnp.where(row_map_ref[0] == row_ids, 1.0, 0.0).astype(BF16)
    col_pick = jnp.where(col_map_ref[0, 0] == col_ids, 1.0, 0.0).astype(BF16)
    rowed = jnp.dot(row_pick, schur_ref[...], preferred_element_type=F32).astype(BF16)
    placed = jnp.dot(rowed, col_pick, preferred_element_type=F32)

    @pl.when(child == 0)
    def _():
        out_ref[...] = base_ref[...].astype(F32) + placed

    @pl.when(child == 1)
    def _():
        rows = row_ids + place_ref[2] * 1024
        cols = col_ids + (place_ref[3] * 2048 + b * 1024)
        out_ref[...] = jnp.where(rows >= cols, out_ref[...] + placed, 0.0)


def place_children(b, place, arrived, row_maps, col_maps, base, half_done=None):
    grid_spec = pltpu.PrefetchScalarGridSpec(
        num_scalar_prefetch=1,
        grid=(2,),
        in_specs=[
            pl.BlockSpec((64, 128, 128), lambda c, s: (c, 0, 0)),
            pl.BlockSpec((1, 1, 1024), lambda c, s: (c, 0, 0)),
            pl.BlockSpec((1, 1, 1024, 1), lambda c, s: (c, b, 0, 0)),
            pl.BlockSpec((1024, 1024), lambda c, s: (0, b)),
        ]
        + ([] if half_done is None else [pl.BlockSpec(memory_space=pl.ANY)]),
        out_specs=pl.BlockSpec((1024, 1024), lambda c, s: (0, b)),
        scratch_shapes=[pltpu.VMEM((1024, 1024), BF16)],
    )
    return pl.pallas_call(
        functools.partial(place_kernel, b),
        grid_spec=grid_spec,
        out_shape=jax.ShapeDtypeStruct((1024, 2048), F32),
        input_output_aliases={} if half_done is None else {5: 0},
        compiler_params=pltpu.CompilerParams(vmem_limit_bytes=VMEM_LIMIT),
        cost_estimate=pl.CostEstimate(
            flops=8 << 30, bytes_accessed=10 << 20, transcendentals=0
        ),
        name="place",
    )(
        place,
        arrived,
        row_maps,
        col_maps,
        base,
        *(() if half_done is None else (half_done,)),
    )


def body(front, panel, inverse_block, child_maps, root_front):
    half = lax.axis_index("half")
    row = lax.axis_index("row")
    col = lax.axis_index("col")
    x, core = row // 2, row % 2
    target = half * 8 + row
    place = jnp.stack([x, core, target, col]).astype(jnp.int32)

    turned = shift(panel[0], lambda h, r, c: (h, c, r))
    inverse_share = lax.dynamic_slice_in_dim(inverse_block[0], core * 512, 512, 0)
    packet = jnp.concatenate([panel[0], inverse_share])
    packet = lax.all_to_all(
        jnp.broadcast_to(packet, (8, 2560, 128)), "col", 0, 0, tiled=True
    )
    inverse_other = shift(packet[:, 2048:], lambda h, r, c: (h, r ^ 1, c))
    mine = jnp.stack(
        [
            turned,
            shift(turned, lambda h, r, c: (h, (r + 2) % 8, c)),
            shift(turned, lambda h, r, c: (h, (r + 6) % 8, c)),
            shift(turned, lambda h, r, c: (h, (r + 4) % 8, c)),
        ]
    )
    other = shift(mine, lambda h, r, c: (h, r ^ 1, c))
    left, right = lower_rows(place, packet, mine, other, inverse_other)

    maps = child_maps.reshape(2, 8, 16, 128)
    row_maps = (
        lax.dynamic_index_in_dim(maps, target, 2, keepdims=False).reshape(2, 1, 1024)
        - target * 1024
    )
    col_maps = lax.dynamic_slice_in_dim(maps, 2 * col, 2, 2).transpose(0, 2, 1, 3)
    col_maps = col_maps - (2 * col + jnp.arange(2, dtype=jnp.int32))[None, :, None, None] * 1024
    col_maps = col_maps.reshape(2, 2, 1024, 1)

    out = None
    for b in range(2):
        parcels = schur_parcels(b, left, right, front[0])
        arrived = lax.all_to_all(parcels.reshape(128, 128, 128), ALL, 0, 0, tiled=True)
        out = place_children(b, place, arrived, row_maps, col_maps, root_front, out)
    return out


def solution(mesh):
    return jax.shard_map(
        body,
        mesh=mesh,
        in_specs=(
            P("half", "row", "col"),
            P("half", "row", "col"),
            P("half", None, "col"),
            P(),
            P(("half", "row"), "col"),
        ),
        out_specs=P(("half", "row"), "col"),
        check_vma=False,
    )
```

time: 272 us -> 303 us (1.11)
  waiting for transfers between devices: 176 us -> 199 us
  between operations: 13.5 us -> 0.15 us
  Pallas kernels: 50.2 us -> 62.3 us
  starting transfers between devices: 21.9 us -> 29.7 us
  local copies, waits for them, and re-layouts: 4.71 us -> 9.3 us
    ppermute x6, waiting for transfers between devices: 77.7 us -> 123 us  [shift(): return lax.ppermute(array, ALL, pairs)]
    all_to_all x2 -> x3, waiting for transfers between devices: 97.7 us -> 75.8 us  [the longest x2 75.8 us: body(): lax.all_to_all(parcels.reshape(128, 128, 128), ALL, 0, 0, tiled=True)]
    pallas_call x2 -> x5, Pallas kernels: 50.2 us -> 62.3 us  [the longest x2 30.8 us: place_children(): pl.pallas_call(functools.partial(place_kernel, b), grid_spec=grid_spec, o...]
    all_to_all x2 -> x3, starting transfers between devices: 14.2 us -> 23.6 us  [the longest x2 17.1 us: body(): lax.all_to_all(parcels.reshape(128, 128, 128), ALL, 0, 0, tiled=True)]
  transfers between devices with their start and end apart: 9 -> 9, of which waited for: 4 -> 7; matrix products, arithmetic and copies ran while one was open for 3% -> 2% of each run, Pallas kernels for 0% -> 8%
where the time goes in v1:
time: 303 us
  waiting for transfers between devices  199 us (66%)
  Pallas kernels  62.3 us (21%)
  starting transfers between devices  29.7 us (10%)
  local copies, waits for them, and re-layouts  9.3 us (3%)
    ppermute x6, waiting for transfers between devices, shift(): return lax.ppermute(array, ALL, pairs)  123 us
    all_to_all x2, waiting for transfers between devices, body(): lax.all_to_all(parcels.reshape(128, 128, 128), ALL, 0, 0, tiled=True)  75.8 us
    pallas_call x2, Pallas kernels, place_children(): pl.pallas_call(functools.partial(place_kernel, b), grid_spec=grid_spec, o...  30.8 us
    pallas_call x2, Pallas kernels, schur_parcels(): pl.pallas_call(schur_kernel, grid=(4,), in_specs=[pl.BlockSpec((2048, 102...  19.1 us
    all_to_all x2, starting transfers between devices, body(): lax.all_to_all(parcels.reshape(128, 128, 128), ALL, 0, 0, tiled=True)  17.1 us
    pallas_call x1, Pallas kernels, lower_rows(): pl.pallas_call(lower_kernel, grid_spec=grid_spec, out_shape=[out, out], c...  12.4 us
    all_to_all x1, starting transfers between devices, body(): lax.all_to_all(jnp.broadcast_to(packet, (8, 2560, 128)), 'col', 0, 0, til...  6.51 us
    ppermute x6, starting transfers between devices, shift(): return lax.ppermute(array, ALL, pairs)  6.12 us
  transfers between devices with their start and end apart: 9, of which 7 were waited for; matrix products, arithmetic and copies ran while one was open for 2% of the time, Pallas kernels for 8%

profile of v1, /device:TPU:1, one launch (start us, length us, event | category | flops | bytes accessed | tf_op | source)
XLA Modules:
  0.0 302.8 jit_solution(11098198084319901838)
XLA Ops:
  0.0 0.0 copy-start
  0.0 0.9 copy-done
  1.0 1.1 pad_maximum_fusion.1
  2.1 3.0 %broadcast_in_dim.4 = bf16[8,2560,128]{2,1,0:T(8,128)(2,1)} broadcast(bf16[2560,128]{1,0:T(8,128)(2,1)S(1)} %pad_maximum_fusion.1), dimensions={1,2} | broadcast | bytes 5898240 | tf_op jit(solution)/shard_map/broadcast_in_dim | solution.py:211
  5.1 0.0 copy-start.3
  5.1 6.5 %all-to-all-start = ((bf16[8,2560,128]{2,1,0:T(8,128)(2,1)}), bf16[8,2560,128]{2,1,0:T(8,128)(2,1)}, u32[]{:S(2)}, u32[]{:S(2)}) async-start(bf16[8,2560,128]{2,1,0:T(8,128)(2,1)} %broadcast_in_dim.4), calls=%async_computation | async-start | bytes 10485760 | tf_op jit(solution)/shard_map/all_to_all | solution.py:210
  11.6 0.0 copy-done.3
  11.6 4.5 %collective-permute-start = (bf16[2048,128]{1,0:T(8,128)(2,1)S(1)}, bf16[2048,128]{1,0:T(8,128)(2,1)S(1)}, u32[]{:S(2)}, u32[]{:S(2)}) collective-permute-start(bf16[2048,128]{1,0:T(8,128)(2,1)S(1)} %bitcast.33), channel_id=1, source_target_pairs={{0,0},{1,8},{2,16},{3,24},{4,32},{5,40},{6,48},{7,56},{8,1},{9,9},... | collective-permute-start | bytes 1572872 | tf_op jit(solution)/shard_map/ppermute | solution.py:24
  16.1 106.0 %collective-permute-done = bf16[2048,128]{1,0:T(8,128)(2,1)S(1)} collective-permute-done((bf16[2048,128]{1,0:T(8,128)(2,1)S(1)}, bf16[2048,128]{1,0:T(8,128)(2,1)S(1)}, u32[]{:S(2)}, u32[]{:S(2)}) %collective-permute-start) | collective-permute-done | bytes 524320 | tf_op jit(solution)/shard_map/ppermute | solution.py:24
  122.1 0.0 collective-permute-start.3
  122.1 0.0 collective-permute-start.2
  122.1 1.5 collective-permute-start.1
  123.6 8.2 %collective-permute-done.3 = bf16[2048,128]{1,0:T(8,128)(2,1)S(1)} collective-permute-done((bf16[2048,128]{1,0:T(8,128)(2,1)S(1)}, bf16[2048,128]{1,0:T(8,128)(2,1)S(1)}, u32[]{:S(2)}, u32[]{:S(2)}) %collective-permute-start.3) | collective-permute-done | bytes 524320 | tf_op jit(solution)/shard_map/ppermute | solution.py:24
  131.8 0.0 collective-permute-done.2
  131.8 5.5 %collective-permute-done.1 = bf16[2048,128]{1,0:T(8,128)(2,1)S(1)} collective-permute-done((bf16[2048,128]{1,0:T(8,128)(2,1)S(1)}, bf16[2048,128]{1,0:T(8,128)(2,1)S(1)}, u32[]{:S(2)}, u32[]{:S(2)}) %collective-permute-start.1) | collective-permute-done | bytes 524320 | tf_op jit(solution)/shard_map/ppermute | solution.py:24
  137.3 0.3 pad_maximum_fusion.mine_ref
  137.5 0.0 copy-start.2
  137.6 0.1 collective-permute-start.4
  137.6 0.0 all-to-all-done.rows_ref.inverse_mine_ref
  137.7 1.9 slice.4
  139.6 0.1 collective-permute-start.5
  139.7 0.7 pad_add_fusion.place_ref
  140.4 1.5 collective-permute-done.4.other_ref
  141.9 1.5 collective-permute-done.5.inverse_other_ref
  143.4 0.0 copy-done.2
  143.4 12.4 %lower.1 = (bf16[2048,1024]{1,0:T(8,128)(2,1)}, bf16[2048,1024]{1,0:T(8,128)(2,1)}) custom-call(s32[4]{0:T(128)} %pad_add_fusion.place_ref, bf16[8,2560,128]{2,1,0:T(8,128)(2,1)} %all-to-all-done.rows_ref.inverse_mine_ref, bf16[4,2048,128]{2,1,0:T(8,128)(2,1)} %copy-done.2, bf16[4,2048,128]{2,1,0:T(8,128)(2,1)} %collective-permute-done.4.other_ref, ...), custom_call_target="tpu_custom_call" | custom-call | flops 5368709120 | bytes 18874368 | tf_op jit(solution)/shard_map/lower/pallas_call | solution.py:91
  155.9 9.5 %schur.3 = bf16[16,8,128,128]{3,2,1,0:T(8,128)(2,1)} custom-call(bf16[2048,1024]{1,0:T(8,128)(2,1)} %get-tuple-element.7.left_ref, bf16[8,2,128,1024]{3,2,1,0:T(8,128)(2,1)} %bitcast.28, bf16[2048,2048]{1,0:T(8,128)(2,1)} %bitcast.24, bf16[2048,2048]{1,0:T(8,128)(2,1)} %bitcast.25), custom_call_target="tpu_custom_call" | custom-call | flops 4294967296 | bytes 14680064 | tf_op jit(solution)/shard_map/schur/pallas_call | solution.py:118
  165.4 10.6 %all-to-all-start.2 = ((bf16[128,128,128]{2,1,0:T(8,128)(2,1)}), bf16[128,128,128]{2,1,0:T(8,128)(2,1)}, u32[]{:S(2)}, u32[]{:S(2)}) async-start(bf16[128,128,128]{2,1,0:T(8,128)(2,1)} %bitcast.31), calls=%async_computation.2 | async-start | bytes 8388608 | tf_op jit(solution)/shard_map/all_to_all | solution.py:237
  176.1 9.5 %schur.2 = bf16[16,8,128,128]{3,2,1,0:T(8,128)(2,1)} custom-call(bf16[2048,1024]{1,0:T(8,128)(2,1)} %get-tuple-element.7.left_ref, bf16[8,2,128,1024]{3,2,1,0:T(8,128)(2,1)} %bitcast.29, bf16[2048,2048]{1,0:T(8,128)(2,1)} %bitcast.26, bf16[2048,2048]{1,0:T(8,128)(2,1)} %bitcast.27), custom_call_target="tpu_custom_call" | custom-call | flops 4294967296 | bytes 14680064 | tf_op jit(solution)/shard_map/schur/pallas_call | solution.py:118
  185.6 42.8 %all-to-all-done.2.schur_in_ref = bf16[128,128,128]{2,1,0:T(8,128)(2,1)} async-done(((bf16[128,128,128]{2,1,0:T(8,128)(2,1)}), bf16[128,128,128]{2,1,0:T(8,128)(2,1)}, u32[]{:S(2)}, u32[]{:S(2)}) %all-to-all-start.2) | async-done | bytes 4194336 | tf_op jit(solution)/shard_map/all_to_all | solution.py:237
  228.4 0.0 copy-start.4
  228.4 6.5 %all-to-all-start.1 = ((bf16[128,128,128]{2,1,0:T(8,128)(2,1)}), bf16[128,128,128]{2,1,0:T(8,128)(2,1)}, u32[]{:S(2)}, u32[]{:S(2)}) async-start(bf16[128,128,128]{2,1,0:T(8,128)(2,1)} %bitcast.30), calls=%async_computation.1 | async-start | bytes 8388608 | tf_op jit(solution)/shard_map/all_to_all | solution.py:237
  234.9 0.0 copy-done.4
  235.0 0.1 fusion
  235.1 3.3 %reshape.44.col_map_ref = s32[2,2,1024,1]{3,2,1,0:T(8,128)} reshape(s32[2,2,8,128]{3,2,1,0:T(8,128)S(1)} %fusion) | data formatting | bytes 32768 | tf_op jit(solution)/shard_map/reshape | solution.py:232
  238.4 0.6 broadcast_subtract_fusion
  239.0 15.3 %place.2.refs_0_ = f32[1024,2048]{1,0:T(8,128)} custom-call(s32[4]{0:T(128)} %pad_add_fusion.place_ref, bf16[128,128,128]{2,1,0:T(8,128)(2,1)} %all-to-all-done.2.schur_in_ref, s32[2,1,1024]{2,1,0:T(1,128)} %bitcast.42, s32[2,2,1024,1]{3,2,1,0:T(8,128)} %reshape.44.col_map_ref, bf16[1024,2048]{1,0:T(8,128)(2,1)} %base_ref.3), custom_call_target="tpu_custom_call" | custom-call | flops 8589934592 | bytes 10485760 | tf_op jit(solution)/shard_map/place/pallas_call | solution.py:179
  254.3 33.0 %all-to-all-done.1.schur_in_ref = bf16[128,128,128]{2,1,0:T(8,128)(2,1)} async-done(((bf16[128,128,128]{2,1,0:T(8,128)(2,1)}), bf16[128,128,128]{2,1,0:T(8,128)(2,1)}, u32[]{:S(2)}, u32[]{:S(2)}) %all-to-all-start.1) | async-done | bytes 4194336 | tf_op jit(solution)/shard_map/all_to_all | solution.py:237
  287.3 0.0 copy-start.1
  287.3 15.5 %place.3 = f32[1024,2048]{1,0:T(8,128)} custom-call(s32[4]{0:T(128)} %pad_add_fusion.place_ref, bf16[128,128,128]{2,1,0:T(8,128)(2,1)} %all-to-all-done.1.schur_in_ref, s32[2,1,1024]{2,1,0:T(1,128)} %bitcast.43, s32[2,2,1024,1]{3,2,1,0:T(8,128)} %reshape.44.col_map_ref, bf16[1024,2048]{1,0:T(8,128)(2,1)} %base_ref.3, ...), custom_call_target="tpu_custom_call", output_to_operand_aliasing={{}: (5, {})} | custom-call | flops 8589934592 | bytes 10485760 | tf_op jit(solution)/shard_map/place/pallas_call | solution.py:179
  302.8 0.0 copy-done.1
  (5 shorter events, 0.1 us)
Async XLA Ops:
  0.0 1.0 copy-start
  5.1 6.5 %copy-start.3 = (bf16[1,2048,128]{2,1,0:T(8,128)(2,1)S(1)}, bf16[1,2048,128]{2,1,0:T(8,128)(2,1)}, u32[]{:S(2)}) copy-start(bf16[1,2048,128]{2,1,0:T(8,128)(2,1)} %param.6) | copy-start | bytes 1572868
  5.1 132.6 %all-to-all-start = ((bf16[8,2560,128]{2,1,0:T(8,128)(2,1)}), bf16[8,2560,128]{2,1,0:T(8,128)(2,1)}, u32[]{:S(2)}, u32[]{:S(2)}) async-start(bf16[8,2560,128]{2,1,0:T(8,128)(2,1)} %broadcast_in_dim.4), calls=%async_computation | async-start | bytes 10485760 | tf_op jit(solution)/shard_map/all_to_all | solution.py:210
  11.6 110.5 %collective-permute-start = (bf16[2048,128]{1,0:T(8,128)(2,1)S(1)}, bf16[2048,128]{1,0:T(8,128)(2,1)S(1)}, u32[]{:S(2)}, u32[]{:S(2)}) collective-permute-start(bf16[2048,128]{1,0:T(8,128)(2,1)S(1)} %bitcast.33), channel_id=1, source_target_pairs={{0,0},{1,8},{2,16},{3,24},{4,32},{5,40},{6,48},{7,56},{8,1},{9,9},... | collective-permute-start | bytes 1572872 | tf_op jit(solution)/shard_map/ppermute | solution.py:24
  122.1 9.6 %collective-permute-start.3 = (bf16[2048,128]{1,0:T(8,128)(2,1)S(1)}, bf16[2048,128]{1,0:T(8,128)(2,1)S(1)}, u32[]{:S(2)}, u32[]{:S(2)}) collective-permute-start(bf16[2048,128]{1,0:T(8,128)(2,1)S(1)} %collective-permute-done), channel_id=1, source_target_pairs={{0,32},{1,33},{2,34},{3,35},{4,36},{5,37},{6,38},{7,39},{8,40},{9,... | collective-permute-start | bytes 1572872 | tf_op jit(solution)/shard_map/ppermute | solution.py:24
  122.1 9.6 %collective-permute-start.2 = (bf16[2048,128]{1,0:T(8,128)(2,1)S(1)}, bf16[2048,128]{1,0:T(8,128)(2,1)S(1)}, u32[]{:S(2)}, u32[]{:S(2)}) collective-permute-start(bf16[2048,128]{1,0:T(8,128)(2,1)S(1)} %collective-permute-done), channel_id=1, source_target_pairs={{0,48},{1,49},{2,50},{3,51},{4,52},{5,53},{6,54},{7,55},{8,56},{9,... | collective-permute-start | bytes 1572872 | tf_op jit(solution)/shard_map/ppermute | solution.py:24
  122.1 15.1 %collective-permute-start.1 = (bf16[2048,128]{1,0:T(8,128)(2,1)S(1)}, bf16[2048,128]{1,0:T(8,128)(2,1)S(1)}, u32[]{:S(2)}, u32[]{:S(2)}) collective-permute-start(bf16[2048,128]{1,0:T(8,128)(2,1)S(1)} %collective-permute-done), channel_id=1, source_target_pairs={{0,16},{1,17},{2,18},{3,19},{4,20},{5,21},{6,22},{7,23},{8,24},{9,... | collective-permute-start | bytes 1572872 | tf_op jit(solution)/shard_map/ppermute | solution.py:24
  137.5 5.9 %copy-start.2 = (bf16[4,2048,128]{2,1,0:T(8,128)(2,1)}, bf16[4,2048,128]{2,1,0:T(8,128)(2,1)S(1)}, u32[]{:S(2)}) copy-start(bf16[4,2048,128]{2,1,0:T(8,128)(2,1)S(1)} %pad_maximum_fusion.mine_ref) | copy-start | bytes 6291460
  137.6 4.4 %collective-permute-start.4 = (bf16[4,2048,128]{2,1,0:T(8,128)(2,1)S(1)}, bf16[4,2048,128]{2,1,0:T(8,128)(2,1)}, u32[]{:S(2)}, u32[]{:S(2)}) collective-permute-start(bf16[4,2048,128]{2,1,0:T(8,128)(2,1)S(1)} %pad_maximum_fusion.mine_ref), channel_id=1, source_target_pairs={{0,8},{1,9},{2,10},{3,11},{4,12},{5,13},{6,14},{7,15},{8,0},{9,1},... | collective-permute-start | bytes 6291464 | tf_op jit(solution)/shard_map/ppermute | solution.py:24
  139.6 3.8 %collective-permute-start.5 = (bf16[8,512,128]{2,1,0:T(8,128)(2,1)S(1)}, bf16[8,512,128]{2,1,0:T(8,128)(2,1)}, u32[]{:S(2)}, u32[]{:S(2)}) collective-permute-start(bf16[8,512,128]{2,1,0:T(8,128)(2,1)S(1)} %slice.4), channel_id=1, source_target_pairs={{0,8},{1,9},{2,10},{3,11},{4,12},{5,13},{6,14},{7,15},{8,0},{9,1},... | collective-permute-start | bytes 3145736 | tf_op jit(solution)/shard_map/ppermute | solution.py:24
  165.4 63.0 %all-to-all-start.2 = ((bf16[128,128,128]{2,1,0:T(8,128)(2,1)}), bf16[128,128,128]{2,1,0:T(8,128)(2,1)}, u32[]{:S(2)}, u32[]{:S(2)}) async-start(bf16[128,128,128]{2,1,0:T(8,128)(2,1)} %bitcast.31), calls=%async_computation.2 | async-start | bytes 8388608 | tf_op jit(solution)/shard_map/all_to_all | solution.py:237
  228.4 6.5 %copy-start.4 = (s32[2,16384]{1,0:T(2,128)S(1)}, s32[2,16384]{1,0:T(2,128)}, u32[]{:S(2)}) copy-start(s32[2,16384]{1,0:T(2,128)} %param.8) | copy-start | bytes 393220
  228.4 58.9 %all-to-all-start.1 = ((bf16[128,128,128]{2,1,0:T(8,128)(2,1)}), bf16[128,128,128]{2,1,0:T(8,128)(2,1)}, u32[]{:S(2)}, u32[]{:S(2)}) async-start(bf16[128,128,128]{2,1,0:T(8,128)(2,1)} %bitcast.30), calls=%async_computation.1 | async-start | bytes 8388608 | tf_op jit(solution)/shard_map/all_to_all | solution.py:237
  287.3 15.5 %copy-start.1 = (bf16[1,1024,128]{2,1,0:T(8,128)(2,1)S(1)}, bf16[1,1024,128]{2,1,0:T(8,128)(2,1)}, u32[]{:S(2)}) copy-start(bf16[1,1024,128]{2,1,0:T(8,128)(2,1)} %param.7) | copy-start | bytes 786436

commit v2 on v1

--- a/solution.py
+++ b/solution.py
@@ -29,7 +29,11 @@
 
 def lower_kernel(
     place_ref,
-    rows_ref,
+    near_ref,
+    behind_ref,
+    ahead_ref,
+    far_first_ref,
+    far_second_ref,
     mine_ref,
     other_ref,
     inverse_mine_ref,
@@ -39,16 +43,16 @@
     inverse_ref,
     wide_ref,
 ):
-    x, core = place_ref[0], place_ref[1]
+    x, core, y = place_ref[0], place_ref[1], place_ref[4]
+
+    def columns(chunk):
+        return pl.ds(pl.multiple_of(chunk * 128, 128), 128)
 
     @pl.when(pl.program_id(0) == 0)
     def _():
         for ref, part in ((inverse_mine_ref, core), (inverse_other_ref, 1 - core)):
-            for chunk in range(8):
-                inverse_ref[
-                    pl.ds(pl.multiple_of(part * 512, 512), 512),
-                    chunk * 128 : (chunk + 1) * 128,
-                ] = ref[chunk]
+            for index, away in enumerate((0, 3, 1, 2)):
+                inverse_ref[:, columns(((x + away) % 4) * 2 + part)] = ref[index]
 
     def lower(out_ref):
         for n in range(4):
@@ -60,28 +64,28 @@
                 preferred_element_type=F32,
             ).astype(BF16)
 
-    for chunk in range(8):
-        wide_ref[:, chunk * 128 : (chunk + 1) * 128] = rows_ref[chunk]
+    for ref, away in ((near_ref, 0), (behind_ref, 3), (ahead_ref, 1)):
+        for zl in range(2):
+            wide_ref[:, columns(zl * 4 + (y + away) % 4)] = ref[zl]
+    wide_ref[:, columns((y + 2) % 4)] = far_first_ref[...]
+    wide_ref[:, columns(4 + (y + 2) % 4)] = far_second_ref[...]
     lower(left_ref)
     for ref, part in ((mine_ref, core), (other_ref, 1 - core)):
         for index, away in enumerate((0, 3, 1, 2)):
-            chunk = ((x + away) % 4) * 2 + part
-            wide_ref[:, pl.ds(pl.multiple_of(chunk * 128, 128), 128)] = ref[index]
+            wide_ref[:, columns(((x + away) % 4) * 2 + part)] = ref[index]
     lower(right_ref)
 
 
-def lower_rows(place, packet, mine, other, inverse_other):
+def lower_rows(place, rows, mine, other):
     out = jax.ShapeDtypeStruct((2048, 1024), BF16)
+    pair = pl.BlockSpec((2, LOWER_ROWS, 128), lambda i, s: (0, i, 0))
+    single = pl.BlockSpec((LOWER_ROWS, 128), lambda i, s: (i, 0))
+    four = pl.BlockSpec((4, LOWER_ROWS, 128), lambda i, s: (0, i, 0))
+    inverse = pl.BlockSpec((4, 1024, 128), lambda i, s: (0, 2, 0))
     grid_spec = pltpu.PrefetchScalarGridSpec(
         num_scalar_prefetch=1,
         grid=(2048 // LOWER_ROWS,),
-        in_specs=[
-            pl.BlockSpec((8, LOWER_ROWS, 128), lambda i, s: (0, i, 0)),
-            pl.BlockSpec((4, LOWER_ROWS, 128), lambda i, s: (0, i, 0)),
-            pl.BlockSpec((4, LOWER_ROWS, 128), lambda i, s: (0, i, 0)),
-            pl.BlockSpec((8, 512, 128), lambda i, s: (0, 4, 0)),
-            pl.BlockSpec((8, 512, 128), lambda i, s: (0, 0, 0)),
-        ],
+        in_specs=[pair] * 3 + [single] * 2 + [four] * 2 + [inverse] * 2,
         out_specs=[pl.BlockSpec((LOWER_ROWS, 1024), lambda i, s: (i, 0))] * 2,
         scratch_shapes=[
             pltpu.VMEM((1024, 1024), BF16),
@@ -97,7 +101,7 @@
             flops=5 << 30, bytes_accessed=18 << 20, transcendentals=0
         ),
         name="lower",
-    )(place, packet, mine, other, packet, inverse_other)
+    )(place, *rows, mine, other, mine, other)
 
 
 def schur_kernel(left_ref, right_ref, front_even_ref, front_odd_ref, out_ref):
@@ -202,25 +206,36 @@
     col = lax.axis_index("col")
     x, core = row // 2, row % 2
     target = half * 8 + row
-    place = jnp.stack([x, core, target, col]).astype(jnp.int32)
-
-    turned = shift(panel[0], lambda h, r, c: (h, c, r))
-    inverse_share = lax.dynamic_slice_in_dim(inverse_block[0], core * 512, 512, 0)
-    packet = jnp.concatenate([panel[0], inverse_share])
-    packet = lax.all_to_all(
-        jnp.broadcast_to(packet, (8, 2560, 128)), "col", 0, 0, tiled=True
-    )
-    inverse_other = shift(packet[:, 2048:], lambda h, r, c: (h, r ^ 1, c))
-    mine = jnp.stack(
-        [
-            turned,
-            shift(turned, lambda h, r, c: (h, (r + 2) % 8, c)),
-            shift(turned, lambda h, r, c: (h, (r + 6) % 8, c)),
-            shift(turned, lambda h, r, c: (h, (r + 4) % 8, c)),
-        ]
-    )
+    place = jnp.stack([x, core, target, col, col % 4]).astype(jnp.int32)
+
+    turned = shift(
+        jnp.concatenate([panel[0], inverse_block[0]]), lambda h, r, c: (h, c, r)
+    )
+    twin = shift(panel[0], lambda h, r, c: (h, r, c ^ 4))
+    pair = jnp.stack(
+        [jnp.where(col < 4, panel[0], twin), jnp.where(col < 4, twin, panel[0])]
+    )
+
+    def forward(h, r, c):
+        return h, r, c // 4 * 4 + (c + 1) % 4
+
+    def backward(h, r, c):
+        return h, r, c // 4 * 4 + (c + 3) % 4
+
+    turned, pair = lax.optimization_barrier((turned, pair))
+    one = shift(turned, lambda h, r, c: (h, (r + 2) % 8, c))
+    three = shift(turned, lambda h, r, c: (h, (r + 6) % 8, c))
+    behind = shift(pair, forward)
+    ahead = shift(pair, backward)
+    two = shift(turned, lambda h, r, c: (h, (r + 4) % 8, c))
+    one, three, behind, ahead = lax.optimization_barrier((one, three, behind, ahead))
+    far_first, far_second, two = lax.optimization_barrier(
+        (shift(behind[0], forward), shift(ahead[1], backward), two)
+    )
+    rows = (pair, behind, ahead, far_first, far_second)
+    mine = jnp.stack([turned, one, three, two])
     other = shift(mine, lambda h, r, c: (h, r ^ 1, c))
-    left, right = lower_rows(place, packet, mine, other, inverse_other)
+    left, right = lower_rows(place, rows, mine, other)
 
     maps = child_maps.reshape(2, 8, 16, 128)
     row_maps = (

time: 303 us -> 266 us (0.88)
  waiting for transfers between devices: 199 us -> 154 us
  starting transfers between devices: 29.7 us -> 38.9 us
  local copies, waits for them, and re-layouts: 9.3 us -> 4.83 us
    ppermute x6 -> x10, waiting for transfers between devices: 123 us -> 77.9 us  [shift(): return lax.ppermute(array, ALL, pairs)]
    ppermute x6 -> x10, starting transfers between devices: 6.12 us -> 24 us  [shift(): return lax.ppermute(array, ALL, pairs)]
    all_to_all x1 -> x0, starting transfers between devices: 6.51 us -> none  [body(): lax.all_to_all(jnp.broadcast_to(packet, (8, 2560, 128)), 'col', 0, 0, til...]
    broadcast_in_dim x1 -> x0, local copies, waits for them, and re-layouts: 3.03 us -> none  [body(): jnp.broadcast_to(packet, (8, 2560, 128))]
  transfers between devices with their start and end apart: 9 -> 12, of which waited for: 7 -> 9; matrix products, arithmetic and copies ran while one was open for 2% -> 3% of each run, Pallas kernels for 8% -> 9%
where the time goes in v2:
time: 266 us; the launch traced here: 265 us
  waiting for transfers between devices  154 us (58%)
  Pallas kernels  63 us (24%)
  starting transfers between devices  38.9 us (15%)
  local copies, waits for them, and re-layouts  4.83 us (2%)
  other arithmetic  4.49 us (2%)
    ppermute x10, waiting for transfers between devices, shift(): return lax.ppermute(array, ALL, pairs)  77.9 us
    all_to_all x2, waiting for transfers between devices, body(): lax.all_to_all(parcels.reshape(128, 128, 128), ALL, 0, 0, tiled=True)  75.8 us
    pallas_call x2, Pallas kernels, place_children(): pl.pallas_call(functools.partial(place_kernel, b), grid_spec=grid_spec, o...  30.7 us
    ppermute x10, starting transfers between devices, shift(): return lax.ppermute(array, ALL, pairs)  24 us
    pallas_call x2, Pallas kernels, schur_parcels(): pl.pallas_call(schur_kernel, grid=(4,), in_specs=[pl.BlockSpec((2048, 102...  19.1 us
    all_to_all x2, starting transfers between devices, body(): lax.all_to_all(parcels.reshape(128, 128, 128), ALL, 0, 0, tiled=True)  14.9 us
    pallas_call x1, Pallas kernels, lower_rows(): pl.pallas_call(lower_kernel, grid_spec=grid_spec, out_shape=[out, out], c...  13.2 us
  transfers between devices with their start and end apart: 12, of which 9 were waited for; matrix products, arithmetic and copies ran while one was open for 3% of the time, Pallas kernels for 9%

profile of v2, /device:TPU:1, one launch (start us, length us, event | category | flops | bytes accessed | tf_op | source)
XLA Modules:
  0.0 265.1 jit_solution(391542235280182432)
XLA Ops:
  0.0 2.5 collective-permute-start.1
  2.5 1.2 pad_maximum_fusion.2
  3.6 4.0 %collective-permute-start = (bf16[3072,128]{1,0:T(8,128)(2,1)S(1)}, bf16[3072,128]{1,0:T(8,128)(2,1)S(1)}, u32[]{:S(2)}, u32[]{:S(2)}) collective-permute-start(bf16[3072,128]{1,0:T(8,128)(2,1)S(1)} %pad_maximum_fusion.2), channel_id=1, source_target_pairs={{0,0},{1,8},{2,16},{3,24},{4,32},{5,40},{6,48},{7,56},{8,1},{9,9},... | collective-permute-start | bytes 2359304 | tf_op jit(solution)/shard_map/ppermute | solution.py:24
  7.7 22.5 %collective-permute-done.1 = bf16[2048,128]{1,0:T(8,128)(2,1)S(1)} collective-permute-done((bf16[2048,128]{1,0:T(8,128)(2,1)}, bf16[2048,128]{1,0:T(8,128)(2,1)S(1)}, u32[]{:S(2)}, u32[]{:S(2)}) %collective-permute-start.1) | collective-permute-done | bytes 524320 | tf_op jit(solution)/shard_map/ppermute | solution.py:24
  30.2 1.1 select_bitcast_fusion.1
  31.3 0.1 pad_maximum_fusion.1.near_ref
  31.5 0.0 copy-start.1
  31.5 10.1 %collective-permute-done = bf16[3072,128]{1,0:T(8,128)(2,1)S(1)} collective-permute-done((bf16[3072,128]{1,0:T(8,128)(2,1)S(1)}, bf16[3072,128]{1,0:T(8,128)(2,1)S(1)}, u32[]{:S(2)}, u32[]{:S(2)}) %collective-permute-start) | collective-permute-done | bytes 786464 | tf_op jit(solution)/shard_map/ppermute | solution.py:24
  41.6 0.0 collective-permute-start.5
  41.6 1.5 collective-permute-start.4
  43.1 7.5 %collective-permute-start.3 = (bf16[3072,128]{1,0:T(8,128)(2,1)S(1)}, bf16[3072,128]{1,0:T(8,128)(2,1)S(1)}, u32[]{:S(2)}, u32[]{:S(2)}) collective-permute-start(bf16[3072,128]{1,0:T(8,128)(2,1)S(1)} %collective-permute-done), channel_id=1, source_target_pairs={{0,48},{1,49},{2,50},{3,51},{4,52},{5,53},{6,54},{7,55},{8,56},{9,... | collective-permute-start | bytes 2359304 | tf_op jit(solution)/shard_map/ppermute | solution.py:24
  50.5 0.0 collective-permute-start.2
  50.5 1.2 collective-permute-start.8
  51.8 30.6 %collective-permute-done.3 = bf16[3072,128]{1,0:T(8,128)(2,1)S(1)} collective-permute-done((bf16[3072,128]{1,0:T(8,128)(2,1)S(1)}, bf16[3072,128]{1,0:T(8,128)(2,1)S(1)}, u32[]{:S(2)}, u32[]{:S(2)}) %collective-permute-start.3) | collective-permute-done | bytes 786464 | tf_op jit(solution)/shard_map/ppermute | solution.py:24
  82.4 0.0 collective-permute-done.2
  82.4 0.0 collective-permute-done.5.ahead_ref
  82.4 0.0 collective-permute-done.4.behind_ref
  82.4 0.0 copy-start.4
  82.5 1.6 collective-permute-start.7
  84.1 0.0 collective-permute-start.6
  84.1 0.4 collective-permute-done.8
  84.5 6.4 %collective-permute-done.7.far_second_ref = bf16[2048,128]{1,0:T(8,128)(2,1)S(1)} collective-permute-done((bf16[2048,128]{1,0:T(8,128)(2,1)S(1)}, bf16[2048,128]{1,0:T(8,128)(2,1)S(1)}, u32[]{:S(2)}, u32[]{:S(2)}) %collective-permute-start.7) | collective-permute-done | bytes 524320 | tf_op jit(solution)/shard_map/ppermute | solution.py:24
  90.9 3.1 %collective-permute-done.6.far_first_ref = bf16[2048,128]{1,0:T(8,128)(2,1)S(1)} collective-permute-done((bf16[2048,128]{1,0:T(8,128)(2,1)S(1)}, bf16[2048,128]{1,0:T(8,128)(2,1)S(1)}, u32[]{:S(2)}, u32[]{:S(2)}) %collective-permute-start.6) | collective-permute-done | bytes 524320 | tf_op jit(solution)/shard_map/ppermute | solution.py:24
  93.9 0.0 copy-done.1
  94.0 0.0 copy-done.2
  94.0 0.0 copy-done.3
  94.0 0.0 copy-done.4
  94.0 0.0 copy-done.6
  94.0 0.8 copy-done.7
  94.8 1.4 pad_maximum_fusion.mine_ref.inverse_mine_ref
  96.2 0.0 copy-start
  96.2 5.8 %collective-permute-start.9 = (bf16[4,3072,128]{2,1,0:T(8,128)(2,1)S(1)}, bf16[4,3072,128]{2,1,0:T(8,128)(2,1)}, u32[]{:S(2)}, u32[]{:S(2)}) collective-permute-start(bf16[4,3072,128]{2,1,0:T(8,128)(2,1)S(1)} %pad_maximum_fusion.mine_ref.inverse_mine_ref), channel_id=1, source_target_pairs={{0,8},{1,9},{2,10},{3,11},{4,12},{5,13},{6,14},{7,15},{8,0},{9,1},... | collective-permute-start | bytes 9437192 | tf_op jit(solution)/shard_map/ppermute | solution.py:24
  101.9 0.6 stack.47.place_ref
  102.6 4.8 %collective-permute-done.9.other_ref.inverse_other_ref = bf16[4,3072,128]{2,1,0:T(8,128)(2,1)} collective-permute-done((bf16[4,3072,128]{2,1,0:T(8,128)(2,1)S(1)}, bf16[4,3072,128]{2,1,0:T(8,128)(2,1)}, u32[]{:S(2)}, u32[]{:S(2)}) %collective-permute-start.9) | collective-permute-done | bytes 3145760 | tf_op jit(solution)/shard_map/ppermute | solution.py:24
  107.4 0.0 copy-done
  107.4 13.2 %lower.1 = (bf16[2048,1024]{1,0:T(8,128)(2,1)}, bf16[2048,1024]{1,0:T(8,128)(2,1)}) custom-call(s32[5]{0:T(128)} %stack.47.place_ref, bf16[2,2048,128]{2,1,0:T(8,128)(2,1)} %copy-done.1, bf16[2,2048,128]{2,1,0:T(8,128)(2,1)} %copy-done.4, bf16[2,2048,128]{2,1,0:T(8,128)(2,1)} %copy-done.3, bf16[2048,128]{1,0:T(8,128)(2,1)} %copy-done.7, ...), custom_call_target="tpu_custom_call" | custom-call | flops 5368709120 | bytes 18874368 | tf_op jit(solution)/shard_map/lower/pallas_call | solution.py:95
  120.6 9.6 %schur.3 = bf16[16,8,128,128]{3,2,1,0:T(8,128)(2,1)} custom-call(bf16[2048,1024]{1,0:T(8,128)(2,1)} %get-tuple-element.25.left_ref, bf16[8,2,128,1024]{3,2,1,0:T(8,128)(2,1)} %bitcast.38, bf16[2048,2048]{1,0:T(8,128)(2,1)} %bitcast.34, bf16[2048,2048]{1,0:T(8,128)(2,1)} %bitcast.35), custom_call_target="tpu_custom_call" | custom-call | flops 4294967296 | bytes 14680064 | tf_op jit(solution)/shard_map/schur/pallas_call | solution.py:122
  130.1 8.4 %all-to-all-start.1 = ((bf16[128,128,128]{2,1,0:T(8,128)(2,1)}), bf16[128,128,128]{2,1,0:T(8,128)(2,1)}, u32[]{:S(2)}, u32[]{:S(2)}) async-start(bf16[128,128,128]{2,1,0:T(8,128)(2,1)} %bitcast.41), calls=%async_computation.1 | async-start | bytes 8388608 | tf_op jit(solution)/shard_map/all_to_all | solution.py:252
  138.5 9.6 %schur.2 = bf16[16,8,128,128]{3,2,1,0:T(8,128)(2,1)} custom-call(bf16[2048,1024]{1,0:T(8,128)(2,1)} %get-tuple-element.25.left_ref, bf16[8,2,128,1024]{3,2,1,0:T(8,128)(2,1)} %bitcast.39, bf16[2048,2048]{1,0:T(8,128)(2,1)} %bitcast.36, bf16[2048,2048]{1,0:T(8,128)(2,1)} %bitcast.37), custom_call_target="tpu_custom_call" | custom-call | flops 4294967296 | bytes 14680064 | tf_op jit(solution)/shard_map/schur/pallas_call | solution.py:122
  148.1 42.8 %all-to-all-done.1.schur_in_ref = bf16[128,128,128]{2,1,0:T(8,128)(2,1)} async-done(((bf16[128,128,128]{2,1,0:T(8,128)(2,1)}), bf16[128,128,128]{2,1,0:T(8,128)(2,1)}, u32[]{:S(2)}, u32[]{:S(2)}) %all-to-all-start.1) | async-done | bytes 4194336 | tf_op jit(solution)/shard_map/all_to_all | solution.py:252
  190.9 6.5 %all-to-all-start = ((bf16[128,128,128]{2,1,0:T(8,128)(2,1)}), bf16[128,128,128]{2,1,0:T(8,128)(2,1)}, u32[]{:S(2)}, u32[]{:S(2)}) async-start(bf16[128,128,128]{2,1,0:T(8,128)(2,1)} %bitcast.40), calls=%async_computation | async-start | bytes 8388608 | tf_op jit(solution)/shard_map/all_to_all | solution.py:252
  197.4 0.0 copy-done.5
  197.5 0.1 fusion
  197.6 3.3 %reshape.43.col_map_ref = s32[2,2,1024,1]{3,2,1,0:T(8,128)} reshape(s32[2,2,8,128]{3,2,1,0:T(8,128)S(1)} %fusion) | data formatting | bytes 32768 | tf_op jit(solution)/shard_map/reshape | solution.py:247
  200.9 0.6 broadcast_subtract_fusion
  201.5 15.3 %place.2.refs_0_ = f32[1024,2048]{1,0:T(8,128)} custom-call(s32[5]{0:T(128)} %stack.47.place_ref, bf16[128,128,128]{2,1,0:T(8,128)(2,1)} %all-to-all-done.1.schur_in_ref, s32[2,1,1024]{2,1,0:T(1,128)} %bitcast.53, s32[2,2,1024,1]{3,2,1,0:T(8,128)} %reshape.43.col_map_ref, bf16[1024,2048]{1,0:T(8,128)(2,1)} %base_ref.3), custom_call_target="tpu_custom_call" | custom-call | flops 8589934592 | bytes 10485760 | tf_op jit(solution)/shard_map/place/pallas_call | solution.py:183
  216.8 33.0 %all-to-all-done.schur_in_ref = bf16[128,128,128]{2,1,0:T(8,128)(2,1)} async-done(((bf16[128,128,128]{2,1,0:T(8,128)(2,1)}), bf16[128,128,128]{2,1,0:T(8,128)(2,1)}, u32[]{:S(2)}, u32[]{:S(2)}) %all-to-all-start) | async-done | bytes 4194336 | tf_op jit(solution)/shard_map/all_to_all | solution.py:252
  249.8 15.3 %place.3 = f32[1024,2048]{1,0:T(8,128)} custom-call(s32[5]{0:T(128)} %stack.47.place_ref, bf16[128,128,128]{2,1,0:T(8,128)(2,1)} %all-to-all-done.schur_in_ref, s32[2,1,1024]{2,1,0:T(1,128)} %bitcast.54, s32[2,2,1024,1]{3,2,1,0:T(8,128)} %reshape.43.col_map_ref, bf16[1024,2048]{1,0:T(8,128)(2,1)} %base_ref.3, ...), custom_call_target="tpu_custom_call", output_to_operand_aliasing={{}: (5, {})} | custom-call | flops 8589934592 | bytes 10485760 | tf_op jit(solution)/shard_map/place/pallas_call | solution.py:183
  (11 shorter events, 0.1 us)
Async XLA Ops:
  0.0 30.2 %collective-permute-start.1 = (bf16[2048,128]{1,0:T(8,128)(2,1)}, bf16[2048,128]{1,0:T(8,128)(2,1)S(1)}, u32[]{:S(2)}, u32[]{:S(2)}) collective-permute-start(bf16[2048,128]{1,0:T(8,128)(2,1)} %bitcast.42), channel_id=1, source_target_pairs={{0,4},{1,5},{2,6},{3,7},{4,0},{5,1},{6,2},{7,3},{8,12},{9,13},{10,... | collective-permute-start | bytes 1572872 | tf_op jit(solution)/shard_map/ppermute | solution.py:24
  3.6 37.9 %collective-permute-start = (bf16[3072,128]{1,0:T(8,128)(2,1)S(1)}, bf16[3072,128]{1,0:T(8,128)(2,1)S(1)}, u32[]{:S(2)}, u32[]{:S(2)}) collective-permute-start(bf16[3072,128]{1,0:T(8,128)(2,1)S(1)} %pad_maximum_fusion.2), channel_id=1, source_target_pairs={{0,0},{1,8},{2,16},{3,24},{4,32},{5,40},{6,48},{7,56},{8,1},{9,9},... | collective-permute-start | bytes 2359304 | tf_op jit(solution)/shard_map/ppermute | solution.py:24
  31.5 62.5 %copy-start.1 = (bf16[2,2048,128]{2,1,0:T(8,128)(2,1)}, bf16[2,2048,128]{2,1,0:T(8,128)(2,1)S(1)}, u32[]{:S(2)}) copy-start(bf16[2,2048,128]{2,1,0:T(8,128)(2,1)S(1)} %pad_maximum_fusion.1.near_ref) | copy-start | bytes 3145732
  41.6 52.4 %copy-start.2 = (bf16[3072,128]{1,0:T(8,128)(2,1)}, bf16[3072,128]{1,0:T(8,128)(2,1)S(1)}, u32[]{:S(2)}) copy-start(bf16[3072,128]{1,0:T(8,128)(2,1)S(1)} %collective-permute-done) | copy-start | bytes 2359300
  41.6 40.8 %collective-permute-start.5 = (bf16[2,2048,128]{2,1,0:T(8,128)(2,1)S(1)}, bf16[2,2048,128]{2,1,0:T(8,128)(2,1)S(1)}, u32[]{:S(2)}, u32[]{:S(2)}) collective-permute-start(bf16[2,2048,128]{2,1,0:T(8,128)(2,1)S(1)} %pad_maximum_fusion.1.near_ref), channel_id=1, source_target_pairs={{0,3},{1,0},{2,1},{3,2},{4,7},{5,4},{6,5},{7,6},{8,11},{9,8},{10,9... | collective-permute-start | bytes 3145736 | tf_op jit(solution)/shard_map/ppermute | solution.py:24
  41.6 40.8 %collective-permute-start.4 = (bf16[2,2048,128]{2,1,0:T(8,128)(2,1)S(1)}, bf16[2,2048,128]{2,1,0:T(8,128)(2,1)S(1)}, u32[]{:S(2)}, u32[]{:S(2)}) collective-permute-start(bf16[2,2048,128]{2,1,0:T(8,128)(2,1)S(1)} %pad_maximum_fusion.1.near_ref), channel_id=1, source_target_pairs={{0,1},{1,2},{2,3},{3,0},{4,5},{5,6},{6,7},{7,4},{8,9},{9,10},{10,1... | collective-permute-start | bytes 3145736 | tf_op jit(solution)/shard_map/ppermute | solution.py:24
  43.1 39.3 %collective-permute-start.3 = (bf16[3072,128]{1,0:T(8,128)(2,1)S(1)}, bf16[3072,128]{1,0:T(8,128)(2,1)S(1)}, u32[]{:S(2)}, u32[]{:S(2)}) collective-permute-start(bf16[3072,128]{1,0:T(8,128)(2,1)S(1)} %collective-permute-done), channel_id=1, source_target_pairs={{0,48},{1,49},{2,50},{3,51},{4,52},{5,53},{6,54},{7,55},{8,56},{9,... | collective-permute-start | bytes 2359304 | tf_op jit(solution)/shard_map/ppermute | solution.py:24
  50.5 31.9 %collective-permute-start.2 = (bf16[3072,128]{1,0:T(8,128)(2,1)S(1)}, bf16[3072,128]{1,0:T(8,128)(2,1)S(1)}, u32[]{:S(2)}, u32[]{:S(2)}) collective-permute-start(bf16[3072,128]{1,0:T(8,128)(2,1)S(1)} %collective-permute-done), channel_id=1, source_target_pairs={{0,16},{1,17},{2,18},{3,19},{4,20},{5,21},{6,22},{7,23},{8,24},{9,... | collective-permute-start | bytes 2359304 | tf_op jit(solution)/shard_map/ppermute | solution.py:24
  50.5 33.9 %collective-permute-start.8 = (bf16[3072,128]{1,0:T(8,128)(2,1)S(1)}, bf16[3072,128]{1,0:T(8,128)(2,1)S(1)}, u32[]{:S(2)}, u32[]{:S(2)}) collective-permute-start(bf16[3072,128]{1,0:T(8,128)(2,1)S(1)} %collective-permute-done), channel_id=1, source_target_pairs={{0,32},{1,33},{2,34},{3,35},{4,36},{5,37},{6,38},{7,39},{8,40},{9,... | collective-permute-start | bytes 2359304 | tf_op jit(solution)/shard_map/ppermute | solution.py:24
  82.4 11.6 %copy-start.3 = (bf16[2,2048,128]{2,1,0:T(8,128)(2,1)}, bf16[2,2048,128]{2,1,0:T(8,128)(2,1)S(1)}, u32[]{:S(2)}) copy-start(bf16[2,2048,128]{2,1,0:T(8,128)(2,1)S(1)} %collective-permute-done.5.ahead_ref) | copy-start | bytes 3145732
  82.4 11.6 %copy-start.4 = (bf16[2,2048,128]{2,1,0:T(8,128)(2,1)}, bf16[2,2048,128]{2,1,0:T(8,128)(2,1)S(1)}, u32[]{:S(2)}) copy-start(bf16[2,2048,128]{2,1,0:T(8,128)(2,1)S(1)} %collective-permute-done.4.behind_ref) | copy-start | bytes 3145732
  82.5 8.4 %collective-permute-start.7 = (bf16[2048,128]{1,0:T(8,128)(2,1)S(1)}, bf16[2048,128]{1,0:T(8,128)(2,1)S(1)}, u32[]{:S(2)}, u32[]{:S(2)}) collective-permute-start(bf16[2048,128]{1,0:T(8,128)(2,1)S(1)} %slice_bitcast_fusion), channel_id=1, source_target_pairs={{0,3},{1,0},{2,1},{3,2},{4,7},{5,4},{6,5},{7,6},{8,11},{9,8},{10,9... | collective-permute-start | bytes 1572872 | tf_op jit(solution)/shard_map/ppermute | solution.py:24
  84.1 9.9 %collective-permute-start.6 = (bf16[2048,128]{1,0:T(8,128)(2,1)S(1)}, bf16[2048,128]{1,0:T(8,128)(2,1)S(1)}, u32[]{:S(2)}, u32[]{:S(2)}) collective-permute-start(bf16[2048,128]{1,0:T(8,128)(2,1)S(1)} %slice_bitcast_fusion.1), channel_id=1, source_target_pairs={{0,1},{1,2},{2,3},{3,0},{4,5},{5,6},{6,7},{7,4},{8,9},{9,10},{10,1... | collective-permute-start | bytes 1572872 | tf_op jit(solution)/shard_map/ppermute | solution.py:24
  90.9 3.1 %copy-start.6 = (bf16[2048,128]{1,0:T(8,128)(2,1)}, bf16[2048,128]{1,0:T(8,128)(2,1)S(1)}, u32[]{:S(2)}) copy-start(bf16[2048,128]{1,0:T(8,128)(2,1)S(1)} %collective-permute-done.7.far_second_ref) | copy-start | bytes 1572868
  93.9 0.8 copy-start.7
  96.2 11.2 %copy-start = (bf16[4,3072,128]{2,1,0:T(8,128)(2,1)}, bf16[4,3072,128]{2,1,0:T(8,128)(2,1)S(1)}, u32[]{:S(2)}) copy-start(bf16[4,3072,128]{2,1,0:T(8,128)(2,1)S(1)} %pad_maximum_fusion.mine_ref.inverse_mine_ref) | copy-start | bytes 9437188
  96.2 11.2 %collective-permute-start.9 = (bf16[4,3072,128]{2,1,0:T(8,128)(2,1)S(1)}, bf16[4,3072,128]{2,1,0:T(8,128)(2,1)}, u32[]{:S(2)}, u32[]{:S(2)}) collective-permute-start(bf16[4,3072,128]{2,1,0:T(8,128)(2,1)S(1)} %pad_maximum_fusion.mine_ref.inverse_mine_ref), channel_id=1, source_target_pairs={{0,8},{1,9},{2,10},{3,11},{4,12},{5,13},{6,14},{7,15},{8,0},{9,1},... | collective-permute-start | bytes 9437192 | tf_op jit(solution)/shard_map/ppermute | solution.py:24
  130.1 60.8 %all-to-all-start.1 = ((bf16[128,128,128]{2,1,0:T(8,128)(2,1)}), bf16[128,128,128]{2,1,0:T(8,128)(2,1)}, u32[]{:S(2)}, u32[]{:S(2)}) async-start(bf16[128,128,128]{2,1,0:T(8,128)(2,1)} %bitcast.41), calls=%async_computation.1 | async-start | bytes 8388608 | tf_op jit(solution)/shard_map/all_to_all | solution.py:252
  190.9 6.5 %copy-start.5 = (s32[2,16384]{1,0:T(2,128)S(1)}, s32[2,16384]{1,0:T(2,128)}, u32[]{:S(2)}) copy-start(s32[2,16384]{1,0:T(2,128)} %param.8) | copy-start | bytes 393220
  190.9 58.9 %all-to-all-start = ((bf16[128,128,128]{2,1,0:T(8,128)(2,1)}), bf16[128,128,128]{2,1,0:T(8,128)(2,1)}, u32[]{:S(2)}, u32[]{:S(2)}) async-start(bf16[128,128,128]{2,1,0:T(8,128)(2,1)} %bitcast.40), calls=%async_computation | async-start | bytes 8388608 | tf_op jit(solution)/shard_map/all_to_all | solution.py:252

commit v3 on v2

--- a/solution.py
+++ b/solution.py
@@ -24,7 +24,7 @@
     return lax.ppermute(array, ALL, pairs)
 
 
-LOWER_ROWS = 512
+LOWER_ROWS = 1024
 
 
 def lower_kernel(
@@ -43,7 +43,7 @@
     inverse_ref,
     wide_ref,
 ):
-    x, core, y = place_ref[0], place_ref[1], place_ref[4]
+    turn, core, y = place_ref[0], place_ref[1], place_ref[4]
 
     def columns(chunk):
         return pl.ds(pl.multiple_of(chunk * 128, 128), 128)
@@ -52,7 +52,7 @@
     def _():
         for ref, part in ((inverse_mine_ref, core), (inverse_other_ref, 1 - core)):
             for index, away in enumerate((0, 3, 1, 2)):
-                inverse_ref[:, columns(((x + away) % 4) * 2 + part)] = ref[index]
+                inverse_ref[:, columns(((turn + away) % 4) * 2 + part)] = ref[index]
 
     def lower(out_ref):
         for n in range(4):
@@ -72,7 +72,7 @@
     lower(left_ref)
     for ref, part in ((mine_ref, core), (other_ref, 1 - core)):
         for index, away in enumerate((0, 3, 1, 2)):
-            wide_ref[:, columns(((x + away) % 4) * 2 + part)] = ref[index]
+            wide_ref[:, columns(((turn + away) % 4) * 2 + part)] = ref[index]
     lower(right_ref)
 
 
@@ -106,16 +106,16 @@
 
 def schur_kernel(left_ref, right_ref, front_even_ref, front_odd_ref, out_ref):
     block = right_ref[...].reshape(256, 1024)
-    for part in range(4):
-        rows = slice(part * 512, (part + 1) * 512)
-        product = lax.dot_general(
-            left_ref[rows, :], block, ROWS_AXIS, preferred_element_type=F32
-        )
-        for which, front_ref in enumerate((front_even_ref, front_odd_ref)):
-            lanes = slice(which * 128, (which + 1) * 128)
-            schur = (front_ref[rows, :].astype(F32) - product[:, lanes]).astype(BF16)
-            for k in range(4):
-                out_ref[part * 4 + k, which] = schur[k * 128 : (k + 1) * 128]
+    product = lax.dot_general(
+        left_ref[...], block, ROWS_AXIS, preferred_element_type=F32
+    )
+    for which, front_ref in enumerate((front_even_ref, front_odd_ref)):
+        lanes = slice(which * 128, (which + 1) * 128)
+        for k in range(16):
+            rows = slice(k * 128, (k + 1) * 128)
+            out_ref[k, which] = (
+                front_ref[rows, :].astype(F32) - product[rows, lanes]
+            ).astype(BF16)
 
 
 def schur_parcels(b, left, right, front):
@@ -206,10 +206,10 @@
     col = lax.axis_index("col")
     x, core = row // 2, row % 2
     target = half * 8 + row
-    place = jnp.stack([x, core, target, col, col % 4]).astype(jnp.int32)
+    place = jnp.stack([(x + 4 - col // 2) % 4, core, target, col, col % 4]).astype(jnp.int32)
 
     turned = shift(
-        jnp.concatenate([panel[0], inverse_block[0]]), lambda h, r, c: (h, c, r)
+        jnp.concatenate([panel[0], inverse_block[0]]), lambda h, r, c: (h, (c // 2 + r // 2) % 4 * 2 + c % 2, r)
     )
     twin = shift(panel[0], lambda h, r, c: (h, r, c ^ 4))
     pair = jnp.stack(

time: 266 us -> 253 us (0.951)
  waiting for transfers between devices: 154 us -> 120 us
  starting transfers between devices: 38.9 us -> 58.7 us
    ppermute x10, waiting for transfers between devices: 77.9 us -> 44.4 us  [shift(): return lax.ppermute(array, ALL, pairs)]
    ppermute x10, starting transfers between devices: 24 us -> 46.9 us  [shift(): return lax.ppermute(array, ALL, pairs)]
    all_to_all x2, starting transfers between devices: 14.9 us -> 11.9 us  [body(): lax.all_to_all(parcels.reshape(128, 128, 128), ALL, 0, 0, tiled=True)]
  transfers between devices with their start and end apart: 12 -> 12, of which waited for: 9 -> 9; matrix products, arithmetic and copies ran while one was open for 3% -> 3% of each run, Pallas kernels for 9% -> 10%
where the time goes in v3:
time: 253 us
  waiting for transfers between devices  120 us (47%)
  Pallas kernels  64 us (25%)
  starting transfers between devices  58.7 us (23%)
  local copies, waits for them, and re-layouts  4.97 us (2%)
  other arithmetic  4.49 us (2%)
    all_to_all x2, waiting for transfers between devices, body(): lax.all_to_all(parcels.reshape(128, 128, 128), ALL, 0, 0, tiled=True)  75.8 us
    ppermute x10, starting transfers between devices, shift(): return lax.ppermute(array, ALL, pairs)  46.9 us
    ppermute x10, waiting for transfers between devices, shift(): return lax.ppermute(array, ALL, pairs)  44.4 us
    pallas_call x2, Pallas kernels, place_children(): pl.pallas_call(functools.partial(place_kernel, b), grid_spec=grid_spec, o...  30.7 us
    pallas_call x2, Pallas kernels, schur_parcels(): pl.pallas_call(schur_kernel, grid=(4,), in_specs=[pl.BlockSpec((2048, 102...  19.1 us
    pallas_call x1, Pallas kernels, lower_rows(): pl.pallas_call(lower_kernel, grid_spec=grid_spec, out_shape=[out, out], c...  14.2 us
    all_to_all x2, starting transfers between devices, body(): lax.all_to_all(parcels.reshape(128, 128, 128), ALL, 0, 0, tiled=True)  11.9 us
  transfers between devices with their start and end apart: 12, of which 9 were waited for; matrix products, arithmetic and copies ran while one was open for 3% of the time, Pallas kernels for 10%

profile of v3, /device:TPU:1, one launch (start us, length us, event | category | flops | bytes accessed | tf_op | source)
XLA Modules:
  0.0 252.6 jit_solution(8368763107463384915)
XLA Ops:
  0.0 2.5 collective-permute-start.1
  2.5 1.2 pad_maximum_fusion.2
  3.6 4.0 %collective-permute-start = (bf16[3072,128]{1,0:T(8,128)(2,1)S(1)}, bf16[3072,128]{1,0:T(8,128)(2,1)S(1)}, u32[]{:S(2)}, u32[]{:S(2)}) collective-permute-start(bf16[3072,128]{1,0:T(8,128)(2,1)S(1)} %pad_maximum_fusion.2), channel_id=1, source_target_pairs={{0,0},{1,8},{2,16},{3,24},{4,32},{5,40},{6,48},{7,56},{8,1},{9,9},... | collective-permute-start | bytes 2359304 | tf_op jit(solution)/shard_map/ppermute | solution.py:24
  7.7 6.6 %collective-permute-done.1 = bf16[2048,128]{1,0:T(8,128)(2,1)S(1)} collective-permute-done((bf16[2048,128]{1,0:T(8,128)(2,1)}, bf16[2048,128]{1,0:T(8,128)(2,1)S(1)}, u32[]{:S(2)}, u32[]{:S(2)}) %collective-permute-start.1) | collective-permute-done | bytes 524320 | tf_op jit(solution)/shard_map/ppermute | solution.py:24
  14.3 1.1 select_bitcast_fusion.1
  15.4 0.1 pad_maximum_fusion.1.near_ref
  15.5 0.0 copy-start.1
  15.5 1.8 collective-permute-done
  17.4 17.8 %collective-permute-start.5 = (bf16[2,2048,128]{2,1,0:T(8,128)(2,1)S(1)}, bf16[2,2048,128]{2,1,0:T(8,128)(2,1)S(1)}, u32[]{:S(2)}, u32[]{:S(2)}) collective-permute-start(bf16[2,2048,128]{2,1,0:T(8,128)(2,1)S(1)} %pad_maximum_fusion.1.near_ref), channel_id=1, source_target_pairs={{0,3},{1,0},{2,1},{3,2},{4,7},{5,4},{6,5},{7,6},{8,11},{9,8},{10,9... | collective-permute-start | bytes 3145736 | tf_op jit(solution)/shard_map/ppermute | solution.py:24
  35.1 0.0 collective-permute-start.4
  35.1 2.5 collective-permute-start.3
  37.6 0.0 collective-permute-start.2
  37.6 1.2 collective-permute-start.8
  38.8 14.8 %collective-permute-done.3 = bf16[3072,128]{1,0:T(8,128)(2,1)S(1)} collective-permute-done((bf16[3072,128]{1,0:T(8,128)(2,1)S(1)}, bf16[3072,128]{1,0:T(8,128)(2,1)S(1)}, u32[]{:S(2)}, u32[]{:S(2)}) %collective-permute-start.3) | collective-permute-done | bytes 786464 | tf_op jit(solution)/shard_map/ppermute | solution.py:24
  53.6 3.5 %collective-permute-done.2 = bf16[3072,128]{1,0:T(8,128)(2,1)S(1)} collective-permute-done((bf16[3072,128]{1,0:T(8,128)(2,1)S(1)}, bf16[3072,128]{1,0:T(8,128)(2,1)S(1)}, u32[]{:S(2)}, u32[]{:S(2)}) %collective-permute-start.2) | collective-permute-done | bytes 786464 | tf_op jit(solution)/shard_map/ppermute | solution.py:24
  57.1 0.0 collective-permute-done.5.ahead_ref
  57.1 2.2 collective-permute-done.4.behind_ref
  59.4 0.4 collective-permute-start.7
  59.8 1.2 collective-permute-start.6
  61.0 10.7 %collective-permute-done.8 = bf16[3072,128]{1,0:T(8,128)(2,1)S(1)} collective-permute-done((bf16[3072,128]{1,0:T(8,128)(2,1)S(1)}, bf16[3072,128]{1,0:T(8,128)(2,1)S(1)}, u32[]{:S(2)}, u32[]{:S(2)}) %collective-permute-start.8) | collective-permute-done | bytes 786464 | tf_op jit(solution)/shard_map/ppermute | solution.py:24
  71.6 0.0 collective-permute-done.7.far_second_ref
  71.6 0.0 collective-permute-done.6.far_first_ref
  71.6 0.0 copy-start.7
  71.6 0.0 copy-done.1
  71.6 0.0 copy-done.2
  71.7 0.0 copy-done.3
  71.7 0.0 copy-done.4
  71.7 0.8 copy-done.6
  72.4 0.2 copy-done.7
  72.6 1.4 pad_maximum_fusion.mine_ref.inverse_mine_ref
  74.0 0.0 copy-start
  74.0 17.4 %collective-permute-start.9 = (bf16[4,3072,128]{2,1,0:T(8,128)(2,1)S(1)}, bf16[4,3072,128]{2,1,0:T(8,128)(2,1)}, u32[]{:S(2)}, u32[]{:S(2)}) collective-permute-start(bf16[4,3072,128]{2,1,0:T(8,128)(2,1)S(1)} %pad_maximum_fusion.mine_ref.inverse_mine_ref), channel_id=1, source_target_pairs={{0,8},{1,9},{2,10},{3,11},{4,12},{5,13},{6,14},{7,15},{8,0},{9,1},... | collective-permute-start | bytes 9437192 | tf_op jit(solution)/shard_map/ppermute | solution.py:24
  91.5 0.6 stack.47.place_ref
  92.1 4.8 %collective-permute-done.9.other_ref.inverse_other_ref = bf16[4,3072,128]{2,1,0:T(8,128)(2,1)} collective-permute-done((bf16[4,3072,128]{2,1,0:T(8,128)(2,1)S(1)}, bf16[4,3072,128]{2,1,0:T(8,128)(2,1)}, u32[]{:S(2)}, u32[]{:S(2)}) %collective-permute-start.9) | collective-permute-done | bytes 3145760 | tf_op jit(solution)/shard_map/ppermute | solution.py:24
  96.9 0.0 copy-done
  96.9 14.2 %lower.1 = (bf16[2048,1024]{1,0:T(8,128)(2,1)}, bf16[2048,1024]{1,0:T(8,128)(2,1)}) custom-call(s32[5]{0:T(128)} %stack.47.place_ref, bf16[2,2048,128]{2,1,0:T(8,128)(2,1)} %copy-done.1, bf16[2,2048,128]{2,1,0:T(8,128)(2,1)} %copy-done.4, bf16[2,2048,128]{2,1,0:T(8,128)(2,1)} %copy-done.3, bf16[2048,128]{1,0:T(8,128)(2,1)} %copy-done.7, ...), custom_call_target="tpu_custom_call" | custom-call | flops 5368709120 | bytes 18874368 | tf_op jit(solution)/shard_map/lower/pallas_call | solution.py:95
  111.1 9.5 %schur.3 = bf16[16,8,128,128]{3,2,1,0:T(8,128)(2,1)} custom-call(bf16[2048,1024]{1,0:T(8,128)(2,1)} %get-tuple-element.25.left_ref, bf16[8,2,128,1024]{3,2,1,0:T(8,128)(2,1)} %bitcast.38, bf16[2048,2048]{1,0:T(8,128)(2,1)} %bitcast.34, bf16[2048,2048]{1,0:T(8,128)(2,1)} %bitcast.35), custom_call_target="tpu_custom_call" | custom-call | flops 4294967296 | bytes 14680064 | tf_op jit(solution)/shard_map/schur/pallas_call | solution.py:122
  120.6 5.4 %all-to-all-start.1 = ((bf16[128,128,128]{2,1,0:T(8,128)(2,1)}), bf16[128,128,128]{2,1,0:T(8,128)(2,1)}, u32[]{:S(2)}, u32[]{:S(2)}) async-start(bf16[128,128,128]{2,1,0:T(8,128)(2,1)} %bitcast.41), calls=%async_computation.1 | async-start | bytes 8388608 | tf_op jit(solution)/shard_map/all_to_all | solution.py:252
  126.0 9.6 %schur.2 = bf16[16,8,128,128]{3,2,1,0:T(8,128)(2,1)} custom-call(bf16[2048,1024]{1,0:T(8,128)(2,1)} %get-tuple-element.25.left_ref, bf16[8,2,128,1024]{3,2,1,0:T(8,128)(2,1)} %bitcast.39, bf16[2048,2048]{1,0:T(8,128)(2,1)} %bitcast.36, bf16[2048,2048]{1,0:T(8,128)(2,1)} %bitcast.37), custom_call_target="tpu_custom_call" | custom-call | flops 4294967296 | bytes 14680064 | tf_op jit(solution)/shard_map/schur/pallas_call | solution.py:122
  135.6 42.8 %all-to-all-done.1.schur_in_ref = bf16[128,128,128]{2,1,0:T(8,128)(2,1)} async-done(((bf16[128,128,128]{2,1,0:T(8,128)(2,1)}), bf16[128,128,128]{2,1,0:T(8,128)(2,1)}, u32[]{:S(2)}, u32[]{:S(2)}) %all-to-all-start.1) | async-done | bytes 4194336 | tf_op jit(solution)/shard_map/all_to_all | solution.py:252
  178.4 6.5 %all-to-all-start = ((bf16[128,128,128]{2,1,0:T(8,128)(2,1)}), bf16[128,128,128]{2,1,0:T(8,128)(2,1)}, u32[]{:S(2)}, u32[]{:S(2)}) async-start(bf16[128,128,128]{2,1,0:T(8,128)(2,1)} %bitcast.40), calls=%async_computation | async-start | bytes 8388608 | tf_op jit(solution)/shard_map/all_to_all | solution.py:252
  184.9 0.0 copy-done.5
  185.0 0.1 fusion
  185.0 3.3 %reshape.43.col_map_ref = s32[2,2,1024,1]{3,2,1,0:T(8,128)} reshape(s32[2,2,8,128]{3,2,1,0:T(8,128)S(1)} %fusion) | data formatting | bytes 32768 | tf_op jit(solution)/shard_map/reshape | solution.py:247
  188.3 0.6 broadcast_subtract_fusion
  188.9 15.3 %place.2.refs_0_ = f32[1024,2048]{1,0:T(8,128)} custom-call(s32[5]{0:T(128)} %stack.47.place_ref, bf16[128,128,128]{2,1,0:T(8,128)(2,1)} %all-to-all-done.1.schur_in_ref, s32[2,1,1024]{2,1,0:T(1,128)} %bitcast.53, s32[2,2,1024,1]{3,2,1,0:T(8,128)} %reshape.43.col_map_ref, bf16[1024,2048]{1,0:T(8,128)(2,1)} %base_ref.3), custom_call_target="tpu_custom_call" | custom-call | flops 8589934592 | bytes 10485760 | tf_op jit(solution)/shard_map/place/pallas_call | solution.py:183
  204.3 33.0 %all-to-all-done.schur_in_ref = bf16[128,128,128]{2,1,0:T(8,128)(2,1)} async-done(((bf16[128,128,128]{2,1,0:T(8,128)(2,1)}), bf16[128,128,128]{2,1,0:T(8,128)(2,1)}, u32[]{:S(2)}, u32[]{:S(2)}) %all-to-all-start) | async-done | bytes 4194336 | tf_op jit(solution)/shard_map/all_to_all | solution.py:252
  237.3 15.3 %place.3 = f32[1024,2048]{1,0:T(8,128)} custom-call(s32[5]{0:T(128)} %stack.47.place_ref, bf16[128,128,128]{2,1,0:T(8,128)(2,1)} %all-to-all-done.schur_in_ref, s32[2,1,1024]{2,1,0:T(1,128)} %bitcast.54, s32[2,2,1024,1]{3,2,1,0:T(8,128)} %reshape.43.col_map_ref, bf16[1024,2048]{1,0:T(8,128)(2,1)} %base_ref.3, ...), custom_call_target="tpu_custom_call", output_to_operand_aliasing={{}: (5, {})} | custom-call | flops 8589934592 | bytes 10485760 | tf_op jit(solution)/shard_map/place/pallas_call | solution.py:183
  (11 shorter events, 0.1 us)
Async XLA Ops:
  0.0 14.3 %collective-permute-start.1 = (bf16[2048,128]{1,0:T(8,128)(2,1)}, bf16[2048,128]{1,0:T(8,128)(2,1)S(1)}, u32[]{:S(2)}, u32[]{:S(2)}) collective-permute-start(bf16[2048,128]{1,0:T(8,128)(2,1)} %bitcast.42), channel_id=1, source_target_pairs={{0,4},{1,5},{2,6},{3,7},{4,0},{5,1},{6,2},{7,3},{8,12},{9,13},{10,... | collective-permute-start | bytes 1572872 | tf_op jit(solution)/shard_map/ppermute | solution.py:24
  3.6 13.7 %collective-permute-start = (bf16[3072,128]{1,0:T(8,128)(2,1)S(1)}, bf16[3072,128]{1,0:T(8,128)(2,1)S(1)}, u32[]{:S(2)}, u32[]{:S(2)}) collective-permute-start(bf16[3072,128]{1,0:T(8,128)(2,1)S(1)} %pad_maximum_fusion.2), channel_id=1, source_target_pairs={{0,0},{1,8},{2,16},{3,24},{4,32},{5,40},{6,48},{7,56},{8,1},{9,9},... | collective-permute-start | bytes 2359304 | tf_op jit(solution)/shard_map/ppermute | solution.py:24
  15.5 56.1 %copy-start.1 = (bf16[2,2048,128]{2,1,0:T(8,128)(2,1)}, bf16[2,2048,128]{2,1,0:T(8,128)(2,1)S(1)}, u32[]{:S(2)}) copy-start(bf16[2,2048,128]{2,1,0:T(8,128)(2,1)S(1)} %pad_maximum_fusion.1.near_ref) | copy-start | bytes 3145732
  17.4 54.3 %copy-start.2 = (bf16[3072,128]{1,0:T(8,128)(2,1)}, bf16[3072,128]{1,0:T(8,128)(2,1)S(1)}, u32[]{:S(2)}) copy-start(bf16[3072,128]{1,0:T(8,128)(2,1)S(1)} %collective-permute-done) | copy-start | bytes 2359300
  17.4 39.8 %collective-permute-start.5 = (bf16[2,2048,128]{2,1,0:T(8,128)(2,1)S(1)}, bf16[2,2048,128]{2,1,0:T(8,128)(2,1)S(1)}, u32[]{:S(2)}, u32[]{:S(2)}) collective-permute-start(bf16[2,2048,128]{2,1,0:T(8,128)(2,1)S(1)} %pad_maximum_fusion.1.near_ref), channel_id=1, source_target_pairs={{0,3},{1,0},{2,1},{3,2},{4,7},{5,4},{6,5},{7,6},{8,11},{9,8},{10,9... | collective-permute-start | bytes 3145736 | tf_op jit(solution)/shard_map/ppermute | solution.py:24
  35.1 24.2 %collective-permute-start.4 = (bf16[2,2048,128]{2,1,0:T(8,128)(2,1)S(1)}, bf16[2,2048,128]{2,1,0:T(8,128)(2,1)S(1)}, u32[]{:S(2)}, u32[]{:S(2)}) collective-permute-start(bf16[2,2048,128]{2,1,0:T(8,128)(2,1)S(1)} %pad_maximum_fusion.1.near_ref), channel_id=1, source_target_pairs={{0,1},{1,2},{2,3},{3,0},{4,5},{5,6},{6,7},{7,4},{8,9},{9,10},{10,1... | collective-permute-start | bytes 3145736 | tf_op jit(solution)/shard_map/ppermute | solution.py:24
  35.1 18.5 %collective-permute-start.3 = (bf16[3072,128]{1,0:T(8,128)(2,1)S(1)}, bf16[3072,128]{1,0:T(8,128)(2,1)S(1)}, u32[]{:S(2)}, u32[]{:S(2)}) collective-permute-start(bf16[3072,128]{1,0:T(8,128)(2,1)S(1)} %collective-permute-done), channel_id=1, source_target_pairs={{0,48},{1,49},{2,50},{3,51},{4,52},{5,53},{6,54},{7,55},{8,56},{9,... | collective-permute-start | bytes 2359304 | tf_op jit(solution)/shard_map/ppermute | solution.py:24
  37.6 19.5 %collective-permute-start.2 = (bf16[3072,128]{1,0:T(8,128)(2,1)S(1)}, bf16[3072,128]{1,0:T(8,128)(2,1)S(1)}, u32[]{:S(2)}, u32[]{:S(2)}) collective-permute-start(bf16[3072,128]{1,0:T(8,128)(2,1)S(1)} %collective-permute-done), channel_id=1, source_target_pairs={{0,16},{1,17},{2,18},{3,19},{4,20},{5,21},{6,22},{7,23},{8,24},{9,... | collective-permute-start | bytes 2359304 | tf_op jit(solution)/shard_map/ppermute | solution.py:24
  37.6 34.0 %collective-permute-start.8 = (bf16[3072,128]{1,0:T(8,128)(2,1)S(1)}, bf16[3072,128]{1,0:T(8,128)(2,1)S(1)}, u32[]{:S(2)}, u32[]{:S(2)}) collective-permute-start(bf16[3072,128]{1,0:T(8,128)(2,1)S(1)} %collective-permute-done), channel_id=1, source_target_pairs={{0,32},{1,33},{2,34},{3,35},{4,36},{5,37},{6,38},{7,39},{8,40},{9,... | collective-permute-start | bytes 2359304 | tf_op jit(solution)/shard_map/ppermute | solution.py:24
  57.1 14.5 %copy-start.3 = (bf16[2,2048,128]{2,1,0:T(8,128)(2,1)}, bf16[2,2048,128]{2,1,0:T(8,128)(2,1)S(1)}, u32[]{:S(2)}) copy-start(bf16[2,2048,128]{2,1,0:T(8,128)(2,1)S(1)} %collective-permute-done.5.ahead_ref) | copy-start | bytes 3145732
  59.3 12.3 %copy-start.4 = (bf16[2,2048,128]{2,1,0:T(8,128)(2,1)}, bf16[2,2048,128]{2,1,0:T(8,128)(2,1)S(1)}, u32[]{:S(2)}) copy-start(bf16[2,2048,128]{2,1,0:T(8,128)(2,1)S(1)} %collective-permute-done.4.behind_ref) | copy-start | bytes 3145732
  59.4 12.2 %collective-permute-start.7 = (bf16[2048,128]{1,0:T(8,128)(2,1)S(1)}, bf16[2048,128]{1,0:T(8,128)(2,1)S(1)}, u32[]{:S(2)}, u32[]{:S(2)}) collective-permute-start(bf16[2048,128]{1,0:T(8,128)(2,1)S(1)} %slice_bitcast_fusion), channel_id=1, source_target_pairs={{0,3},{1,0},{2,1},{3,2},{4,7},{5,4},{6,5},{7,6},{8,11},{9,8},{10,9... | collective-permute-start | bytes 1572872 | tf_op jit(solution)/shard_map/ppermute | solution.py:24
  59.8 11.8 %collective-permute-start.6 = (bf16[2048,128]{1,0:T(8,128)(2,1)S(1)}, bf16[2048,128]{1,0:T(8,128)(2,1)S(1)}, u32[]{:S(2)}, u32[]{:S(2)}) collective-permute-start(bf16[2048,128]{1,0:T(8,128)(2,1)S(1)} %slice_bitcast_fusion.1), channel_id=1, source_target_pairs={{0,1},{1,2},{2,3},{3,0},{4,5},{5,6},{6,7},{7,4},{8,9},{9,10},{10,1... | collective-permute-start | bytes 1572872 | tf_op jit(solution)/shard_map/ppermute | solution.py:24
  71.6 0.8 copy-start.6
  71.6 1.0 copy-start.7
  74.0 22.9 %copy-start = (bf16[4,3072,128]{2,1,0:T(8,128)(2,1)}, bf16[4,3072,128]{2,1,0:T(8,128)(2,1)S(1)}, u32[]{:S(2)}) copy-start(bf16[4,3072,128]{2,1,0:T(8,128)(2,1)S(1)} %pad_maximum_fusion.mine_ref.inverse_mine_ref) | copy-start | bytes 9437188
  74.0 22.8 %collective-permute-start.9 = (bf16[4,3072,128]{2,1,0:T(8,128)(2,1)S(1)}, bf16[4,3072,128]{2,1,0:T(8,128)(2,1)}, u32[]{:S(2)}, u32[]{:S(2)}) collective-permute-start(bf16[4,3072,128]{2,1,0:T(8,128)(2,1)S(1)} %pad_maximum_fusion.mine_ref.inverse_mine_ref), channel_id=1, source_target_pairs={{0,8},{1,9},{2,10},{3,11},{4,12},{5,13},{6,14},{7,15},{8,0},{9,1},... | collective-permute-start | bytes 9437192 | tf_op jit(solution)/shard_map/ppermute | solution.py:24
  120.6 57.8 %all-to-all-start.1 = ((bf16[128,128,128]{2,1,0:T(8,128)(2,1)}), bf16[128,128,128]{2,1,0:T(8,128)(2,1)}, u32[]{:S(2)}, u32[]{:S(2)}) async-start(bf16[128,128,128]{2,1,0:T(8,128)(2,1)} %bitcast.41), calls=%async_computation.1 | async-start | bytes 8388608 | tf_op jit(solution)/shard_map/all_to_all | solution.py:252
  178.4 6.5 %copy-start.5 = (s32[2,16384]{1,0:T(2,128)S(1)}, s32[2,16384]{1,0:T(2,128)}, u32[]{:S(2)}) copy-start(s32[2,16384]{1,0:T(2,128)} %param.8) | copy-start | bytes 393220
  178.4 58.9 %all-to-all-start = ((bf16[128,128,128]{2,1,0:T(8,128)(2,1)}), bf16[128,128,128]{2,1,0:T(8,128)(2,1)}, u32[]{:S(2)}, u32[]{:S(2)}) async-start(bf16[128,128,128]{2,1,0:T(8,128)(2,1)} %bitcast.40), calls=%async_computation | async-start | bytes 8388608 | tf_op jit(solution)/shard_map/all_to_all | solution.py:252

commit v4 on v3

--- a/solution.py
+++ b/solution.py
@@ -24,10 +24,29 @@
     return lax.ppermute(array, ALL, pairs)
 
 
-LOWER_ROWS = 1024
-
-
-def lower_kernel(
+def spans(chunk):
+    return pl.ds(pl.multiple_of(chunk * 128, 128), 128)
+
+
+def gather_columns(place_ref, mine_ref, other_ref, out_ref):
+    turn, core = place_ref[0], place_ref[1]
+    for ref, part in ((mine_ref, core), (other_ref, 1 - core)):
+        for index, away in enumerate((0, 3, 1, 2)):
+            out_ref[:, spans((turn + away) % 4 * 2 + part)] = ref[index]
+
+
+def inverse_product(wide_ref, inverse_ref, out_ref):
+    for n in range(4):
+        reach = (n + 1) * 256
+        out_ref[:, n * 256 : reach] = lax.dot_general(
+            wide_ref[:, :reach],
+            inverse_ref[n * 256 : reach, :reach],
+            ROWS_AXIS,
+            preferred_element_type=F32,
+        ).astype(BF16)
+
+
+def first_kernel(
     place_ref,
     near_ref,
     behind_ref,
@@ -38,76 +57,103 @@
     other_ref,
     inverse_mine_ref,
     inverse_other_ref,
+    right_ref,
     left_ref,
-    right_ref,
     inverse_ref,
     wide_ref,
 ):
-    turn, core, y = place_ref[0], place_ref[1], place_ref[4]
-
-    def columns(chunk):
-        return pl.ds(pl.multiple_of(chunk * 128, 128), 128)
+    y = place_ref[4]
 
     @pl.when(pl.program_id(0) == 0)
     def _():
-        for ref, part in ((inverse_mine_ref, core), (inverse_other_ref, 1 - core)):
-            for index, away in enumerate((0, 3, 1, 2)):
-                inverse_ref[:, columns(((turn + away) % 4) * 2 + part)] = ref[index]
-
-    def lower(out_ref):
-        for n in range(4):
-            reach = (n + 1) * 256
-            out_ref[:, n * 256 : reach] = lax.dot_general(
-                wide_ref[:, :reach],
-                inverse_ref[n * 256 : reach, :reach],
-                ROWS_AXIS,
-                preferred_element_type=F32,
-            ).astype(BF16)
-
-    for ref, away in ((near_ref, 0), (behind_ref, 3), (ahead_ref, 1)):
-        for zl in range(2):
-            wide_ref[:, columns(zl * 4 + (y + away) % 4)] = ref[zl]
-    wide_ref[:, columns((y + 2) % 4)] = far_first_ref[...]
-    wide_ref[:, columns(4 + (y + 2) % 4)] = far_second_ref[...]
-    lower(left_ref)
-    for ref, part in ((mine_ref, core), (other_ref, 1 - core)):
-        for index, away in enumerate((0, 3, 1, 2)):
-            wide_ref[:, columns(((turn + away) % 4) * 2 + part)] = ref[index]
-    lower(right_ref)
-
-
-def lower_rows(place, rows, mine, other):
-    out = jax.ShapeDtypeStruct((2048, 1024), BF16)
-    pair = pl.BlockSpec((2, LOWER_ROWS, 128), lambda i, s: (0, i, 0))
-    single = pl.BlockSpec((LOWER_ROWS, 128), lambda i, s: (i, 0))
-    four = pl.BlockSpec((4, LOWER_ROWS, 128), lambda i, s: (0, i, 0))
-    inverse = pl.BlockSpec((4, 1024, 128), lambda i, s: (0, 2, 0))
+        gather_columns(place_ref, inverse_mine_ref, inverse_other_ref, inverse_ref)
+        gather_columns(place_ref, mine_ref, other_ref, wide_ref)
+        inverse_product(wide_ref, inverse_ref, right_ref)
+
+    @pl.when(pl.program_id(0) > 0)
+    def _():
+        for ref, away in ((near_ref, 0), (behind_ref, 3), (ahead_ref, 1)):
+            for zl in range(2):
+                wide_ref[:, spans(zl * 4 + (y + away) % 4)] = ref[zl]
+        wide_ref[:, spans((y + 2) % 4)] = far_first_ref[...]
+        wide_ref[:, spans(4 + (y + 2) % 4)] = far_second_ref[...]
+        inverse_product(wide_ref, inverse_ref, left_ref)
+
+
+FOUR_PANELS = pl.BlockSpec((4, 1024, 128), lambda i, s: (0, 0, 0))
+FOUR_INVERSES = pl.BlockSpec((4, 1024, 128), lambda i, s: (0, 1, 0))
+SQUARE = (1024, 1024)
+
+
+def lower_first(place, rows, mine, other):
+    def part(i):
+        return jnp.maximum(i - 1, 0)
+
+    pair = pl.BlockSpec((2, 1024, 128), lambda i, s: (0, part(i), 0))
+    single = pl.BlockSpec((1024, 128), lambda i, s: (part(i), 0))
     grid_spec = pltpu.PrefetchScalarGridSpec(
         num_scalar_prefetch=1,
-        grid=(2048 // LOWER_ROWS,),
-        in_specs=[pair] * 3 + [single] * 2 + [four] * 2 + [inverse] * 2,
-        out_specs=[pl.BlockSpec((LOWER_ROWS, 1024), lambda i, s: (i, 0))] * 2,
-        scratch_shapes=[
-            pltpu.VMEM((1024, 1024), BF16),
-            pltpu.VMEM((LOWER_ROWS, 1024), BF16),
+        grid=(3,),
+        in_specs=[pair] * 3 + [single] * 2 + [FOUR_PANELS] * 2 + [FOUR_INVERSES] * 2,
+        out_specs=[
+            pl.BlockSpec(SQUARE, lambda i, s: (0, 0)),
+            pl.BlockSpec(SQUARE, lambda i, s: (part(i), 0)),
         ],
+        scratch_shapes=[pltpu.VMEM(SQUARE, BF16), pltpu.VMEM(SQUARE, BF16)],
     )
     return pl.pallas_call(
-        lower_kernel,
+        first_kernel,
         grid_spec=grid_spec,
-        out_shape=[out, out],
+        out_shape=[
+            jax.ShapeDtypeStruct(SQUARE, BF16),
+            jax.ShapeDtypeStruct((2048, 1024), BF16),
+        ],
         compiler_params=pltpu.CompilerParams(vmem_limit_bytes=VMEM_LIMIT),
         cost_estimate=pl.CostEstimate(
-            flops=5 << 30, bytes_accessed=18 << 20, transcendentals=0
-        ),
-        name="lower",
+            flops=4 << 30, bytes_accessed=14 << 20, transcendentals=0
+        ),
+        name="lower_first",
     )(place, *rows, mine, other, mine, other)
 
 
+def right_kernel(
+    place_ref,
+    mine_ref,
+    other_ref,
+    inverse_mine_ref,
+    inverse_other_ref,
+    out_ref,
+    inverse_ref,
+    wide_ref,
+):
+    gather_columns(place_ref, inverse_mine_ref, inverse_other_ref, inverse_ref)
+    gather_columns(place_ref, mine_ref, other_ref, wide_ref)
+    inverse_product(wide_ref, inverse_ref, out_ref)
+
+
+def lower_right(place, mine, other, inverse_mine, inverse_other):
+    grid_spec = pltpu.PrefetchScalarGridSpec(
+        num_scalar_prefetch=1,
+        grid=(1,),
+        in_specs=[FOUR_PANELS] * 2 + [FOUR_INVERSES] * 2,
+        out_specs=pl.BlockSpec(SQUARE, lambda i, s: (0, 0)),
+        scratch_shapes=[pltpu.VMEM(SQUARE, BF16), pltpu.VMEM(SQUARE, BF16)],
+    )
+    return pl.pallas_call(
+        right_kernel,
+        grid_spec=grid_spec,
+        out_shape=jax.ShapeDtypeStruct(SQUARE, BF16),
+        compiler_params=pltpu.CompilerParams(vmem_limit_bytes=VMEM_LIMIT),
+        cost_estimate=pl.CostEstimate(
+            flops=3 << 29, bytes_accessed=6 << 20, transcendentals=0
+        ),
+        name="lower_right",
+    )(place, mine, other, inverse_mine, inverse_other)
+
+
 def schur_kernel(left_ref, right_ref, front_even_ref, front_odd_ref, out_ref):
-    block = right_ref[...].reshape(256, 1024)
     product = lax.dot_general(
-        left_ref[...], block, ROWS_AXIS, preferred_element_type=F32
+        left_ref[...], right_ref[...], ROWS_AXIS, preferred_element_type=F32
     )
     for which, front_ref in enumerate((front_even_ref, front_odd_ref)):
         lanes = slice(which * 128, (which + 1) * 128)
@@ -124,7 +170,7 @@
         grid=(4,),
         in_specs=[
             pl.BlockSpec((2048, 1024), lambda i: (0, 0)),
-            pl.BlockSpec((2, 1, 128, 1024), lambda i: (i, b, 0, 0)),
+            pl.BlockSpec((256, 1024), lambda i: (i, 0)),
             pl.BlockSpec((2048, 128), lambda i: (0, 4 * i + b)),
             pl.BlockSpec((2048, 128), lambda i: (0, 4 * i + 2 + b)),
         ],
@@ -135,7 +181,7 @@
             flops=4 << 30, bytes_accessed=14 << 20, transcendentals=0
         ),
         name="schur",
-    )(left, right.reshape(8, 2, 128, 1024), front, front)
+    )(left, right, front, front)
 
 
 def place_kernel(
@@ -208,34 +254,56 @@
     target = half * 8 + row
     place = jnp.stack([(x + 4 - col // 2) % 4, core, target, col, col % 4]).astype(jnp.int32)
 
-    turned = shift(
-        jnp.concatenate([panel[0], inverse_block[0]]), lambda h, r, c: (h, (c // 2 + r // 2) % 4 * 2 + c % 2, r)
-    )
+    def spread(array):
+        return shift(array, lambda h, r, c: (h, (c // 2 + r // 2) % 4 * 2 + c % 2, r))
+
+    def ahead_x(array):
+        return shift(array, lambda h, r, c: (h, (r + 2) % 8, c))
+
+    def behind_x(array):
+        return shift(array, lambda h, r, c: (h, (r + 6) % 8, c))
+
+    def ahead_y(array):
+        return shift(array, lambda h, r, c: (h, r, c // 4 * 4 + (c + 1) % 4))
+
+    def behind_y(array):
+        return shift(array, lambda h, r, c: (h, r, c // 4 * 4 + (c + 3) % 4))
+
+    def swap_core(array):
+        return shift(array, lambda h, r, c: (h, r ^ 1, c))
+
+    runs = panel[0].reshape(8, 2, 128, 128)
+    even = spread(jnp.concatenate([runs[:, 0].reshape(1024, 128), inverse_block[0]]))
+    odd = spread(runs[:, 1].reshape(1024, 128))
     twin = shift(panel[0], lambda h, r, c: (h, r, c ^ 4))
     pair = jnp.stack(
         [jnp.where(col < 4, panel[0], twin), jnp.where(col < 4, twin, panel[0])]
     )
-
-    def forward(h, r, c):
-        return h, r, c // 4 * 4 + (c + 1) % 4
-
-    def backward(h, r, c):
-        return h, r, c // 4 * 4 + (c + 3) % 4
-
-    turned, pair = lax.optimization_barrier((turned, pair))
-    one = shift(turned, lambda h, r, c: (h, (r + 2) % 8, c))
-    three = shift(turned, lambda h, r, c: (h, (r + 6) % 8, c))
-    behind = shift(pair, forward)
-    ahead = shift(pair, backward)
-    two = shift(turned, lambda h, r, c: (h, (r + 4) % 8, c))
-    one, three, behind, ahead = lax.optimization_barrier((one, three, behind, ahead))
-    far_first, far_second, two = lax.optimization_barrier(
-        (shift(behind[0], forward), shift(ahead[1], backward), two)
+    even, pair = lax.optimization_barrier((even, pair))
+    one, three, behind, ahead, odd = lax.optimization_barrier(
+        (ahead_x(even), behind_x(even), ahead_y(pair), behind_y(pair), odd)
+    )
+    far_first, far_second, two_first, two_second, odd_one, odd_three = (
+        lax.optimization_barrier(
+            (
+                ahead_y(behind[0]),
+                behind_y(ahead[1]),
+                ahead_x(one[:1024]),
+                behind_x(three[1024:]),
+                ahead_x(odd),
+                behind_x(odd),
+            )
+        )
     )
     rows = (pair, behind, ahead, far_first, far_second)
-    mine = jnp.stack([turned, one, three, two])
-    other = shift(mine, lambda h, r, c: (h, r ^ 1, c))
-    left, right = lower_rows(place, rows, mine, other)
+    mine = jnp.stack([even, one, three, jnp.concatenate([two_first, two_second])])
+    other, odd_two_first, odd_two_second = lax.optimization_barrier(
+        (swap_core(mine), ahead_x(odd_one[:512]), behind_x(odd_three[512:]))
+    )
+    right_even, left = lower_first(place, rows, mine, other)
+    odd_two = jnp.concatenate([odd_two_first, odd_two_second])
+    odd_mine = jnp.stack([odd, odd_one, odd_three, odd_two])
+    odd_other = swap_core(odd_mine)
 
     maps = child_maps.reshape(2, 8, 16, 128)
     row_maps = (
@@ -246,12 +314,18 @@
     col_maps = col_maps - (2 * col + jnp.arange(2, dtype=jnp.int32))[None, :, None, None] * 1024
     col_maps = col_maps.reshape(2, 2, 1024, 1)
 
-    out = None
-    for b in range(2):
-        parcels = schur_parcels(b, left, right, front[0])
-        arrived = lax.all_to_all(parcels.reshape(128, 128, 128), ALL, 0, 0, tiled=True)
-        out = place_children(b, place, arrived, row_maps, col_maps, root_front, out)
-    return out
+    def exchange(parcels):
+        return lax.all_to_all(parcels.reshape(128, 128, 128), ALL, 0, 0, tiled=True)
+
+    def placed(b, arrived, done=None):
+        return place_children(b, place, arrived, row_maps, col_maps, root_front, done)
+
+    parcels = schur_parcels(0, left, right_even, front[0])
+    parcels, odd_mine, odd_other = lax.optimization_barrier((parcels, odd_mine, odd_other))
+    arrived = exchange(parcels)
+    right_odd = lower_right(place, odd_mine, odd_other, mine, other)
+    arrived_odd = exchange(schur_parcels(1, left, right_odd, front[0]))
+    return placed(1, arrived_odd, placed(0, arrived))
 
 
 def solution(mesh):

time: 253 us -> 244 us (0.964)
  waiting for transfers between devices: 120 us -> 108 us
  Pallas kernels: 64 us -> 70.2 us
    all_to_all x2, waiting for transfers between devices: 75.8 us -> 68.7 us  [exchange(): return lax.all_to_all(parcels.reshape(128, 128, 128), ALL, 0, 0, tiled=True)]
    pallas_call x1 -> x2, Pallas kernels: 14.2 us -> 20.1 us  [the longest x1 13.1 us: lower_first(): pl.pallas_call(first_kernel, grid_spec=grid_spec, out_shape=[jax.ShapeDty...]
    ppermute x10 -> x17, waiting for transfers between devices: 44.4 us -> 39.8 us  [shift(): return lax.ppermute(array, ALL, pairs)]
    ppermute x10 -> x17, starting transfers between devices: 46.9 us -> 43.9 us  [shift(): return lax.ppermute(array, ALL, pairs)]
  transfers between devices with their start and end apart: 12 -> 19, of which waited for: 9 -> 10; matrix products, arithmetic and copies ran while one was open for 3% -> 3% of each run, Pallas kernels for 10% -> 23%
where the time goes in v4:
time: 244 us; the launch traced here: 243 us
  waiting for transfers between devices  108 us (44%)
  Pallas kernels  70.2 us (29%)
  starting transfers between devices  56.3 us (23%)
  local copies, waits for them, and re-layouts  6 us (2%)
    all_to_all x2, waiting for transfers between devices, exchange(): return lax.all_to_all(parcels.reshape(128, 128, 128), ALL, 0, 0, tiled=True)  68.7 us
    ppermute x17, starting transfers between devices, shift(): return lax.ppermute(array, ALL, pairs)  43.9 us
    ppermute x17, waiting for transfers between devices, shift(): return lax.ppermute(array, ALL, pairs)  39.8 us
    pallas_call x2, Pallas kernels, place_children(): pl.pallas_call(functools.partial(place_kernel, b), grid_spec=grid_spec, o...  30.7 us
    pallas_call x2, Pallas kernels, schur_parcels(): pl.pallas_call(schur_kernel, grid=(4,), in_specs=[pl.BlockSpec((2048, 102...  19.4 us
    pallas_call x1, Pallas kernels, lower_first(): pl.pallas_call(first_kernel, grid_spec=grid_spec, out_shape=[jax.ShapeDty...  13.1 us
    all_to_all x2, starting transfers between devices, exchange(): return lax.all_to_all(parcels.reshape(128, 128, 128), ALL, 0, 0, tiled=True)  12.3 us
    pallas_call x1, Pallas kernels, lower_right(): pl.pallas_call(right_kernel, grid_spec=grid_spec, out_shape=jax.ShapeDtyp...  7.08 us
  transfers between devices with their start and end apart: 19, of which 10 were waited for; matrix products, arithmetic and copies ran while one was open for 3% of the time, Pallas kernels for 23%

profile of v4, /device:TPU:1, one launch (start us, length us, event | category | flops | bytes accessed | tf_op | source)
XLA Modules:
  0.0 243.5 jit_solution(1116409914053388731)
XLA Ops:
  0.0 2.5 %collective-permute-start.1 = (bf16[2048,128]{1,0:T(8,128)(2,1)}, bf16[2048,128]{1,0:T(8,128)(2,1)S(1)}, u32[]{:S(2)}, u32[]{:S(2)}) collective-permute-start(bf16[2048,128]{1,0:T(8,128)(2,1)} %bitcast.52), channel_id=1, source_target_pairs={{0,4},{1,5},{2,6},{3,7},{4,0},{5,1},{6,2},{7,3},{8,12},{9,13},{10,... | collective-permute-start | bytes 1572872 | tf_op jit(solution)/shard_map/ppermute | solution.py:24
  2.5 1.1 fusion.1
  3.5 1.0 pad_maximum_fusion.3
  4.5 4.0 %collective-permute-start = (bf16[2048,128]{1,0:T(8,128)(2,1)S(1)}, bf16[2048,128]{1,0:T(8,128)(2,1)S(1)}, u32[]{:S(2)}, u32[]{:S(2)}) collective-permute-start(bf16[2048,128]{1,0:T(8,128)(2,1)S(1)} %pad_maximum_fusion.3), channel_id=1, source_target_pairs={{0,0},{1,8},{2,16},{3,24},{4,32},{5,40},{6,48},{7,56},{8,1},{9,9},... | collective-permute-start | bytes 1572872 | tf_op jit(solution)/shard_map/ppermute | solution.py:24
  8.6 5.8 %collective-permute-done.1 = bf16[2048,128]{1,0:T(8,128)(2,1)S(1)} collective-permute-done((bf16[2048,128]{1,0:T(8,128)(2,1)}, bf16[2048,128]{1,0:T(8,128)(2,1)S(1)}, u32[]{:S(2)}, u32[]{:S(2)}) %collective-permute-start.1) | collective-permute-done | bytes 524320 | tf_op jit(solution)/shard_map/ppermute | solution.py:24
  14.4 0.1 select_bitcast_fusion.1
  14.5 0.1 pad_maximum_fusion.1.near_ref
  14.6 0.8 collective-permute-done
  15.4 13.2 %collective-permute-start.5 = (bf16[2,2048,128]{2,1,0:T(8,128)(2,1)S(1)}, bf16[2,2048,128]{2,1,0:T(8,128)(2,1)S(1)}, u32[]{:S(2)}, u32[]{:S(2)}) collective-permute-start(bf16[2,2048,128]{2,1,0:T(8,128)(2,1)S(1)} %pad_maximum_fusion.1.near_ref), channel_id=1, source_target_pairs={{0,3},{1,0},{2,1},{3,2},{4,7},{5,4},{6,5},{7,6},{8,11},{9,8},{10,9... | collective-permute-start | bytes 3145736 | tf_op jit(solution)/shard_map/ppermute | solution.py:24
  28.6 0.0 collective-permute-start.4
  28.6 2.5 %collective-permute-start.3 = (bf16[2048,128]{1,0:T(8,128)(2,1)S(1)}, bf16[2048,128]{1,0:T(8,128)(2,1)S(1)}, u32[]{:S(2)}, u32[]{:S(2)}) collective-permute-start(bf16[2048,128]{1,0:T(8,128)(2,1)S(1)} %collective-permute-done), channel_id=1, source_target_pairs={{0,48},{1,49},{2,50},{3,51},{4,52},{5,53},{6,54},{7,55},{8,56},{9,... | collective-permute-start | bytes 1572872 | tf_op jit(solution)/shard_map/ppermute | solution.py:24
  31.1 3.9 %collective-permute-start.6 = (bf16[1024,128]{1,0:T(8,128)(2,1)S(1)}, bf16[1024,128]{1,0:T(8,128)(2,1)S(1)}, u32[]{:S(2)}, u32[]{:S(2)}) collective-permute-start(bf16[1024,128]{1,0:T(8,128)(2,1)S(1)} %bitcast.61), channel_id=1, source_target_pairs={{0,0},{1,8},{2,16},{3,24},{4,32},{5,40},{6,48},{7,56},{8,1},{9,9},... | collective-permute-start | bytes 786440 | tf_op jit(solution)/shard_map/ppermute | solution.py:24
  35.0 19.4 %collective-permute-done.6 = bf16[1024,128]{1,0:T(8,128)(2,1)S(1)} collective-permute-done((bf16[1024,128]{1,0:T(8,128)(2,1)S(1)}, bf16[1024,128]{1,0:T(8,128)(2,1)S(1)}, u32[]{:S(2)}, u32[]{:S(2)}) %collective-permute-start.6) | collective-permute-done | bytes 262176 | tf_op jit(solution)/shard_map/ppermute | solution.py:24
  54.4 0.0 collective-permute-done.3
  54.4 0.0 collective-permute-done.2
  54.4 0.0 collective-permute-done.5.ahead_ref
  54.5 6.6 %collective-permute-start.10 = (bf16[1024,128]{1,0:T(8,128)(2,1)S(1)}, bf16[1024,128]{1,0:T(8,128)(2,1)S(1)}, u32[]{:S(2)}, u32[]{:S(2)}) collective-permute-start(bf16[1024,128]{1,0:T(8,128)(2,1)S(1)} %slice.29), channel_id=1, source_target_pairs={{0,48},{1,49},{2,50},{3,51},{4,52},{5,53},{6,54},{7,55},{8,56},{9,... | collective-permute-start | bytes 786440 | tf_op jit(solution)/shard_map/ppermute | solution.py:24
  61.2 0.1 collective-permute-start.8
  61.3 1.5 collective-permute-start.7
  62.7 0.1 collective-permute-start.9
  62.8 2.7 %collective-permute-start.12 = (bf16[1024,128]{1,0:T(8,128)(2,1)S(1)}, bf16[1024,128]{1,0:T(8,128)(2,1)S(1)}, u32[]{:S(2)}, u32[]{:S(2)}) collective-permute-start(bf16[1024,128]{1,0:T(8,128)(2,1)S(1)} %collective-permute-done.6), channel_id=1, source_target_pairs={{0,48},{1,49},{2,50},{3,51},{4,52},{5,53},{6,54},{7,55},{8,56},{9,... | collective-permute-start | bytes 786440 | tf_op jit(solution)/shard_map/ppermute | solution.py:24
  65.5 0.0 collective-permute-start.11
  65.5 4.1 %collective-permute-done.9 = bf16[1024,128]{1,0:T(8,128)(2,1)S(1)} collective-permute-done((bf16[1024,128]{1,0:T(8,128)(2,1)S(1)}, bf16[1024,128]{1,0:T(8,128)(2,1)S(1)}, u32[]{:S(2)}, u32[]{:S(2)}) %collective-permute-start.9) | collective-permute-done | bytes 262176 | tf_op jit(solution)/shard_map/ppermute | solution.py:24
  69.6 0.5 collective-permute-done.12
  70.2 4.1 %collective-permute-done.11 = bf16[1024,128]{1,0:T(8,128)(2,1)S(1)} collective-permute-done((bf16[1024,128]{1,0:T(8,128)(2,1)S(1)}, bf16[1024,128]{1,0:T(8,128)(2,1)S(1)}, u32[]{:S(2)}, u32[]{:S(2)}) %collective-permute-start.11) | collective-permute-done | bytes 262176 | tf_op jit(solution)/shard_map/ppermute | solution.py:24
  74.2 0.8 copy-done.7
  75.1 0.3 pad_maximum_fusion.mine_ref.inverse_mine_ref
  75.4 4.2 %collective-permute-start.13 = (bf16[4,2048,128]{2,1,0:T(8,128)(2,1)S(1)}, bf16[4,2048,128]{2,1,0:T(8,128)(2,1)}, u32[]{:S(2)}, u32[]{:S(2)}) collective-permute-start(bf16[4,2048,128]{2,1,0:T(8,128)(2,1)S(1)} %pad_maximum_fusion.mine_ref.inverse_mine_ref), channel_id=1, source_target_pairs={{0,8},{1,9},{2,10},{3,11},{4,12},{5,13},{6,14},{7,15},{8,0},{9,1},... | collective-permute-start | bytes 6291464 | tf_op jit(solution)/shard_map/ppermute | solution.py:24
  79.6 0.5 collective-permute-start.15
  80.2 1.0 collective-permute-start.14
  81.2 3.6 %collective-permute-done.15 = bf16[512,128]{1,0:T(8,128)(2,1)S(1)} collective-permute-done((bf16[512,128]{1,0:T(8,128)(2,1)S(1)}, bf16[512,128]{1,0:T(8,128)(2,1)S(1)}, u32[]{:S(2)}, u32[]{:S(2)}) %collective-permute-start.15) | collective-permute-done | bytes 131104 | tf_op jit(solution)/shard_map/ppermute | solution.py:24
  84.8 1.4 collective-permute-done.14
  86.2 0.1 pad_maximum_fusion.2.mine_ref
  86.3 1.2 collective-permute-start.16
  87.5 0.7 stack.62.place_ref
  88.2 13.1 %lower_first.1 = (bf16[1024,1024]{1,0:T(8,128)(2,1)}, bf16[2048,1024]{1,0:T(8,128)(2,1)}) custom-call(s32[5]{0:T(128)} %stack.62.place_ref, bf16[2,2048,128]{2,1,0:T(8,128)(2,1)} %copy-done.3, bf16[2,2048,128]{2,1,0:T(8,128)(2,1)} %copy-done.5, bf16[2,2048,128]{2,1,0:T(8,128)(2,1)} %copy-done.4, bf16[2048,128]{1,0:T(8,128)(2,1)} %collective-permute-done.7.far_first_ref, ...), custom_call_target="tpu_custom_call" | custom-call | flops 4294967296 | bytes 14680064 | tf_op jit(solution)/shard_map/lower_first/pallas_call | solution.py:104
  101.3 9.7 %schur.2 = bf16[16,8,128,128]{3,2,1,0:T(8,128)(2,1)} custom-call(bf16[2048,1024]{1,0:T(8,128)(2,1)} %get-tuple-element.40.left_ref, bf16[1024,1024]{1,0:T(8,128)(2,1)} %get-tuple-element.41.right_ref, bf16[2048,2048]{1,0:T(8,128)(2,1)} %bitcast.46, bf16[2048,2048]{1,0:T(8,128)(2,1)} %bitcast.47), custom_call_target="tpu_custom_call" | custom-call | flops 4294967296 | bytes 14680064 | tf_op jit(solution)/shard_map/schur/pallas_call | solution.py:168
  111.0 5.9 %all-to-all-start.1 = ((bf16[128,128,128]{2,1,0:T(8,128)(2,1)}), bf16[128,128,128]{2,1,0:T(8,128)(2,1)}, u32[]{:S(2)}, u32[]{:S(2)}) async-start(bf16[128,128,128]{2,1,0:T(8,128)(2,1)} %bitcast.51), calls=%async_computation.1 | async-start | bytes 8388608 | tf_op jit(solution)/shard_map/all_to_all | solution.py:318
  116.9 7.1 %lower_right.1.right_ref = bf16[1024,1024]{1,0:T(8,128)(2,1)} custom-call(s32[5]{0:T(128)} %stack.62.place_ref, bf16[4,1024,128]{2,1,0:T(8,128)(2,1)} %copy-done.1, bf16[4,1024,128]{2,1,0:T(8,128)(2,1)} %collective-permute-done.16.other_ref, bf16[4,2048,128]{2,1,0:T(8,128)(2,1)} %copy-done, ...), custom_call_target="tpu_custom_call" | custom-call | flops 1610612736 | bytes 6291456 | tf_op jit(solution)/shard_map/lower_right/pallas_call | solution.py:142
  124.0 9.7 %schur.3 = bf16[16,8,128,128]{3,2,1,0:T(8,128)(2,1)} custom-call(bf16[2048,1024]{1,0:T(8,128)(2,1)} %get-tuple-element.40.left_ref, bf16[1024,1024]{1,0:T(8,128)(2,1)} %lower_right.1.right_ref, bf16[2048,2048]{1,0:T(8,128)(2,1)} %bitcast.48, bf16[2048,2048]{1,0:T(8,128)(2,1)} %bitcast.49), custom_call_target="tpu_custom_call" | custom-call | flops 4294967296 | bytes 14680064 | tf_op jit(solution)/shard_map/schur/pallas_call | solution.py:168
  133.7 35.6 %all-to-all-done.1.schur_in_ref = bf16[128,128,128]{2,1,0:T(8,128)(2,1)} async-done(((bf16[128,128,128]{2,1,0:T(8,128)(2,1)}), bf16[128,128,128]{2,1,0:T(8,128)(2,1)}, u32[]{:S(2)}, u32[]{:S(2)}) %all-to-all-start.1) | async-done | bytes 4194336 | tf_op jit(solution)/shard_map/all_to_all | solution.py:318
  169.3 6.5 %all-to-all-start = ((bf16[128,128,128]{2,1,0:T(8,128)(2,1)}), bf16[128,128,128]{2,1,0:T(8,128)(2,1)}, u32[]{:S(2)}, u32[]{:S(2)}) async-start(bf16[128,128,128]{2,1,0:T(8,128)(2,1)} %bitcast.50), calls=%async_computation | async-start | bytes 8388608 | tf_op jit(solution)/shard_map/all_to_all | solution.py:318
  175.8 0.1 fusion
  175.9 3.3 %reshape.38.col_map_ref = s32[2,2,1024,1]{3,2,1,0:T(8,128)} reshape(s32[2,2,8,128]{3,2,1,0:T(8,128)S(1)} %fusion) | data formatting | bytes 32768 | tf_op jit(solution)/shard_map/reshape | solution.py:315
  179.2 0.6 broadcast_subtract_fusion
  179.8 15.3 %place.2.refs_0_ = f32[1024,2048]{1,0:T(8,128)} custom-call(s32[5]{0:T(128)} %stack.62.place_ref, bf16[128,128,128]{2,1,0:T(8,128)(2,1)} %all-to-all-done.1.schur_in_ref, s32[2,1,1024]{2,1,0:T(1,128)} %bitcast.67, s32[2,2,1024,1]{3,2,1,0:T(8,128)} %reshape.38.col_map_ref, bf16[1024,2048]{1,0:T(8,128)(2,1)} %base_ref.3), custom_call_target="tpu_custom_call" | custom-call | flops 8589934592 | bytes 10485760 | tf_op jit(solution)/shard_map/place/pallas_call | solution.py:229
  195.1 33.0 %all-to-all-done.schur_in_ref = bf16[128,128,128]{2,1,0:T(8,128)(2,1)} async-done(((bf16[128,128,128]{2,1,0:T(8,128)(2,1)}), bf16[128,128,128]{2,1,0:T(8,128)(2,1)}, u32[]{:S(2)}, u32[]{:S(2)}) %all-to-all-start) | async-done | bytes 4194336 | tf_op jit(solution)/shard_map/all_to_all | solution.py:318
  228.2 15.3 %place.3 = f32[1024,2048]{1,0:T(8,128)} custom-call(s32[5]{0:T(128)} %stack.62.place_ref, bf16[128,128,128]{2,1,0:T(8,128)(2,1)} %all-to-all-done.schur_in_ref, s32[2,1,1024]{2,1,0:T(1,128)} %bitcast.68, s32[2,2,1024,1]{3,2,1,0:T(8,128)} %reshape.38.col_map_ref, bf16[1024,2048]{1,0:T(8,128)(2,1)} %base_ref.3, ...), custom_call_target="tpu_custom_call", output_to_operand_aliasing={{}: (5, {})} | custom-call | flops 8589934592 | bytes 10485760 | tf_op jit(solution)/shard_map/place/pallas_call | solution.py:229
  (34 shorter events, 0.3 us)
Async XLA Ops:
  0.0 14.4 %copy-start.2 = (bf16[1,2048,128]{2,1,0:T(8,128)(2,1)S(1)}, bf16[1,2048,128]{2,1,0:T(8,128)(2,1)}, u32[]{:S(2)}) copy-start(bf16[1,2048,128]{2,1,0:T(8,128)(2,1)} %param.6) | copy-start | bytes 1572868
  0.0 14.4 %collective-permute-start.1 = (bf16[2048,128]{1,0:T(8,128)(2,1)}, bf16[2048,128]{1,0:T(8,128)(2,1)S(1)}, u32[]{:S(2)}, u32[]{:S(2)}) collective-permute-start(bf16[2048,128]{1,0:T(8,128)(2,1)} %bitcast.52), channel_id=1, source_target_pairs={{0,4},{1,5},{2,6},{3,7},{4,0},{5,1},{6,2},{7,3},{8,12},{9,13},{10,... | collective-permute-start | bytes 1572872 | tf_op jit(solution)/shard_map/ppermute | solution.py:24
  4.5 10.9 %collective-permute-start = (bf16[2048,128]{1,0:T(8,128)(2,1)S(1)}, bf16[2048,128]{1,0:T(8,128)(2,1)S(1)}, u32[]{:S(2)}, u32[]{:S(2)}) collective-permute-start(bf16[2048,128]{1,0:T(8,128)(2,1)S(1)} %pad_maximum_fusion.3), channel_id=1, source_target_pairs={{0,0},{1,8},{2,16},{3,24},{4,32},{5,40},{6,48},{7,56},{8,1},{9,9},... | collective-permute-start | bytes 1572872 | tf_op jit(solution)/shard_map/ppermute | solution.py:24
  14.6 60.5 %copy-start.3 = (bf16[2,2048,128]{2,1,0:T(8,128)(2,1)}, bf16[2,2048,128]{2,1,0:T(8,128)(2,1)S(1)}, u32[]{:S(2)}) copy-start(bf16[2,2048,128]{2,1,0:T(8,128)(2,1)S(1)} %pad_maximum_fusion.1.near_ref) | copy-start | bytes 3145732
  15.4 39.0 %collective-permute-start.5 = (bf16[2,2048,128]{2,1,0:T(8,128)(2,1)S(1)}, bf16[2,2048,128]{2,1,0:T(8,128)(2,1)S(1)}, u32[]{:S(2)}, u32[]{:S(2)}) collective-permute-start(bf16[2,2048,128]{2,1,0:T(8,128)(2,1)S(1)} %pad_maximum_fusion.1.near_ref), channel_id=1, source_target_pairs={{0,3},{1,0},{2,1},{3,2},{4,7},{5,4},{6,5},{7,6},{8,11},{9,8},{10,9... | collective-permute-start | bytes 3145736 | tf_op jit(solution)/shard_map/ppermute | solution.py:24
  28.6 25.8 %collective-permute-start.4 = (bf16[2,2048,128]{2,1,0:T(8,128)(2,1)S(1)}, bf16[2,2048,128]{2,1,0:T(8,128)(2,1)S(1)}, u32[]{:S(2)}, u32[]{:S(2)}) collective-permute-start(bf16[2,2048,128]{2,1,0:T(8,128)(2,1)S(1)} %pad_maximum_fusion.1.near_ref), channel_id=1, source_target_pairs={{0,1},{1,2},{2,3},{3,0},{4,5},{5,6},{6,7},{7,4},{8,9},{9,10},{10,1... | collective-permute-start | bytes 3145736 | tf_op jit(solution)/shard_map/ppermute | solution.py:24
  28.6 25.8 %collective-permute-start.3 = (bf16[2048,128]{1,0:T(8,128)(2,1)S(1)}, bf16[2048,128]{1,0:T(8,128)(2,1)S(1)}, u32[]{:S(2)}, u32[]{:S(2)}) collective-permute-start(bf16[2048,128]{1,0:T(8,128)(2,1)S(1)} %collective-permute-done), channel_id=1, source_target_pairs={{0,48},{1,49},{2,50},{3,51},{4,52},{5,53},{6,54},{7,55},{8,56},{9,... | collective-permute-start | bytes 1572872 | tf_op jit(solution)/shard_map/ppermute | solution.py:24
  31.1 23.3 %collective-permute-start.2 = (bf16[2048,128]{1,0:T(8,128)(2,1)S(1)}, bf16[2048,128]{1,0:T(8,128)(2,1)S(1)}, u32[]{:S(2)}, u32[]{:S(2)}) collective-permute-start(bf16[2048,128]{1,0:T(8,128)(2,1)S(1)} %collective-permute-done), channel_id=1, source_target_pairs={{0,16},{1,17},{2,18},{3,19},{4,20},{5,21},{6,22},{7,23},{8,24},{9,... | collective-permute-start | bytes 1572872 | tf_op jit(solution)/shard_map/ppermute | solution.py:24
  31.1 23.3 %collective-permute-start.6 = (bf16[1024,128]{1,0:T(8,128)(2,1)S(1)}, bf16[1024,128]{1,0:T(8,128)(2,1)S(1)}, u32[]{:S(2)}, u32[]{:S(2)}) collective-permute-start(bf16[1024,128]{1,0:T(8,128)(2,1)S(1)} %bitcast.61), channel_id=1, source_target_pairs={{0,0},{1,8},{2,16},{3,24},{4,32},{5,40},{6,48},{7,56},{8,1},{9,9},... | collective-permute-start | bytes 786440 | tf_op jit(solution)/shard_map/ppermute | solution.py:24
  54.4 19.8 %copy-start.4 = (bf16[2,2048,128]{2,1,0:T(8,128)(2,1)}, bf16[2,2048,128]{2,1,0:T(8,128)(2,1)S(1)}, u32[]{:S(2)}) copy-start(bf16[2,2048,128]{2,1,0:T(8,128)(2,1)S(1)} %collective-permute-done.5.ahead_ref) | copy-start | bytes 3145732
  54.4 20.7 %copy-start.5 = (bf16[2,2048,128]{2,1,0:T(8,128)(2,1)}, bf16[2,2048,128]{2,1,0:T(8,128)(2,1)S(1)}, u32[]{:S(2)}) copy-start(bf16[2,2048,128]{2,1,0:T(8,128)(2,1)S(1)} %collective-permute-done.4.behind_ref) | copy-start | bytes 3145732
  54.5 11.0 %collective-permute-start.10 = (bf16[1024,128]{1,0:T(8,128)(2,1)S(1)}, bf16[1024,128]{1,0:T(8,128)(2,1)S(1)}, u32[]{:S(2)}, u32[]{:S(2)}) collective-permute-start(bf16[1024,128]{1,0:T(8,128)(2,1)S(1)} %slice.29), channel_id=1, source_target_pairs={{0,48},{1,49},{2,50},{3,51},{4,52},{5,53},{6,54},{7,55},{8,56},{9,... | collective-permute-start | bytes 786440 | tf_op jit(solution)/shard_map/ppermute | solution.py:24
  61.2 13.0 %collective-permute-start.8 = (bf16[2048,128]{1,0:T(8,128)(2,1)S(1)}, bf16[2048,128]{1,0:T(8,128)(2,1)S(1)}, u32[]{:S(2)}, u32[]{:S(2)}) collective-permute-start(bf16[2048,128]{1,0:T(8,128)(2,1)S(1)} %slice_bitcast_fusion), channel_id=1, source_target_pairs={{0,3},{1,0},{2,1},{3,2},{4,7},{5,4},{6,5},{7,6},{8,11},{9,8},{10,9... | collective-permute-start | bytes 1572872 | tf_op jit(solution)/shard_map/ppermute | solution.py:24
  61.3 13.8 %collective-permute-start.7 = (bf16[2048,128]{1,0:T(8,128)(2,1)S(1)}, bf16[2048,128]{1,0:T(8,128)(2,1)}, u32[]{:S(2)}, u32[]{:S(2)}) collective-permute-start(bf16[2048,128]{1,0:T(8,128)(2,1)S(1)} %slice_bitcast_fusion.1), channel_id=1, source_target_pairs={{0,1},{1,2},{2,3},{3,0},{4,5},{5,6},{6,7},{7,4},{8,9},{9,10},{10,1... | collective-permute-start | bytes 1572872 | tf_op jit(solution)/shard_map/ppermute | solution.py:24
  62.7 6.9 %collective-permute-start.9 = (bf16[1024,128]{1,0:T(8,128)(2,1)S(1)}, bf16[1024,128]{1,0:T(8,128)(2,1)S(1)}, u32[]{:S(2)}, u32[]{:S(2)}) collective-permute-start(bf16[1024,128]{1,0:T(8,128)(2,1)S(1)} %slice.28), channel_id=1, source_target_pairs={{0,16},{1,17},{2,18},{3,19},{4,20},{5,21},{6,22},{7,23},{8,24},{9,... | collective-permute-start | bytes 786440 | tf_op jit(solution)/shard_map/ppermute | solution.py:24
  62.8 7.3 %collective-permute-start.12 = (bf16[1024,128]{1,0:T(8,128)(2,1)S(1)}, bf16[1024,128]{1,0:T(8,128)(2,1)S(1)}, u32[]{:S(2)}, u32[]{:S(2)}) collective-permute-start(bf16[1024,128]{1,0:T(8,128)(2,1)S(1)} %collective-permute-done.6), channel_id=1, source_target_pairs={{0,48},{1,49},{2,50},{3,51},{4,52},{5,53},{6,54},{7,55},{8,56},{9,... | collective-permute-start | bytes 786440 | tf_op jit(solution)/shard_map/ppermute | solution.py:24
  65.5 8.7 %collective-permute-start.11 = (bf16[1024,128]{1,0:T(8,128)(2,1)S(1)}, bf16[1024,128]{1,0:T(8,128)(2,1)S(1)}, u32[]{:S(2)}, u32[]{:S(2)}) collective-permute-start(bf16[1024,128]{1,0:T(8,128)(2,1)S(1)} %collective-permute-done.6), channel_id=1, source_target_pairs={{0,16},{1,17},{2,18},{3,19},{4,20},{5,21},{6,22},{7,23},{8,24},{9,... | collective-permute-start | bytes 786440 | tf_op jit(solution)/shard_map/ppermute | solution.py:24
  74.2 0.8 copy-start.7
  75.4 12.9 %copy-start = (bf16[4,2048,128]{2,1,0:T(8,128)(2,1)}, bf16[4,2048,128]{2,1,0:T(8,128)(2,1)S(1)}, u32[]{:S(2)}) copy-start(bf16[4,2048,128]{2,1,0:T(8,128)(2,1)S(1)} %pad_maximum_fusion.mine_ref.inverse_mine_ref) | copy-start | bytes 6291460
  75.4 10.8 %collective-permute-start.13 = (bf16[4,2048,128]{2,1,0:T(8,128)(2,1)S(1)}, bf16[4,2048,128]{2,1,0:T(8,128)(2,1)}, u32[]{:S(2)}, u32[]{:S(2)}) collective-permute-start(bf16[4,2048,128]{2,1,0:T(8,128)(2,1)S(1)} %pad_maximum_fusion.mine_ref.inverse_mine_ref), channel_id=1, source_target_pairs={{0,8},{1,9},{2,10},{3,11},{4,12},{5,13},{6,14},{7,15},{8,0},{9,1},... | collective-permute-start | bytes 6291464 | tf_op jit(solution)/shard_map/ppermute | solution.py:24
  79.6 5.2 %collective-permute-start.15 = (bf16[512,128]{1,0:T(8,128)(2,1)S(1)}, bf16[512,128]{1,0:T(8,128)(2,1)S(1)}, u32[]{:S(2)}, u32[]{:S(2)}) collective-permute-start(bf16[512,128]{1,0:T(8,128)(2,1)S(1)} %slice.31), channel_id=1, source_target_pairs={{0,48},{1,49},{2,50},{3,51},{4,52},{5,53},{6,54},{7,55},{8,56},{9,... | collective-permute-start | bytes 393224 | tf_op jit(solution)/shard_map/ppermute | solution.py:24
  80.2 6.0 %collective-permute-start.14 = (bf16[512,128]{1,0:T(8,128)(2,1)S(1)}, bf16[512,128]{1,0:T(8,128)(2,1)S(1)}, u32[]{:S(2)}, u32[]{:S(2)}) collective-permute-start(bf16[512,128]{1,0:T(8,128)(2,1)S(1)} %slice.30), channel_id=1, source_target_pairs={{0,16},{1,17},{2,18},{3,19},{4,20},{5,21},{6,22},{7,23},{8,24},{9,... | collective-permute-start | bytes 393224 | tf_op jit(solution)/shard_map/ppermute | solution.py:24
  86.3 15.0 %copy-start.1 = (bf16[4,1024,128]{2,1,0:T(8,128)(2,1)}, bf16[4,1024,128]{2,1,0:T(8,128)(2,1)S(1)}, u32[]{:S(2)}) copy-start(bf16[4,1024,128]{2,1,0:T(8,128)(2,1)S(1)} %pad_maximum_fusion.2.mine_ref) | copy-start | bytes 3145732
  86.3 24.7 %collective-permute-start.16 = (bf16[4,1024,128]{2,1,0:T(8,128)(2,1)S(1)}, bf16[4,1024,128]{2,1,0:T(8,128)(2,1)}, u32[]{:S(2)}, u32[]{:S(2)}) collective-permute-start(bf16[4,1024,128]{2,1,0:T(8,128)(2,1)S(1)} %pad_maximum_fusion.2.mine_ref), channel_id=1, source_target_pairs={{0,8},{1,9},{2,10},{3,11},{4,12},{5,13},{6,14},{7,15},{8,0},{9,1},... | collective-permute-start | bytes 3145736 | tf_op jit(solution)/shard_map/ppermute | solution.py:24
  111.0 58.3 %all-to-all-start.1 = ((bf16[128,128,128]{2,1,0:T(8,128)(2,1)}), bf16[128,128,128]{2,1,0:T(8,128)(2,1)}, u32[]{:S(2)}, u32[]{:S(2)}) async-start(bf16[128,128,128]{2,1,0:T(8,128)(2,1)} %bitcast.51), calls=%async_computation.1 | async-start | bytes 8388608 | tf_op jit(solution)/shard_map/all_to_all | solution.py:318
  169.3 6.5 %copy-start.6 = (s32[2,16384]{1,0:T(2,128)S(1)}, s32[2,16384]{1,0:T(2,128)}, u32[]{:S(2)}) copy-start(s32[2,16384]{1,0:T(2,128)} %param.8) | copy-start | bytes 393220
  169.3 58.9 %all-to-all-start = ((bf16[128,128,128]{2,1,0:T(8,128)(2,1)}), bf16[128,128,128]{2,1,0:T(8,128)(2,1)}, u32[]{:S(2)}, u32[]{:S(2)}) async-start(bf16[128,128,128]{2,1,0:T(8,128)(2,1)} %bitcast.50), calls=%async_computation | async-start | bytes 8388608 | tf_op jit(solution)/shard_map/all_to_all | solution.py:318

commit v5 on v4

--- a/solution.py
+++ b/solution.py
@@ -53,6 +53,8 @@
     ahead_ref,
     far_first_ref,
     far_second_ref,
+    below_mine_ref,
+    below_other_ref,
     mine_ref,
     other_ref,
     inverse_mine_ref,
@@ -62,23 +64,31 @@
     inverse_ref,
     wide_ref,
 ):
-    y = place_ref[4]
-
-    @pl.when(pl.program_id(0) == 0)
+    step = pl.program_id(0)
+    y, z = place_ref[4], place_ref[3] // 4
+
+    @pl.when(step == 0)
     def _():
         gather_columns(place_ref, inverse_mine_ref, inverse_other_ref, inverse_ref)
         gather_columns(place_ref, mine_ref, other_ref, wide_ref)
         inverse_product(wide_ref, inverse_ref, right_ref)
 
-    @pl.when(pl.program_id(0) > 0)
+    @pl.when(step == 1)
     def _():
         for ref, away in ((near_ref, 0), (behind_ref, 3), (ahead_ref, 1)):
-            for zl in range(2):
-                wide_ref[:, spans(zl * 4 + (y + away) % 4)] = ref[zl]
+            for side in range(2):
+                wide_ref[:, spans(side * 4 + (y + away) % 4)] = ref[side]
         wide_ref[:, spans((y + 2) % 4)] = far_first_ref[...]
         wide_ref[:, spans(4 + (y + 2) % 4)] = far_second_ref[...]
         inverse_product(wide_ref, inverse_ref, left_ref)
 
+    @pl.when(step == 2)
+    def _():
+        for ref, side in ((below_mine_ref, z), (below_other_ref, 1 - z)):
+            for index, away in enumerate((0, 3, 1, 2)):
+                wide_ref[:, spans(side * 4 + (y + away) % 4)] = ref[index]
+        inverse_product(wide_ref, inverse_ref, left_ref)
+
 
 FOUR_PANELS = pl.BlockSpec((4, 1024, 128), lambda i, s: (0, 0, 0))
 FOUR_INVERSES = pl.BlockSpec((4, 1024, 128), lambda i, s: (0, 1, 0))
@@ -89,12 +99,12 @@
     def part(i):
         return jnp.maximum(i - 1, 0)
 
-    pair = pl.BlockSpec((2, 1024, 128), lambda i, s: (0, part(i), 0))
-    single = pl.BlockSpec((1024, 128), lambda i, s: (part(i), 0))
+    pair = pl.BlockSpec((2, 1024, 128), lambda i, s: (0, 0, 0))
+    single = pl.BlockSpec((1024, 128), lambda i, s: (0, 0))
     grid_spec = pltpu.PrefetchScalarGridSpec(
         num_scalar_prefetch=1,
         grid=(3,),
-        in_specs=[pair] * 3 + [single] * 2 + [FOUR_PANELS] * 2 + [FOUR_INVERSES] * 2,
+        in_specs=[pair] * 3 + [single] * 2 + [FOUR_PANELS] * 4 + [FOUR_INVERSES] * 2,
         out_specs=[
             pl.BlockSpec(SQUARE, lambda i, s: (0, 0)),
             pl.BlockSpec(SQUARE, lambda i, s: (part(i), 0)),
@@ -269,40 +279,52 @@
     def behind_y(array):
         return shift(array, lambda h, r, c: (h, r, c // 4 * 4 + (c + 3) % 4))
 
+    def swap_z(array):
+        return shift(array, lambda h, r, c: (h, r, c ^ 4))
+
     def swap_core(array):
         return shift(array, lambda h, r, c: (h, r ^ 1, c))
 
     runs = panel[0].reshape(8, 2, 128, 128)
     even = spread(jnp.concatenate([runs[:, 0].reshape(1024, 128), inverse_block[0]]))
     odd = spread(runs[:, 1].reshape(1024, 128))
-    twin = shift(panel[0], lambda h, r, c: (h, r, c ^ 4))
-    pair = jnp.stack(
-        [jnp.where(col < 4, panel[0], twin), jnp.where(col < 4, twin, panel[0])]
-    )
-    even, pair = lax.optimization_barrier((even, pair))
-    one, three, behind, ahead, odd = lax.optimization_barrier(
-        (ahead_x(even), behind_x(even), ahead_y(pair), behind_y(pair), odd)
-    )
-    far_first, far_second, two_first, two_second, odd_one, odd_three = (
-        lax.optimization_barrier(
-            (
-                ahead_y(behind[0]),
-                behind_y(ahead[1]),
-                ahead_x(one[:1024]),
-                behind_x(three[1024:]),
-                ahead_x(odd),
-                behind_x(odd),
-            )
+    upper, below = panel[0, :1024], panel[0, 1024:]
+    even, twin, below_one, below_three, below_two = lax.optimization_barrier(
+        (
+            even,
+            swap_z(upper),
+            ahead_y(below),
+            behind_y(below),
+            shift(below, lambda h, r, c: (h, r, c ^ 2)),
         )
     )
-    rows = (pair, behind, ahead, far_first, far_second)
+    pair = jnp.stack([jnp.where(col < 4, upper, twin), jnp.where(col < 4, twin, upper)])
+    below_mine = jnp.stack([below, below_one, below_three, below_two])
+    one, three, behind, ahead = lax.optimization_barrier(
+        (ahead_x(even), behind_x(even), ahead_y(pair), behind_y(pair))
+    )
+    below_other = swap_z(below_mine)
+    far_first, far_second, two_first, two_second, odd, below_other = lax.optimization_barrier(
+        (
+            ahead_y(behind[0]),
+            behind_y(ahead[1]),
+            ahead_x(one[:1024]),
+            behind_x(three[1024:]),
+            odd,
+            below_other,
+        )
+    )
     mine = jnp.stack([even, one, three, jnp.concatenate([two_first, two_second])])
-    other, odd_two_first, odd_two_second = lax.optimization_barrier(
-        (swap_core(mine), ahead_x(odd_one[:512]), behind_x(odd_three[512:]))
+    other = swap_core(mine)
+    rows = (pair, behind, ahead, far_first, far_second, below_mine, below_other)
+    odd_parts = (
+        ahead_x(odd),
+        behind_x(odd),
+        shift(odd, lambda h, r, c: (h, r ^ 4, c)),
     )
     right_even, left = lower_first(place, rows, mine, other)
-    odd_two = jnp.concatenate([odd_two_first, odd_two_second])
-    odd_mine = jnp.stack([odd, odd_one, odd_three, odd_two])
+    odd_parts, right_even, left = lax.optimization_barrier((odd_parts, right_even, left))
+    odd_mine = jnp.stack([odd, *odd_parts])
     odd_other = swap_core(odd_mine)
 
     maps = child_maps.reshape(2, 8, 16, 128)

time: 244 us -> 242 us (level)
  waiting for transfers between devices: 108 us -> 96.3 us
  starting transfers between devices: 56.3 us -> 64.4 us
    ppermute x17 -> x20, waiting for transfers between devices: 39.8 us -> 27.7 us  [shift(): return lax.ppermute(array, ALL, pairs)]
    ppermute x17 -> x20, starting transfers between devices: 43.9 us -> 50.1 us  [shift(): return lax.ppermute(array, ALL, pairs)]
  transfers between devices with their start and end apart: 19 -> 22, of which waited for: 10 -> 10; matrix products, arithmetic and copies ran while one was open for 3% -> 2% of each run, Pallas kernels for 23% -> 23%
where the time goes in v5:
time: 242 us
  waiting for transfers between devices  96.3 us (40%)
  Pallas kernels  70.8 us (29%)
  starting transfers between devices  64.4 us (27%)
  local copies, waits for them, and re-layouts  6.64 us (3%)
  other arithmetic  3.27 us (1%)
    all_to_all x2, waiting for transfers between devices, exchange(): return lax.all_to_all(parcels.reshape(128, 128, 128), ALL, 0, 0, tiled=True)  68.6 us
    ppermute x20, starting transfers between devices, shift(): return lax.ppermute(array, ALL, pairs)  50.1 us
    pallas_call x2, Pallas kernels, place_children(): pl.pallas_call(functools.partial(place_kernel, b), grid_spec=grid_spec, o...  30.7 us
    ppermute x20, waiting for transfers between devices, shift(): return lax.ppermute(array, ALL, pairs)  27.7 us
    pallas_call x2, Pallas kernels, schur_parcels(): pl.pallas_call(schur_kernel, grid=(4,), in_specs=[pl.BlockSpec((2048, 102...  19.4 us
    all_to_all x2, starting transfers between devices, exchange(): return lax.all_to_all(parcels.reshape(128, 128, 128), ALL, 0, 0, tiled=True)  14.3 us
    pallas_call x1, Pallas kernels, lower_first(): pl.pallas_call(first_kernel, grid_spec=grid_spec, out_shape=[jax.ShapeDty...  13.7 us
    pallas_call x1, Pallas kernels, lower_right(): pl.pallas_call(right_kernel, grid_spec=grid_spec, out_shape=jax.ShapeDtyp...  7.08 us
  transfers between devices with their start and end apart: 22, of which 10 were waited for; matrix products, arithmetic and copies ran while one was open for 2% of the time, Pallas kernels for 23%

profile of v5, /device:TPU:1, one launch (start us, length us, event | category | flops | bytes accessed | tf_op | source)
XLA Modules:
  0.0 241.8 jit_solution(11359358211903052948)
XLA Ops:
  0.0 1.1 fusion.2
  1.1 1.0 pad_maximum_fusion.3
  2.1 4.6 %collective-permute-start = (bf16[2048,128]{1,0:T(8,128)(2,1)S(1)}, bf16[2048,128]{1,0:T(8,128)(2,1)S(1)}, u32[]{:S(2)}, u32[]{:S(2)}) collective-permute-start(bf16[2048,128]{1,0:T(8,128)(2,1)S(1)} %pad_maximum_fusion.3), channel_id=1, source_target_pairs={{0,0},{1,8},{2,16},{3,24},{4,32},{5,40},{6,48},{7,56},{8,1},{9,9},... | collective-permute-start | bytes 1572872 | tf_op jit(solution)/shard_map/ppermute | solution.py:24
  6.7 0.1 fusion.1
  6.8 3.7 %collective-permute-start.1 = (bf16[1024,128]{1,0:T(8,128)(2,1)S(1)}, bf16[1024,128]{1,0:T(8,128)(2,1)S(1)}, u32[]{:S(2)}, u32[]{:S(2)}) collective-permute-start(bf16[1024,128]{1,0:T(8,128)(2,1)S(1)} %get-tuple-element.59), channel_id=1, source_target_pairs={{0,4},{1,5},{2,6},{3,7},{4,0},{5,1},{6,2},{7,3},{8,12},{9,13},{10,... | collective-permute-start | bytes 786440 | tf_op jit(solution)/shard_map/ppermute | solution.py:24
  10.6 1.5 collective-permute-start.4
  12.1 0.6 collective-permute-start.3
  12.7 0.9 collective-permute-start.2
  13.5 3.4 %collective-permute-done.1 = bf16[1024,128]{1,0:T(8,128)(2,1)S(1)} collective-permute-done((bf16[1024,128]{1,0:T(8,128)(2,1)S(1)}, bf16[1024,128]{1,0:T(8,128)(2,1)S(1)}, u32[]{:S(2)}, u32[]{:S(2)}) %collective-permute-start.1) | collective-permute-done | bytes 262176 | tf_op jit(solution)/shard_map/ppermute | solution.py:24
  17.0 8.6 %collective-permute-done.4 = bf16[1024,128]{1,0:T(8,128)(2,1)S(1)} collective-permute-done((bf16[1024,128]{1,0:T(8,128)(2,1)S(1)}, bf16[1024,128]{1,0:T(8,128)(2,1)S(1)}, u32[]{:S(2)}, u32[]{:S(2)}) %collective-permute-start.4) | collective-permute-done | bytes 262176 | tf_op jit(solution)/shard_map/ppermute | solution.py:24
  25.6 0.6 collective-permute-done.2
  26.3 5.5 %collective-permute-start.8 = (bf16[2,1024,128]{2,1,0:T(8,128)(2,1)S(1)}, bf16[2,1024,128]{2,1,0:T(8,128)(2,1)S(1)}, u32[]{:S(2)}, u32[]{:S(2)}) collective-permute-start(bf16[2,1024,128]{2,1,0:T(8,128)(2,1)S(1)} %pad_maximum_fusion.4.near_ref), channel_id=1, source_target_pairs={{0,3},{1,0},{2,1},{3,2},{4,7},{5,4},{6,5},{7,6},{8,11},{9,8},{10,9... | collective-permute-start | bytes 1572872 | tf_op jit(solution)/shard_map/ppermute | solution.py:24
  31.8 6.7 %collective-permute-start.6 = (bf16[2048,128]{1,0:T(8,128)(2,1)S(1)}, bf16[2048,128]{1,0:T(8,128)(2,1)S(1)}, u32[]{:S(2)}, u32[]{:S(2)}) collective-permute-start(bf16[2048,128]{1,0:T(8,128)(2,1)S(1)} %collective-permute-done), channel_id=1, source_target_pairs={{0,48},{1,49},{2,50},{3,51},{4,52},{5,53},{6,54},{7,55},{8,56},{9,... | collective-permute-start | bytes 1572872 | tf_op jit(solution)/shard_map/ppermute | solution.py:24
  38.5 1.1 pad_maximum_fusion.1.below_mine_ref
  39.6 1.7 collective-permute-start.14
  41.3 1.3 collective-permute-done.8.ahead_ref
  42.6 3.1 %collective-permute-start.13 = (bf16[1024,128]{1,0:T(8,128)(2,1)S(1)}, bf16[1024,128]{1,0:T(8,128)(2,1)S(1)}, u32[]{:S(2)}, u32[]{:S(2)}) collective-permute-start(bf16[1024,128]{1,0:T(8,128)(2,1)S(1)} %bitcast.65), channel_id=1, source_target_pairs={{0,0},{1,8},{2,16},{3,24},{4,32},{5,40},{6,48},{7,56},{8,1},{9,9},... | collective-permute-start | bytes 786440 | tf_op jit(solution)/shard_map/ppermute | solution.py:24
  45.7 3.0 %collective-permute-done.6 = bf16[2048,128]{1,0:T(8,128)(2,1)S(1)} collective-permute-done((bf16[2048,128]{1,0:T(8,128)(2,1)S(1)}, bf16[2048,128]{1,0:T(8,128)(2,1)S(1)}, u32[]{:S(2)}, u32[]{:S(2)}) %collective-permute-start.6) | collective-permute-done | bytes 524320 | tf_op jit(solution)/shard_map/ppermute | solution.py:24
  48.7 3.1 %collective-permute-done.5 = bf16[2048,128]{1,0:T(8,128)(2,1)S(1)} collective-permute-done((bf16[2048,128]{1,0:T(8,128)(2,1)S(1)}, bf16[2048,128]{1,0:T(8,128)(2,1)S(1)}, u32[]{:S(2)}, u32[]{:S(2)}) %collective-permute-start.5) | collective-permute-done | bytes 524320 | tf_op jit(solution)/shard_map/ppermute | solution.py:24
  51.9 5.5 %collective-permute-start.12 = (bf16[1024,128]{1,0:T(8,128)(2,1)S(1)}, bf16[1024,128]{1,0:T(8,128)(2,1)S(1)}, u32[]{:S(2)}, u32[]{:S(2)}) collective-permute-start(bf16[1024,128]{1,0:T(8,128)(2,1)S(1)} %slice.30), channel_id=1, source_target_pairs={{0,48},{1,49},{2,50},{3,51},{4,52},{5,53},{6,54},{7,55},{8,56},{9,... | collective-permute-start | bytes 786440 | tf_op jit(solution)/shard_map/ppermute | solution.py:24
  57.4 0.1 collective-permute-start.11
  57.5 0.1 collective-permute-start.10
  57.6 1.4 collective-permute-start.9
  59.0 4.3 %collective-permute-done.12 = bf16[1024,128]{1,0:T(8,128)(2,1)S(1)} collective-permute-done((bf16[1024,128]{1,0:T(8,128)(2,1)S(1)}, bf16[1024,128]{1,0:T(8,128)(2,1)S(1)}, u32[]{:S(2)}, u32[]{:S(2)}) %collective-permute-start.12) | collective-permute-done | bytes 262176 | tf_op jit(solution)/shard_map/ppermute | solution.py:24
  63.3 3.3 %collective-permute-done.11 = bf16[1024,128]{1,0:T(8,128)(2,1)S(1)} collective-permute-done((bf16[1024,128]{1,0:T(8,128)(2,1)S(1)}, bf16[1024,128]{1,0:T(8,128)(2,1)S(1)}, u32[]{:S(2)}, u32[]{:S(2)}) %collective-permute-start.11) | collective-permute-done | bytes 262176 | tf_op jit(solution)/shard_map/ppermute | solution.py:24
  66.7 0.3 pad_maximum_fusion.mine_ref.inverse_mine_ref
  67.0 0.3 copy-done.13
  67.3 0.1 copy-done.14
  67.4 1.3 collective-permute-start.18
  68.8 0.6 stack.74.place_ref
  69.4 11.0 %collective-permute-start.17 = (bf16[1024,128]{1,0:T(8,128)(2,1)S(1)}, bf16[1024,128]{1,0:T(8,128)(2,1)S(1)}, u32[]{:S(2)}, u32[]{:S(2)}) collective-permute-start(bf16[1024,128]{1,0:T(8,128)(2,1)S(1)} %copy-done.9), channel_id=1, source_target_pairs={{0,32},{1,33},{2,34},{3,35},{4,36},{5,37},{6,38},{7,39},{8,40},{9,... | collective-permute-start | bytes 786440 | tf_op jit(solution)/shard_map/ppermute | solution.py:24
  80.4 1.5 collective-permute-start.15
  81.9 13.7 %lower_first.1 = (bf16[1024,1024]{1,0:T(8,128)(2,1)}, bf16[2048,1024]{1,0:T(8,128)(2,1)}) custom-call(s32[5]{0:T(128)} %stack.74.place_ref, bf16[2,1024,128]{2,1,0:T(8,128)(2,1)} %copy-done.5, bf16[2,1024,128]{2,1,0:T(8,128)(2,1)} %copy-done.11, bf16[2,1024,128]{2,1,0:T(8,128)(2,1)} %copy-done.10, bf16[1024,128]{1,0:T(8,128)(2,1)} %copy-done.14, ...), custom_call_target="tpu_custom_call" | custom-call | flops 4294967296 | bytes 14680064 | tf_op jit(solution)/shard_map/lower_first/pallas_call | solution.py:114
  95.6 0.1 pad_maximum_fusion.2.mine_ref
  95.7 1.0 collective-permute-start.19
  96.7 9.7 %schur.2 = bf16[16,8,128,128]{3,2,1,0:T(8,128)(2,1)} custom-call(bf16[2048,1024]{1,0:T(8,128)(2,1)} %get-tuple-element.47.left_ref, bf16[1024,1024]{1,0:T(8,128)(2,1)} %get-tuple-element.48.right_ref, bf16[2048,2048]{1,0:T(8,128)(2,1)} %bitcast.53, bf16[2048,2048]{1,0:T(8,128)(2,1)} %bitcast.54), custom_call_target="tpu_custom_call" | custom-call | flops 4294967296 | bytes 14680064 | tf_op jit(solution)/shard_map/schur/pallas_call | solution.py:178
  106.4 1.0 copy-done.3
  107.4 7.8 %all-to-all-start.1 = ((bf16[128,128,128]{2,1,0:T(8,128)(2,1)}), bf16[128,128,128]{2,1,0:T(8,128)(2,1)}, u32[]{:S(2)}, u32[]{:S(2)}) async-start(bf16[128,128,128]{2,1,0:T(8,128)(2,1)} %bitcast.58), calls=%async_computation.1 | async-start | bytes 8388608 | tf_op jit(solution)/shard_map/all_to_all | solution.py:340
  115.2 7.1 %lower_right.1.right_ref = bf16[1024,1024]{1,0:T(8,128)(2,1)} custom-call(s32[5]{0:T(128)} %stack.74.place_ref, bf16[4,1024,128]{2,1,0:T(8,128)(2,1)} %copy-done.1, bf16[4,1024,128]{2,1,0:T(8,128)(2,1)} %copy-done.3, bf16[4,2048,128]{2,1,0:T(8,128)(2,1)} %copy-done, bf16[4,2048,128]{2,1,0:T(8,128)(2,1)} %collective-permute-done.18.other_ref.inverse_other_ref), custom_call_target="tpu_custom_call" | custom-call | flops 1610612736 | bytes 6291456 | tf_op jit(solution)/shard_map/lower_right/pallas_call | solution.py:152
  122.2 9.7 %schur.3 = bf16[16,8,128,128]{3,2,1,0:T(8,128)(2,1)} custom-call(bf16[2048,1024]{1,0:T(8,128)(2,1)} %get-tuple-element.47.left_ref, bf16[1024,1024]{1,0:T(8,128)(2,1)} %lower_right.1.right_ref, bf16[2048,2048]{1,0:T(8,128)(2,1)} %bitcast.55, bf16[2048,2048]{1,0:T(8,128)(2,1)} %bitcast.56), custom_call_target="tpu_custom_call" | custom-call | flops 4294967296 | bytes 14680064 | tf_op jit(solution)/shard_map/schur/pallas_call | solution.py:178
  132.0 35.6 %all-to-all-done.1.schur_in_ref = bf16[128,128,128]{2,1,0:T(8,128)(2,1)} async-done(((bf16[128,128,128]{2,1,0:T(8,128)(2,1)}), bf16[128,128,128]{2,1,0:T(8,128)(2,1)}, u32[]{:S(2)}, u32[]{:S(2)}) %all-to-all-start.1) | async-done | bytes 4194336 | tf_op jit(solution)/shard_map/all_to_all | solution.py:340
  167.6 6.5 %all-to-all-start = ((bf16[128,128,128]{2,1,0:T(8,128)(2,1)}), bf16[128,128,128]{2,1,0:T(8,128)(2,1)}, u32[]{:S(2)}, u32[]{:S(2)}) async-start(bf16[128,128,128]{2,1,0:T(8,128)(2,1)} %bitcast.57), calls=%async_computation | async-start | bytes 8388608 | tf_op jit(solution)/shard_map/all_to_all | solution.py:340
  174.1 0.1 fusion
  174.2 3.3 %reshape.38.col_map_ref = s32[2,2,1024,1]{3,2,1,0:T(8,128)} reshape(s32[2,2,8,128]{3,2,1,0:T(8,128)S(1)} %fusion) | data formatting | bytes 32768 | tf_op jit(solution)/shard_map/reshape | solution.py:337
  177.5 0.6 broadcast_subtract_fusion
  178.1 15.3 %place.2.refs_0_ = f32[1024,2048]{1,0:T(8,128)} custom-call(s32[5]{0:T(128)} %stack.74.place_ref, bf16[128,128,128]{2,1,0:T(8,128)(2,1)} %all-to-all-done.1.schur_in_ref, s32[2,1,1024]{2,1,0:T(1,128)} %bitcast.76, s32[2,2,1024,1]{3,2,1,0:T(8,128)} %reshape.38.col_map_ref, bf16[1024,2048]{1,0:T(8,128)(2,1)} %base_ref.3), custom_call_target="tpu_custom_call" | custom-call | flops 8589934592 | bytes 10485760 | tf_op jit(solution)/shard_map/place/pallas_call | solution.py:239
  193.4 33.0 %all-to-all-done.schur_in_ref = bf16[128,128,128]{2,1,0:T(8,128)(2,1)} async-done(((bf16[128,128,128]{2,1,0:T(8,128)(2,1)}), bf16[128,128,128]{2,1,0:T(8,128)(2,1)}, u32[]{:S(2)}, u32[]{:S(2)}) %all-to-all-start) | async-done | bytes 4194336 | tf_op jit(solution)/shard_map/all_to_all | solution.py:340
  226.4 15.3 %place.3 = f32[1024,2048]{1,0:T(8,128)} custom-call(s32[5]{0:T(128)} %stack.74.place_ref, bf16[128,128,128]{2,1,0:T(8,128)(2,1)} %all-to-all-done.schur_in_ref, s32[2,1,1024]{2,1,0:T(1,128)} %bitcast.77, s32[2,2,1024,1]{3,2,1,0:T(8,128)} %reshape.38.col_map_ref, bf16[1024,2048]{1,0:T(8,128)(2,1)} %base_ref.3, ...), custom_call_target="tpu_custom_call", output_to_operand_aliasing={{}: (5, {})} | custom-call | flops 8589934592 | bytes 10485760 | tf_op jit(solution)/shard_map/place/pallas_call | solution.py:239
  (53 shorter events, 0.4 us)
Async XLA Ops:
  0.0 6.7 %copy-start.2 = (bf16[1,2048,128]{2,1,0:T(8,128)(2,1)S(1)}, bf16[1,2048,128]{2,1,0:T(8,128)(2,1)}, u32[]{:S(2)}) copy-start(bf16[1,2048,128]{2,1,0:T(8,128)(2,1)} %param.6) | copy-start | bytes 1572868
  2.1 24.0 %collective-permute-start = (bf16[2048,128]{1,0:T(8,128)(2,1)S(1)}, bf16[2048,128]{1,0:T(8,128)(2,1)S(1)}, u32[]{:S(2)}, u32[]{:S(2)}) collective-permute-start(bf16[2048,128]{1,0:T(8,128)(2,1)S(1)} %pad_maximum_fusion.3), channel_id=1, source_target_pairs={{0,0},{1,8},{2,16},{3,24},{4,32},{5,40},{6,48},{7,56},{8,1},{9,9},... | collective-permute-start | bytes 1572872 | tf_op jit(solution)/shard_map/ppermute | solution.py:24
  6.8 10.2 %collective-permute-start.1 = (bf16[1024,128]{1,0:T(8,128)(2,1)S(1)}, bf16[1024,128]{1,0:T(8,128)(2,1)S(1)}, u32[]{:S(2)}, u32[]{:S(2)}) collective-permute-start(bf16[1024,128]{1,0:T(8,128)(2,1)S(1)} %get-tuple-element.59), channel_id=1, source_target_pairs={{0,4},{1,5},{2,6},{3,7},{4,0},{5,1},{6,2},{7,3},{8,12},{9,13},{10,... | collective-permute-start | bytes 786440 | tf_op jit(solution)/shard_map/ppermute | solution.py:24
  10.6 15.0 %collective-permute-start.4 = (bf16[1024,128]{1,0:T(8,128)(2,1)S(1)}, bf16[1024,128]{1,0:T(8,128)(2,1)S(1)}, u32[]{:S(2)}, u32[]{:S(2)}) collective-permute-start(bf16[1024,128]{1,0:T(8,128)(2,1)S(1)} %get-tuple-element.58), channel_id=1, source_target_pairs={{0,2},{1,3},{2,0},{3,1},{4,6},{5,7},{6,4},{7,5},{8,10},{9,11},{10,... | collective-permute-start | bytes 786440 | tf_op jit(solution)/shard_map/ppermute | solution.py:24
  12.1 13.5 %collective-permute-start.3 = (bf16[1024,128]{1,0:T(8,128)(2,1)S(1)}, bf16[1024,128]{1,0:T(8,128)(2,1)S(1)}, u32[]{:S(2)}, u32[]{:S(2)}) collective-permute-start(bf16[1024,128]{1,0:T(8,128)(2,1)S(1)} %get-tuple-element.58), channel_id=1, source_target_pairs={{0,3},{1,0},{2,1},{3,2},{4,7},{5,4},{6,5},{7,6},{8,11},{9,8},{10,9... | collective-permute-start | bytes 786440 | tf_op jit(solution)/shard_map/ppermute | solution.py:24
  12.7 13.5 %collective-permute-start.2 = (bf16[1024,128]{1,0:T(8,128)(2,1)S(1)}, bf16[1024,128]{1,0:T(8,128)(2,1)}, u32[]{:S(2)}, u32[]{:S(2)}) collective-permute-start(bf16[1024,128]{1,0:T(8,128)(2,1)S(1)} %get-tuple-element.58), channel_id=1, source_target_pairs={{0,1},{1,2},{2,3},{3,0},{4,5},{5,6},{6,7},{7,4},{8,9},{9,10},{10,1... | collective-permute-start | bytes 786440 | tf_op jit(solution)/shard_map/ppermute | solution.py:24
  26.2 13.4 %copy-start.6 = (bf16[2048,128]{1,0:T(8,128)(2,1)}, bf16[2048,128]{1,0:T(8,128)(2,1)S(1)}, u32[]{:S(2)}) copy-start(bf16[2048,128]{1,0:T(8,128)(2,1)S(1)} %collective-permute-done) | copy-start | bytes 1572868
  26.3 31.1 %copy-start.5 = (bf16[2,1024,128]{2,1,0:T(8,128)(2,1)}, bf16[2,1024,128]{2,1,0:T(8,128)(2,1)S(1)}, u32[]{:S(2)}) copy-start(bf16[2,1024,128]{2,1,0:T(8,128)(2,1)S(1)} %pad_maximum_fusion.4.near_ref) | copy-start | bytes 1572868
  26.3 16.3 %collective-permute-start.8 = (bf16[2,1024,128]{2,1,0:T(8,128)(2,1)S(1)}, bf16[2,1024,128]{2,1,0:T(8,128)(2,1)S(1)}, u32[]{:S(2)}, u32[]{:S(2)}) collective-permute-start(bf16[2,1024,128]{2,1,0:T(8,128)(2,1)S(1)} %pad_maximum_fusion.4.near_ref), channel_id=1, source_target_pairs={{0,3},{1,0},{2,1},{3,2},{4,7},{5,4},{6,5},{7,6},{8,11},{9,8},{10,9... | collective-permute-start | bytes 1572872 | tf_op jit(solution)/shard_map/ppermute | solution.py:24
  31.8 13.9 %collective-permute-start.7 = (bf16[2,1024,128]{2,1,0:T(8,128)(2,1)S(1)}, bf16[2,1024,128]{2,1,0:T(8,128)(2,1)S(1)}, u32[]{:S(2)}, u32[]{:S(2)}) collective-permute-start(bf16[2,1024,128]{2,1,0:T(8,128)(2,1)S(1)} %pad_maximum_fusion.4.near_ref), channel_id=1, source_target_pairs={{0,1},{1,2},{2,3},{3,0},{4,5},{5,6},{6,7},{7,4},{8,9},{9,10},{10,1... | collective-permute-start | bytes 1572872 | tf_op jit(solution)/shard_map/ppermute | solution.py:24
  31.8 16.9 %collective-permute-start.6 = (bf16[2048,128]{1,0:T(8,128)(2,1)S(1)}, bf16[2048,128]{1,0:T(8,128)(2,1)S(1)}, u32[]{:S(2)}, u32[]{:S(2)}) collective-permute-start(bf16[2048,128]{1,0:T(8,128)(2,1)S(1)} %collective-permute-done), channel_id=1, source_target_pairs={{0,48},{1,49},{2,50},{3,51},{4,52},{5,53},{6,54},{7,55},{8,56},{9,... | collective-permute-start | bytes 1572872 | tf_op jit(solution)/shard_map/ppermute | solution.py:24
  38.5 13.3 %collective-permute-start.5 = (bf16[2048,128]{1,0:T(8,128)(2,1)S(1)}, bf16[2048,128]{1,0:T(8,128)(2,1)S(1)}, u32[]{:S(2)}, u32[]{:S(2)}) collective-permute-start(bf16[2048,128]{1,0:T(8,128)(2,1)S(1)} %collective-permute-done), channel_id=1, source_target_pairs={{0,16},{1,17},{2,18},{3,19},{4,20},{5,21},{6,22},{7,23},{8,24},{9,... | collective-permute-start | bytes 1572872 | tf_op jit(solution)/shard_map/ppermute | solution.py:24
  39.6 27.4 %copy-start.4 = (bf16[4,1024,128]{2,1,0:T(8,128)(2,1)}, bf16[4,1024,128]{2,1,0:T(8,128)(2,1)S(1)}, u32[]{:S(2)}) copy-start(bf16[4,1024,128]{2,1,0:T(8,128)(2,1)S(1)} %pad_maximum_fusion.1.below_mine_ref) | copy-start | bytes 3145732
  39.6 27.0 %collective-permute-start.14 = (bf16[4,1024,128]{2,1,0:T(8,128)(2,1)S(1)}, bf16[4,1024,128]{2,1,0:T(8,128)(2,1)}, u32[]{:S(2)}, u32[]{:S(2)}) collective-permute-start(bf16[4,1024,128]{2,1,0:T(8,128)(2,1)S(1)} %pad_maximum_fusion.1.below_mine_ref), channel_id=1, source_target_pairs={{0,4},{1,5},{2,6},{3,7},{4,0},{5,1},{6,2},{7,3},{8,12},{9,13},{10,... | collective-permute-start | bytes 3145736 | tf_op jit(solution)/shard_map/ppermute | solution.py:24
  41.3 25.4 %copy-start.7 = (bf16[2048,128]{1,0:T(8,128)(2,1)S(1)}, bf16[2048,128]{1,0:T(8,128)(2,1)}, u32[]{:S(2)}) copy-start(bf16[2048,128]{1,0:T(8,128)(2,1)} %copy-done.6) | copy-start | bytes 1572868
  42.6 24.4 %copy-start.10 = (bf16[2,1024,128]{2,1,0:T(8,128)(2,1)}, bf16[2,1024,128]{2,1,0:T(8,128)(2,1)S(1)}, u32[]{:S(2)}) copy-start(bf16[2,1024,128]{2,1,0:T(8,128)(2,1)S(1)} %collective-permute-done.8.ahead_ref) | copy-start | bytes 1572868
  42.6 15.0 %collective-permute-start.13 = (bf16[1024,128]{1,0:T(8,128)(2,1)S(1)}, bf16[1024,128]{1,0:T(8,128)(2,1)S(1)}, u32[]{:S(2)}, u32[]{:S(2)}) collective-permute-start(bf16[1024,128]{1,0:T(8,128)(2,1)S(1)} %bitcast.65), channel_id=1, source_target_pairs={{0,0},{1,8},{2,16},{3,24},{4,32},{5,40},{6,48},{7,56},{8,1},{9,9},... | collective-permute-start | bytes 786440 | tf_op jit(solution)/shard_map/ppermute | solution.py:24
  45.7 21.0 %copy-start.11 = (bf16[2,1024,128]{2,1,0:T(8,128)(2,1)}, bf16[2,1024,128]{2,1,0:T(8,128)(2,1)S(1)}, u32[]{:S(2)}) copy-start(bf16[2,1024,128]{2,1,0:T(8,128)(2,1)S(1)} %collective-permute-done.7.behind_ref) | copy-start | bytes 1572868
  51.9 11.4 %collective-permute-start.12 = (bf16[1024,128]{1,0:T(8,128)(2,1)S(1)}, bf16[1024,128]{1,0:T(8,128)(2,1)S(1)}, u32[]{:S(2)}, u32[]{:S(2)}) collective-permute-start(bf16[1024,128]{1,0:T(8,128)(2,1)S(1)} %slice.30), channel_id=1, source_target_pairs={{0,48},{1,49},{2,50},{3,51},{4,52},{5,53},{6,54},{7,55},{8,56},{9,... | collective-permute-start | bytes 786440 | tf_op jit(solution)/shard_map/ppermute | solution.py:24
  57.4 9.2 %collective-permute-start.11 = (bf16[1024,128]{1,0:T(8,128)(2,1)S(1)}, bf16[1024,128]{1,0:T(8,128)(2,1)S(1)}, u32[]{:S(2)}, u32[]{:S(2)}) collective-permute-start(bf16[1024,128]{1,0:T(8,128)(2,1)S(1)} %slice.29), channel_id=1, source_target_pairs={{0,16},{1,17},{2,18},{3,19},{4,20},{5,21},{6,22},{7,23},{8,24},{9,... | collective-permute-start | bytes 786440 | tf_op jit(solution)/shard_map/ppermute | solution.py:24
  57.5 9.2 %collective-permute-start.10 = (bf16[1024,128]{1,0:T(8,128)(2,1)S(1)}, bf16[1024,128]{1,0:T(8,128)(2,1)S(1)}, u32[]{:S(2)}, u32[]{:S(2)}) collective-permute-start(bf16[1024,128]{1,0:T(8,128)(2,1)S(1)} %slice_bitcast_fusion), channel_id=1, source_target_pairs={{0,3},{1,0},{2,1},{3,2},{4,7},{5,4},{6,5},{7,6},{8,11},{9,8},{10,9... | collective-permute-start | bytes 786440 | tf_op jit(solution)/shard_map/ppermute | solution.py:24
  57.6 9.1 %copy-start.8 = (bf16[1024,128]{1,0:T(8,128)(2,1)}, bf16[1024,128]{1,0:T(8,128)(2,1)S(1)}, u32[]{:S(2)}) copy-start(bf16[1024,128]{1,0:T(8,128)(2,1)S(1)} %collective-permute-done.13) | copy-start | bytes 786436
  57.6 9.1 %collective-permute-start.9 = (bf16[1024,128]{1,0:T(8,128)(2,1)S(1)}, bf16[1024,128]{1,0:T(8,128)(2,1)S(1)}, u32[]{:S(2)}, u32[]{:S(2)}) collective-permute-start(bf16[1024,128]{1,0:T(8,128)(2,1)S(1)} %slice_bitcast_fusion.1), channel_id=1, source_target_pairs={{0,1},{1,2},{2,3},{3,0},{4,5},{5,6},{6,7},{7,4},{8,9},{9,10},{10,1... | collective-permute-start | bytes 786440 | tf_op jit(solution)/shard_map/ppermute | solution.py:24
  66.6 0.7 copy-start.13
  66.6 0.8 copy-start.14
  66.7 2.7 %copy-start.9 = (bf16[1024,128]{1,0:T(8,128)(2,1)S(1)}, bf16[1024,128]{1,0:T(8,128)(2,1)}, u32[]{:S(2)}) copy-start(bf16[1024,128]{1,0:T(8,128)(2,1)} %copy-done.8) | copy-start | bytes 786436
  67.4 14.4 %copy-start = (bf16[4,2048,128]{2,1,0:T(8,128)(2,1)}, bf16[4,2048,128]{2,1,0:T(8,128)(2,1)S(1)}, u32[]{:S(2)}) copy-start(bf16[4,2048,128]{2,1,0:T(8,128)(2,1)S(1)} %pad_maximum_fusion.mine_ref.inverse_mine_ref) | copy-start | bytes 6291460
  67.4 14.4 %collective-permute-start.18 = (bf16[4,2048,128]{2,1,0:T(8,128)(2,1)S(1)}, bf16[4,2048,128]{2,1,0:T(8,128)(2,1)}, u32[]{:S(2)}, u32[]{:S(2)}) collective-permute-start(bf16[4,2048,128]{2,1,0:T(8,128)(2,1)S(1)} %pad_maximum_fusion.mine_ref.inverse_mine_ref), channel_id=1, source_target_pairs={{0,8},{1,9},{2,10},{3,11},{4,12},{5,13},{6,14},{7,15},{8,0},{9,1},... | collective-permute-start | bytes 6291464 | tf_op jit(solution)/shard_map/ppermute | solution.py:24
  69.4 26.2 %collective-permute-start.17 = (bf16[1024,128]{1,0:T(8,128)(2,1)S(1)}, bf16[1024,128]{1,0:T(8,128)(2,1)S(1)}, u32[]{:S(2)}, u32[]{:S(2)}) collective-permute-start(bf16[1024,128]{1,0:T(8,128)(2,1)S(1)} %copy-done.9), channel_id=1, source_target_pairs={{0,32},{1,33},{2,34},{3,35},{4,36},{5,37},{6,38},{7,39},{8,40},{9,... | collective-permute-start | bytes 786440 | tf_op jit(solution)/shard_map/ppermute | solution.py:24
  80.4 15.2 %collective-permute-start.16 = (bf16[1024,128]{1,0:T(8,128)(2,1)S(1)}, bf16[1024,128]{1,0:T(8,128)(2,1)S(1)}, u32[]{:S(2)}, u32[]{:S(2)}) collective-permute-start(bf16[1024,128]{1,0:T(8,128)(2,1)S(1)} %copy-done.9), channel_id=1, source_target_pairs={{0,48},{1,49},{2,50},{3,51},{4,52},{5,53},{6,54},{7,55},{8,56},{9,... | collective-permute-start | bytes 786440 | tf_op jit(solution)/shard_map/ppermute | solution.py:24
  80.4 15.2 %collective-permute-start.15 = (bf16[1024,128]{1,0:T(8,128)(2,1)S(1)}, bf16[1024,128]{1,0:T(8,128)(2,1)S(1)}, u32[]{:S(2)}, u32[]{:S(2)}) collective-permute-start(bf16[1024,128]{1,0:T(8,128)(2,1)S(1)} %copy-done.9), channel_id=1, source_target_pairs={{0,16},{1,17},{2,18},{3,19},{4,20},{5,21},{6,22},{7,23},{8,24},{9,... | collective-permute-start | bytes 786440 | tf_op jit(solution)/shard_map/ppermute | solution.py:24
  95.7 10.7 %copy-start.1 = (bf16[4,1024,128]{2,1,0:T(8,128)(2,1)}, bf16[4,1024,128]{2,1,0:T(8,128)(2,1)S(1)}, u32[]{:S(2)}) copy-start(bf16[4,1024,128]{2,1,0:T(8,128)(2,1)S(1)} %pad_maximum_fusion.2.mine_ref) | copy-start | bytes 3145732
  95.7 10.7 %collective-permute-start.19 = (bf16[4,1024,128]{2,1,0:T(8,128)(2,1)S(1)}, bf16[4,1024,128]{2,1,0:T(8,128)(2,1)S(1)}, u32[]{:S(2)}, u32[]{:S(2)}) collective-permute-start(bf16[4,1024,128]{2,1,0:T(8,128)(2,1)S(1)} %pad_maximum_fusion.2.mine_ref), channel_id=1, source_target_pairs={{0,8},{1,9},{2,10},{3,11},{4,12},{5,13},{6,14},{7,15},{8,0},{9,1},... | collective-permute-start | bytes 3145736 | tf_op jit(solution)/shard_map/ppermute | solution.py:24
  106.4 1.0 copy-start.3
  107.4 60.2 %all-to-all-start.1 = ((bf16[128,128,128]{2,1,0:T(8,128)(2,1)}), bf16[128,128,128]{2,1,0:T(8,128)(2,1)}, u32[]{:S(2)}, u32[]{:S(2)}) async-start(bf16[128,128,128]{2,1,0:T(8,128)(2,1)} %bitcast.58), calls=%async_computation.1 | async-start | bytes 8388608 | tf_op jit(solution)/shard_map/all_to_all | solution.py:340
  167.6 6.5 %copy-start.12 = (s32[2,16384]{1,0:T(2,128)S(1)}, s32[2,16384]{1,0:T(2,128)}, u32[]{:S(2)}) copy-start(s32[2,16384]{1,0:T(2,128)} %param.8) | copy-start | bytes 393220
  167.6 58.9 %all-to-all-start = ((bf16[128,128,128]{2,1,0:T(8,128)(2,1)}), bf16[128,128,128]{2,1,0:T(8,128)(2,1)}, u32[]{:S(2)}, u32[]{:S(2)}) async-start(bf16[128,128,128]{2,1,0:T(8,128)(2,1)} %bitcast.57), calls=%async_computation | async-start | bytes 8388608 | tf_op jit(solution)/shard_map/all_to_all | solution.py:340

commit v6 on v5

--- a/solution.py
+++ b/solution.py
@@ -286,12 +286,19 @@
         return shift(array, lambda h, r, c: (h, r ^ 1, c))
 
     runs = panel[0].reshape(8, 2, 128, 128)
-    even = spread(jnp.concatenate([runs[:, 0].reshape(1024, 128), inverse_block[0]]))
-    odd = spread(runs[:, 1].reshape(1024, 128))
+    turned = spread(
+        jnp.concatenate(
+            [
+                runs[:, 0].reshape(1024, 128),
+                inverse_block[0],
+                runs[:, 1].reshape(1024, 128),
+            ]
+        )
+    )
     upper, below = panel[0, :1024], panel[0, 1024:]
-    even, twin, below_one, below_three, below_two = lax.optimization_barrier(
+    turned, twin, below_one, below_three, below_two = lax.optimization_barrier(
         (
-            even,
+            turned,
             swap_z(upper),
             ahead_y(below),
             behind_y(below),
@@ -301,31 +308,24 @@
     pair = jnp.stack([jnp.where(col < 4, upper, twin), jnp.where(col < 4, twin, upper)])
     below_mine = jnp.stack([below, below_one, below_three, below_two])
     one, three, behind, ahead = lax.optimization_barrier(
-        (ahead_x(even), behind_x(even), ahead_y(pair), behind_y(pair))
-    )
-    below_other = swap_z(below_mine)
-    far_first, far_second, two_first, two_second, odd, below_other = lax.optimization_barrier(
+        (ahead_x(turned), behind_x(turned), ahead_y(pair), behind_y(pair))
+    )
+    far_first, far_second, two_first, two_second, below_other = lax.optimization_barrier(
         (
             ahead_y(behind[0]),
             behind_y(ahead[1]),
-            ahead_x(one[:1024]),
-            behind_x(three[1024:]),
-            odd,
-            below_other,
+            ahead_x(one[:1536]),
+            behind_x(three[1536:]),
+            swap_z(below_mine),
         )
     )
-    mine = jnp.stack([even, one, three, jnp.concatenate([two_first, two_second])])
+    two = jnp.concatenate([two_first, two_second])
+    mine = jnp.stack([part[:2048] for part in (turned, one, three, two)])
+    odd_mine = jnp.stack([part[2048:] for part in (turned, one, three, two)])
     other = swap_core(mine)
+    odd_other = swap_core(odd_mine)
     rows = (pair, behind, ahead, far_first, far_second, below_mine, below_other)
-    odd_parts = (
-        ahead_x(odd),
-        behind_x(odd),
-        shift(odd, lambda h, r, c: (h, r ^ 4, c)),
-    )
     right_even, left = lower_first(place, rows, mine, other)
-    odd_parts, right_even, left = lax.optimization_barrier((odd_parts, right_even, left))
-    odd_mine = jnp.stack([odd, *odd_parts])
-    odd_other = swap_core(odd_mine)
 
     maps = child_maps.reshape(2, 8, 16, 128)
     row_maps = (

time: 242 us -> 240 us (level)
  starting transfers between devices: 64.4 us -> 51.9 us
  waiting for transfers between devices: 96.3 us -> 108 us
    ppermute x20 -> x16, starting transfers between devices: 50.1 us -> 37.6 us  [shift(): return lax.ppermute(array, ALL, pairs)]
    ppermute x20 -> x16, waiting for transfers between devices: 27.7 us -> 39 us  [shift(): return lax.ppermute(array, ALL, pairs)]
  transfers between devices with their start and end apart: 22 -> 18, of which waited for: 10 -> 14; matrix products, arithmetic and copies ran while one was open for 2% -> 3% of each run, Pallas kernels for 23% -> 23%
where the time goes in v6:
time: 240 us; the launch traced here: 239 us
  waiting for transfers between devices  108 us (45%)
  Pallas kernels  70.9 us (30%)
  starting transfers between devices  51.9 us (22%)
  local copies, waits for them, and re-layouts  5.42 us (2%)
  other arithmetic  3.37 us (1%)
    all_to_all x2, waiting for transfers between devices, exchange(): return lax.all_to_all(parcels.reshape(128, 128, 128), ALL, 0, 0, tiled=True)  68.6 us
    ppermute x16, waiting for transfers between devices, shift(): return lax.ppermute(array, ALL, pairs)  39 us
    ppermute x16, starting transfers between devices, shift(): return lax.ppermute(array, ALL, pairs)  37.6 us
    pallas_call x2, Pallas kernels, place_children(): pl.pallas_call(functools.partial(place_kernel, b), grid_spec=grid_spec, o...  30.7 us
    pallas_call x2, Pallas kernels, schur_parcels(): pl.pallas_call(schur_kernel, grid=(4,), in_specs=[pl.BlockSpec((2048, 102...  19.4 us
    all_to_all x2, starting transfers between devices, exchange(): return lax.all_to_all(parcels.reshape(128, 128, 128), ALL, 0, 0, tiled=True)  14.3 us
    pallas_call x1, Pallas kernels, lower_first(): pl.pallas_call(first_kernel, grid_spec=grid_spec, out_shape=[jax.ShapeDty...  13.7 us
    pallas_call x1, Pallas kernels, lower_right(): pl.pallas_call(right_kernel, grid_spec=grid_spec, out_shape=jax.ShapeDtyp...  7.1 us
  transfers between devices with their start and end apart: 18, of which 14 were waited for; matrix products, arithmetic and copies ran while one was open for 3% of the time, Pallas kernels for 23%

profile of v6, /device:TPU:1, one launch (start us, length us, event | category | flops | bytes accessed | tf_op | source)
XLA Modules:
  0.0 239.4 jit_solution(18415956887543278638)
XLA Ops:
  0.0 1.1 fusion.3
  1.1 1.0 pad_maximum_fusion.3
  2.1 4.6 %collective-permute-start = (bf16[3072,128]{1,0:T(8,128)(2,1)S(1)}, bf16[3072,128]{1,0:T(8,128)(2,1)S(1)}, u32[]{:S(2)}, u32[]{:S(2)}) collective-permute-start(bf16[3072,128]{1,0:T(8,128)(2,1)S(1)} %pad_maximum_fusion.3), channel_id=1, source_target_pairs={{0,0},{1,8},{2,16},{3,24},{4,32},{5,40},{6,48},{7,56},{8,1},{9,9},... | collective-permute-start | bytes 2359304 | tf_op jit(solution)/shard_map/ppermute | solution.py:24
  6.8 0.1 fusion.2
  6.8 3.7 %collective-permute-start.1 = (bf16[1024,128]{1,0:T(8,128)(2,1)S(1)}, bf16[1024,128]{1,0:T(8,128)(2,1)S(1)}, u32[]{:S(2)}, u32[]{:S(2)}) collective-permute-start(bf16[1024,128]{1,0:T(8,128)(2,1)S(1)} %get-tuple-element.47), channel_id=1, source_target_pairs={{0,4},{1,5},{2,6},{3,7},{4,0},{5,1},{6,2},{7,3},{8,12},{9,13},{10,... | collective-permute-start | bytes 786440 | tf_op jit(solution)/shard_map/ppermute | solution.py:24
  10.6 1.5 collective-permute-start.4
  12.1 0.6 collective-permute-start.3
  12.7 0.9 collective-permute-start.2
  13.6 3.4 %collective-permute-done.1 = bf16[1024,128]{1,0:T(8,128)(2,1)S(1)} collective-permute-done((bf16[1024,128]{1,0:T(8,128)(2,1)S(1)}, bf16[1024,128]{1,0:T(8,128)(2,1)S(1)}, u32[]{:S(2)}, u32[]{:S(2)}) %collective-permute-start.1) | collective-permute-done | bytes 262176 | tf_op jit(solution)/shard_map/ppermute | solution.py:24
  17.0 8.9 %collective-permute-done.4 = bf16[1024,128]{1,0:T(8,128)(2,1)S(1)} collective-permute-done((bf16[1024,128]{1,0:T(8,128)(2,1)S(1)}, bf16[1024,128]{1,0:T(8,128)(2,1)S(1)}, u32[]{:S(2)}, u32[]{:S(2)}) %collective-permute-start.4) | collective-permute-done | bytes 262176 | tf_op jit(solution)/shard_map/ppermute | solution.py:24
  25.9 1.1 collective-permute-done.2
  26.9 15.5 %collective-permute-start.6 = (bf16[3072,128]{1,0:T(8,128)(2,1)S(1)}, bf16[3072,128]{1,0:T(8,128)(2,1)S(1)}, u32[]{:S(2)}, u32[]{:S(2)}) collective-permute-start(bf16[3072,128]{1,0:T(8,128)(2,1)S(1)} %collective-permute-done), channel_id=1, source_target_pairs={{0,48},{1,49},{2,50},{3,51},{4,52},{5,53},{6,54},{7,55},{8,56},{9,... | collective-permute-start | bytes 2359304 | tf_op jit(solution)/shard_map/ppermute | solution.py:24
  42.6 1.2 collective-permute-start.8
  43.8 0.4 collective-permute-start.7
  44.1 1.2 pad_maximum_fusion.1.below_mine_ref
  45.3 1.8 collective-permute-start.13
  47.1 8.2 %collective-permute-done.8.ahead_ref = bf16[2,1024,128]{2,1,0:T(8,128)(2,1)S(1)} collective-permute-done((bf16[2,1024,128]{2,1,0:T(8,128)(2,1)S(1)}, bf16[2,1024,128]{2,1,0:T(8,128)(2,1)S(1)}, u32[]{:S(2)}, u32[]{:S(2)}) %collective-permute-start.8) | collective-permute-done | bytes 524320 | tf_op jit(solution)/shard_map/ppermute | solution.py:24
  55.4 2.9 %collective-permute-done.7.behind_ref = bf16[2,1024,128]{2,1,0:T(8,128)(2,1)S(1)} collective-permute-done((bf16[2,1024,128]{2,1,0:T(8,128)(2,1)S(1)}, bf16[2,1024,128]{2,1,0:T(8,128)(2,1)S(1)}, u32[]{:S(2)}, u32[]{:S(2)}) %collective-permute-start.7) | collective-permute-done | bytes 524320 | tf_op jit(solution)/shard_map/ppermute | solution.py:24
  58.2 0.7 collective-permute-done.6
  58.9 3.1 %collective-permute-done.5 = bf16[3072,128]{1,0:T(8,128)(2,1)S(1)} collective-permute-done((bf16[3072,128]{1,0:T(8,128)(2,1)S(1)}, bf16[3072,128]{1,0:T(8,128)(2,1)S(1)}, u32[]{:S(2)}, u32[]{:S(2)}) %collective-permute-start.5) | collective-permute-done | bytes 786464 | tf_op jit(solution)/shard_map/ppermute | solution.py:24
  62.0 2.1 collective-permute-start.10
  64.1 0.1 collective-permute-start.9
  64.3 0.3 collective-permute-start.12
  64.6 1.3 collective-permute-start.11
  65.8 0.1 slice_bitcast_fusion
  65.9 3.1 %collective-permute-done.10.far_second_ref = bf16[1024,128]{1,0:T(8,128)(2,1)S(1)} collective-permute-done((bf16[1024,128]{1,0:T(8,128)(2,1)S(1)}, bf16[1024,128]{1,0:T(8,128)(2,1)S(1)}, u32[]{:S(2)}, u32[]{:S(2)}) %collective-permute-start.10) | collective-permute-done | bytes 262176 | tf_op jit(solution)/shard_map/ppermute | solution.py:24
  69.0 3.2 %collective-permute-done.9.far_first_ref = bf16[1024,128]{1,0:T(8,128)(2,1)S(1)} collective-permute-done((bf16[1024,128]{1,0:T(8,128)(2,1)S(1)}, bf16[1024,128]{1,0:T(8,128)(2,1)S(1)}, u32[]{:S(2)}, u32[]{:S(2)}) %collective-permute-start.9) | collective-permute-done | bytes 262176 | tf_op jit(solution)/shard_map/ppermute | solution.py:24
  72.2 1.1 collective-permute-done.12
  73.3 1.3 collective-permute-done.11
  74.7 0.3 pad_maximum_fusion.mine_ref.inverse_mine_ref
  75.0 2.7 %collective-permute-start.14 = (bf16[4,2048,128]{2,1,0:T(8,128)(2,1)S(1)}, bf16[4,2048,128]{2,1,0:T(8,128)(2,1)}, u32[]{:S(2)}, u32[]{:S(2)}) collective-permute-start(bf16[4,2048,128]{2,1,0:T(8,128)(2,1)S(1)} %pad_maximum_fusion.mine_ref.inverse_mine_ref), channel_id=1, source_target_pairs={{0,8},{1,9},{2,10},{3,11},{4,12},{5,13},{6,14},{7,15},{8,0},{9,1},... | collective-permute-start | bytes 6291464 | tf_op jit(solution)/shard_map/ppermute | solution.py:24
  77.8 0.1 pad_maximum_fusion.2.mine_ref
  78.0 1.0 collective-permute-start.15
  79.0 0.6 stack.74.place_ref
  79.6 2.0 collective-permute-done.14.other_ref.inverse_other_ref
  81.7 13.7 %lower_first.1 = (bf16[1024,1024]{1,0:T(8,128)(2,1)}, bf16[2048,1024]{1,0:T(8,128)(2,1)}) custom-call(s32[5]{0:T(128)} %stack.74.place_ref, bf16[2,1024,128]{2,1,0:T(8,128)(2,1)} %copy-done.4, bf16[2,1024,128]{2,1,0:T(8,128)(2,1)} %copy-done.6, bf16[2,1024,128]{2,1,0:T(8,128)(2,1)} %copy-done.5, bf16[1024,128]{1,0:T(8,128)(2,1)} %copy-done.10, ...), custom_call_target="tpu_custom_call" | custom-call | flops 4294967296 | bytes 14680064 | tf_op jit(solution)/shard_map/lower_first/pallas_call | solution.py:114
  95.3 9.7 %schur.2 = bf16[16,8,128,128]{3,2,1,0:T(8,128)(2,1)} custom-call(bf16[2048,1024]{1,0:T(8,128)(2,1)} %get-tuple-element.38.left_ref, bf16[1024,1024]{1,0:T(8,128)(2,1)} %get-tuple-element.39.right_ref, bf16[2048,2048]{1,0:T(8,128)(2,1)} %bitcast.60, bf16[2048,2048]{1,0:T(8,128)(2,1)} %bitcast.61), custom_call_target="tpu_custom_call" | custom-call | flops 4294967296 | bytes 14680064 | tf_op jit(solution)/shard_map/schur/pallas_call | solution.py:178
  105.0 7.8 %all-to-all-start.1 = ((bf16[128,128,128]{2,1,0:T(8,128)(2,1)}), bf16[128,128,128]{2,1,0:T(8,128)(2,1)}, u32[]{:S(2)}, u32[]{:S(2)}) async-start(bf16[128,128,128]{2,1,0:T(8,128)(2,1)} %bitcast.65), calls=%async_computation.1 | async-start | bytes 8388608 | tf_op jit(solution)/shard_map/all_to_all | solution.py:340
  112.8 7.1 %lower_right.1.right_ref = bf16[1024,1024]{1,0:T(8,128)(2,1)} custom-call(s32[5]{0:T(128)} %stack.74.place_ref, bf16[4,1024,128]{2,1,0:T(8,128)(2,1)} %copy-done.1, bf16[4,1024,128]{2,1,0:T(8,128)(2,1)} %collective-permute-done.15.other_ref, bf16[4,2048,128]{2,1,0:T(8,128)(2,1)} %copy-done, ...), custom_call_target="tpu_custom_call" | custom-call | flops 1610612736 | bytes 6291456 | tf_op jit(solution)/shard_map/lower_right/pallas_call | solution.py:152
  119.9 9.7 %schur.3 = bf16[16,8,128,128]{3,2,1,0:T(8,128)(2,1)} custom-call(bf16[2048,1024]{1,0:T(8,128)(2,1)} %get-tuple-element.38.left_ref, bf16[1024,1024]{1,0:T(8,128)(2,1)} %lower_right.1.right_ref, bf16[2048,2048]{1,0:T(8,128)(2,1)} %bitcast.62, bf16[2048,2048]{1,0:T(8,128)(2,1)} %bitcast.63), custom_call_target="tpu_custom_call" | custom-call | flops 4294967296 | bytes 14680064 | tf_op jit(solution)/shard_map/schur/pallas_call | solution.py:178
  129.6 35.6 %all-to-all-done.1.schur_in_ref = bf16[128,128,128]{2,1,0:T(8,128)(2,1)} async-done(((bf16[128,128,128]{2,1,0:T(8,128)(2,1)}), bf16[128,128,128]{2,1,0:T(8,128)(2,1)}, u32[]{:S(2)}, u32[]{:S(2)}) %all-to-all-start.1) | async-done | bytes 4194336 | tf_op jit(solution)/shard_map/all_to_all | solution.py:340
  165.2 6.5 %all-to-all-start = ((bf16[128,128,128]{2,1,0:T(8,128)(2,1)}), bf16[128,128,128]{2,1,0:T(8,128)(2,1)}, u32[]{:S(2)}, u32[]{:S(2)}) async-start(bf16[128,128,128]{2,1,0:T(8,128)(2,1)} %bitcast.64), calls=%async_computation | async-start | bytes 8388608 | tf_op jit(solution)/shard_map/all_to_all | solution.py:340
  171.8 0.1 fusion.1
  171.8 3.3 %reshape.38.col_map_ref = s32[2,2,1024,1]{3,2,1,0:T(8,128)} reshape(s32[2,2,8,128]{3,2,1,0:T(8,128)S(1)} %fusion.1) | data formatting | bytes 32768 | tf_op jit(solution)/shard_map/reshape | solution.py:337
  175.1 0.6 broadcast_subtract_fusion
  175.7 15.3 %place.2.refs_0_ = f32[1024,2048]{1,0:T(8,128)} custom-call(s32[5]{0:T(128)} %stack.74.place_ref, bf16[128,128,128]{2,1,0:T(8,128)(2,1)} %all-to-all-done.1.schur_in_ref, s32[2,1,1024]{2,1,0:T(1,128)} %bitcast.75, s32[2,2,1024,1]{3,2,1,0:T(8,128)} %reshape.38.col_map_ref, bf16[1024,2048]{1,0:T(8,128)(2,1)} %base_ref.3), custom_call_target="tpu_custom_call" | custom-call | flops 8589934592 | bytes 10485760 | tf_op jit(solution)/shard_map/place/pallas_call | solution.py:239
  191.1 33.0 %all-to-all-done.schur_in_ref = bf16[128,128,128]{2,1,0:T(8,128)(2,1)} async-done(((bf16[128,128,128]{2,1,0:T(8,128)(2,1)}), bf16[128,128,128]{2,1,0:T(8,128)(2,1)}, u32[]{:S(2)}, u32[]{:S(2)}) %all-to-all-start) | async-done | bytes 4194336 | tf_op jit(solution)/shard_map/all_to_all | solution.py:340
  224.1 15.3 %place.3 = f32[1024,2048]{1,0:T(8,128)} custom-call(s32[5]{0:T(128)} %stack.74.place_ref, bf16[128,128,128]{2,1,0:T(8,128)(2,1)} %all-to-all-done.schur_in_ref, s32[2,1,1024]{2,1,0:T(1,128)} %bitcast.76, s32[2,2,1024,1]{3,2,1,0:T(8,128)} %reshape.38.col_map_ref, bf16[1024,2048]{1,0:T(8,128)(2,1)} %base_ref.3, ...), custom_call_target="tpu_custom_call", output_to_operand_aliasing={{}: (5, {})} | custom-call | flops 8589934592 | bytes 10485760 | tf_op jit(solution)/shard_map/place/pallas_call | solution.py:239
  (42 shorter events, 0.4 us)
Async XLA Ops:
  0.0 6.7 %copy-start.2 = (bf16[1,2048,128]{2,1,0:T(8,128)(2,1)S(1)}, bf16[1,2048,128]{2,1,0:T(8,128)(2,1)}, u32[]{:S(2)}) copy-start(bf16[1,2048,128]{2,1,0:T(8,128)(2,1)} %param.6) | copy-start | bytes 1572868
  2.1 24.8 %collective-permute-start = (bf16[3072,128]{1,0:T(8,128)(2,1)S(1)}, bf16[3072,128]{1,0:T(8,128)(2,1)S(1)}, u32[]{:S(2)}, u32[]{:S(2)}) collective-permute-start(bf16[3072,128]{1,0:T(8,128)(2,1)S(1)} %pad_maximum_fusion.3), channel_id=1, source_target_pairs={{0,0},{1,8},{2,16},{3,24},{4,32},{5,40},{6,48},{7,56},{8,1},{9,9},... | collective-permute-start | bytes 2359304 | tf_op jit(solution)/shard_map/ppermute | solution.py:24
  6.8 10.2 %collective-permute-start.1 = (bf16[1024,128]{1,0:T(8,128)(2,1)S(1)}, bf16[1024,128]{1,0:T(8,128)(2,1)S(1)}, u32[]{:S(2)}, u32[]{:S(2)}) collective-permute-start(bf16[1024,128]{1,0:T(8,128)(2,1)S(1)} %get-tuple-element.47), channel_id=1, source_target_pairs={{0,4},{1,5},{2,6},{3,7},{4,0},{5,1},{6,2},{7,3},{8,12},{9,13},{10,... | collective-permute-start | bytes 786440 | tf_op jit(solution)/shard_map/ppermute | solution.py:24
  10.6 15.3 %collective-permute-start.4 = (bf16[1024,128]{1,0:T(8,128)(2,1)S(1)}, bf16[1024,128]{1,0:T(8,128)(2,1)S(1)}, u32[]{:S(2)}, u32[]{:S(2)}) collective-permute-start(bf16[1024,128]{1,0:T(8,128)(2,1)S(1)} %get-tuple-element.46), channel_id=1, source_target_pairs={{0,2},{1,3},{2,0},{3,1},{4,6},{5,7},{6,4},{7,5},{8,10},{9,11},{10,... | collective-permute-start | bytes 786440 | tf_op jit(solution)/shard_map/ppermute | solution.py:24
  12.1 13.8 %collective-permute-start.3 = (bf16[1024,128]{1,0:T(8,128)(2,1)S(1)}, bf16[1024,128]{1,0:T(8,128)(2,1)}, u32[]{:S(2)}, u32[]{:S(2)}) collective-permute-start(bf16[1024,128]{1,0:T(8,128)(2,1)S(1)} %get-tuple-element.46), channel_id=1, source_target_pairs={{0,3},{1,0},{2,1},{3,2},{4,7},{5,4},{6,5},{7,6},{8,11},{9,8},{10,9... | collective-permute-start | bytes 786440 | tf_op jit(solution)/shard_map/ppermute | solution.py:24
  12.7 14.2 %collective-permute-start.2 = (bf16[1024,128]{1,0:T(8,128)(2,1)S(1)}, bf16[1024,128]{1,0:T(8,128)(2,1)}, u32[]{:S(2)}, u32[]{:S(2)}) collective-permute-start(bf16[1024,128]{1,0:T(8,128)(2,1)S(1)} %get-tuple-element.46), channel_id=1, source_target_pairs={{0,1},{1,2},{2,3},{3,0},{4,5},{5,6},{6,7},{7,4},{8,9},{9,10},{10,1... | collective-permute-start | bytes 786440 | tf_op jit(solution)/shard_map/ppermute | solution.py:24
  26.9 32.0 %collective-permute-start.6 = (bf16[3072,128]{1,0:T(8,128)(2,1)S(1)}, bf16[3072,128]{1,0:T(8,128)(2,1)S(1)}, u32[]{:S(2)}, u32[]{:S(2)}) collective-permute-start(bf16[3072,128]{1,0:T(8,128)(2,1)S(1)} %collective-permute-done), channel_id=1, source_target_pairs={{0,48},{1,49},{2,50},{3,51},{4,52},{5,53},{6,54},{7,55},{8,56},{9,... | collective-permute-start | bytes 2359304 | tf_op jit(solution)/shard_map/ppermute | solution.py:24
  42.5 19.5 %collective-permute-start.5 = (bf16[3072,128]{1,0:T(8,128)(2,1)S(1)}, bf16[3072,128]{1,0:T(8,128)(2,1)S(1)}, u32[]{:S(2)}, u32[]{:S(2)}) collective-permute-start(bf16[3072,128]{1,0:T(8,128)(2,1)S(1)} %collective-permute-done), channel_id=1, source_target_pairs={{0,16},{1,17},{2,18},{3,19},{4,20},{5,21},{6,22},{7,23},{8,24},{9,... | collective-permute-start | bytes 2359304 | tf_op jit(solution)/shard_map/ppermute | solution.py:24
  42.6 21.5 %copy-start.4 = (bf16[2,1024,128]{2,1,0:T(8,128)(2,1)}, bf16[2,1024,128]{2,1,0:T(8,128)(2,1)S(1)}, u32[]{:S(2)}) copy-start(bf16[2,1024,128]{2,1,0:T(8,128)(2,1)S(1)} %pad_maximum_fusion.5.near_ref) | copy-start | bytes 1572868
  42.6 12.8 %collective-permute-start.8 = (bf16[2,1024,128]{2,1,0:T(8,128)(2,1)S(1)}, bf16[2,1024,128]{2,1,0:T(8,128)(2,1)S(1)}, u32[]{:S(2)}, u32[]{:S(2)}) collective-permute-start(bf16[2,1024,128]{2,1,0:T(8,128)(2,1)S(1)} %pad_maximum_fusion.5.near_ref), channel_id=1, source_target_pairs={{0,3},{1,0},{2,1},{3,2},{4,7},{5,4},{6,5},{7,6},{8,11},{9,8},{10,9... | collective-permute-start | bytes 1572872 | tf_op jit(solution)/shard_map/ppermute | solution.py:24
  43.8 14.5 %collective-permute-start.7 = (bf16[2,1024,128]{2,1,0:T(8,128)(2,1)S(1)}, bf16[2,1024,128]{2,1,0:T(8,128)(2,1)S(1)}, u32[]{:S(2)}, u32[]{:S(2)}) collective-permute-start(bf16[2,1024,128]{2,1,0:T(8,128)(2,1)S(1)} %pad_maximum_fusion.5.near_ref), channel_id=1, source_target_pairs={{0,1},{1,2},{2,3},{3,0},{4,5},{5,6},{6,7},{7,4},{8,9},{9,10},{10,1... | collective-permute-start | bytes 1572872 | tf_op jit(solution)/shard_map/ppermute | solution.py:24
  45.3 20.6 %copy-start.3 = (bf16[4,1024,128]{2,1,0:T(8,128)(2,1)}, bf16[4,1024,128]{2,1,0:T(8,128)(2,1)S(1)}, u32[]{:S(2)}) copy-start(bf16[4,1024,128]{2,1,0:T(8,128)(2,1)S(1)} %pad_maximum_fusion.1.below_mine_ref) | copy-start | bytes 3145732
  45.3 26.9 %collective-permute-start.13 = (bf16[4,1024,128]{2,1,0:T(8,128)(2,1)S(1)}, bf16[4,1024,128]{2,1,0:T(8,128)(2,1)S(1)}, u32[]{:S(2)}, u32[]{:S(2)}) collective-permute-start(bf16[4,1024,128]{2,1,0:T(8,128)(2,1)S(1)} %pad_maximum_fusion.1.below_mine_ref), channel_id=1, source_target_pairs={{0,4},{1,5},{2,6},{3,7},{4,0},{5,1},{6,2},{7,3},{8,12},{9,13},{10,... | collective-permute-start | bytes 3145736 | tf_op jit(solution)/shard_map/ppermute | solution.py:24
  55.4 6.7 %copy-start.5 = (bf16[2,1024,128]{2,1,0:T(8,128)(2,1)}, bf16[2,1024,128]{2,1,0:T(8,128)(2,1)S(1)}, u32[]{:S(2)}) copy-start(bf16[2,1024,128]{2,1,0:T(8,128)(2,1)S(1)} %collective-permute-done.8.ahead_ref) | copy-start | bytes 1572868
  58.2 5.9 %copy-start.6 = (bf16[2,1024,128]{2,1,0:T(8,128)(2,1)}, bf16[2,1024,128]{2,1,0:T(8,128)(2,1)S(1)}, u32[]{:S(2)}) copy-start(bf16[2,1024,128]{2,1,0:T(8,128)(2,1)S(1)} %collective-permute-done.7.behind_ref) | copy-start | bytes 1572868
  62.0 6.9 %collective-permute-start.10 = (bf16[1024,128]{1,0:T(8,128)(2,1)S(1)}, bf16[1024,128]{1,0:T(8,128)(2,1)S(1)}, u32[]{:S(2)}, u32[]{:S(2)}) collective-permute-start(bf16[1024,128]{1,0:T(8,128)(2,1)S(1)} %slice_bitcast_fusion.7), channel_id=1, source_target_pairs={{0,3},{1,0},{2,1},{3,2},{4,7},{5,4},{6,5},{7,6},{8,11},{9,8},{10,9... | collective-permute-start | bytes 786440 | tf_op jit(solution)/shard_map/ppermute | solution.py:24
  64.1 8.0 %collective-permute-start.9 = (bf16[1024,128]{1,0:T(8,128)(2,1)S(1)}, bf16[1024,128]{1,0:T(8,128)(2,1)S(1)}, u32[]{:S(2)}, u32[]{:S(2)}) collective-permute-start(bf16[1024,128]{1,0:T(8,128)(2,1)S(1)} %slice_bitcast_fusion.8), channel_id=1, source_target_pairs={{0,1},{1,2},{2,3},{3,0},{4,5},{5,6},{6,7},{7,4},{8,9},{9,10},{10,1... | collective-permute-start | bytes 786440 | tf_op jit(solution)/shard_map/ppermute | solution.py:24
  64.3 9.0 %collective-permute-start.12 = (bf16[1536,128]{1,0:T(8,128)(2,1)S(1)}, bf16[1536,128]{1,0:T(8,128)(2,1)S(1)}, u32[]{:S(2)}, u32[]{:S(2)}) collective-permute-start(bf16[1536,128]{1,0:T(8,128)(2,1)S(1)} %slice.55), channel_id=1, source_target_pairs={{0,48},{1,49},{2,50},{3,51},{4,52},{5,53},{6,54},{7,55},{8,56},{9,... | collective-permute-start | bytes 1179656 | tf_op jit(solution)/shard_map/ppermute | solution.py:24
  64.6 10.1 %collective-permute-start.11 = (bf16[1536,128]{1,0:T(8,128)(2,1)S(1)}, bf16[1536,128]{1,0:T(8,128)(2,1)S(1)}, u32[]{:S(2)}, u32[]{:S(2)}) collective-permute-start(bf16[1536,128]{1,0:T(8,128)(2,1)S(1)} %slice.54), channel_id=1, source_target_pairs={{0,16},{1,17},{2,18},{3,19},{4,20},{5,21},{6,22},{7,23},{8,24},{9,... | collective-permute-start | bytes 1179656 | tf_op jit(solution)/shard_map/ppermute | solution.py:24
  69.0 6.0 %copy-start.9 = (bf16[1024,128]{1,0:T(8,128)(2,1)}, bf16[1024,128]{1,0:T(8,128)(2,1)S(1)}, u32[]{:S(2)}) copy-start(bf16[1024,128]{1,0:T(8,128)(2,1)S(1)} %collective-permute-done.10.far_second_ref) | copy-start | bytes 786436
  72.2 2.5 %copy-start.10 = (bf16[1024,128]{1,0:T(8,128)(2,1)}, bf16[1024,128]{1,0:T(8,128)(2,1)S(1)}, u32[]{:S(2)}) copy-start(bf16[1024,128]{1,0:T(8,128)(2,1)S(1)} %collective-permute-done.9.far_first_ref) | copy-start | bytes 786436
  72.2 2.5 %copy-start.8 = (bf16[4,1024,128]{2,1,0:T(8,128)(2,1)}, bf16[4,1024,128]{2,1,0:T(8,128)(2,1)S(1)}, u32[]{:S(2)}) copy-start(bf16[4,1024,128]{2,1,0:T(8,128)(2,1)S(1)} %collective-permute-done.13.below_other_ref) | copy-start | bytes 3145732
  75.0 3.0 %copy-start = (bf16[4,2048,128]{2,1,0:T(8,128)(2,1)}, bf16[4,2048,128]{2,1,0:T(8,128)(2,1)S(1)}, u32[]{:S(2)}) copy-start(bf16[4,2048,128]{2,1,0:T(8,128)(2,1)S(1)} %pad_maximum_fusion.mine_ref.inverse_mine_ref) | copy-start | bytes 6291460
  75.0 6.7 %collective-permute-start.14 = (bf16[4,2048,128]{2,1,0:T(8,128)(2,1)S(1)}, bf16[4,2048,128]{2,1,0:T(8,128)(2,1)}, u32[]{:S(2)}, u32[]{:S(2)}) collective-permute-start(bf16[4,2048,128]{2,1,0:T(8,128)(2,1)S(1)} %pad_maximum_fusion.mine_ref.inverse_mine_ref), channel_id=1, source_target_pairs={{0,8},{1,9},{2,10},{3,11},{4,12},{5,13},{6,14},{7,15},{8,0},{9,1},... | collective-permute-start | bytes 6291464 | tf_op jit(solution)/shard_map/ppermute | solution.py:24
  78.0 17.4 %copy-start.1 = (bf16[4,1024,128]{2,1,0:T(8,128)(2,1)}, bf16[4,1024,128]{2,1,0:T(8,128)(2,1)S(1)}, u32[]{:S(2)}) copy-start(bf16[4,1024,128]{2,1,0:T(8,128)(2,1)S(1)} %pad_maximum_fusion.2.mine_ref) | copy-start | bytes 3145732
  78.0 27.0 %collective-permute-start.15 = (bf16[4,1024,128]{2,1,0:T(8,128)(2,1)S(1)}, bf16[4,1024,128]{2,1,0:T(8,128)(2,1)}, u32[]{:S(2)}, u32[]{:S(2)}) collective-permute-start(bf16[4,1024,128]{2,1,0:T(8,128)(2,1)S(1)} %pad_maximum_fusion.2.mine_ref), channel_id=1, source_target_pairs={{0,8},{1,9},{2,10},{3,11},{4,12},{5,13},{6,14},{7,15},{8,0},{9,1},... | collective-permute-start | bytes 3145736 | tf_op jit(solution)/shard_map/ppermute | solution.py:24
  105.0 60.2 %all-to-all-start.1 = ((bf16[128,128,128]{2,1,0:T(8,128)(2,1)}), bf16[128,128,128]{2,1,0:T(8,128)(2,1)}, u32[]{:S(2)}, u32[]{:S(2)}) async-start(bf16[128,128,128]{2,1,0:T(8,128)(2,1)} %bitcast.65), calls=%async_computation.1 | async-start | bytes 8388608 | tf_op jit(solution)/shard_map/all_to_all | solution.py:340
  165.2 6.5 %copy-start.7 = (s32[2,16384]{1,0:T(2,128)S(1)}, s32[2,16384]{1,0:T(2,128)}, u32[]{:S(2)}) copy-start(s32[2,16384]{1,0:T(2,128)} %param.8) | copy-start | bytes 393220
  165.2 58.9 %all-to-all-start = ((bf16[128,128,128]{2,1,0:T(8,128)(2,1)}), bf16[128,128,128]{2,1,0:T(8,128)(2,1)}, u32[]{:S(2)}, u32[]{:S(2)}) async-start(bf16[128,128,128]{2,1,0:T(8,128)(2,1)} %bitcast.64), calls=%async_computation | async-start | bytes 8388608 | tf_op jit(solution)/shard_map/all_to_all | solution.py:340

commit v7 on v6

--- a/solution.py
+++ b/solution.py
@@ -44,6 +44,17 @@
             ROWS_AXIS,
             preferred_element_type=F32,
         ).astype(BF16)
+
+
+def subtract_product(left_ref, right, front_refs, out_ref):
+    product = lax.dot_general(left_ref[...], right, ROWS_AXIS, preferred_element_type=F32)
+    for which, front_ref in enumerate(front_refs):
+        lanes = slice(which * 128, (which + 1) * 128)
+        for k in range(16):
+            rows = slice(k * 128, (k + 1) * 128)
+            out_ref[k, which] = (
+                front_ref[rows, :].astype(F32) - product[rows, lanes]
+            ).astype(BF16)
 
 
 def first_kernel(
@@ -59,10 +70,14 @@
     other_ref,
     inverse_mine_ref,
     inverse_other_ref,
+    front_even_ref,
+    front_odd_ref,
+    out_ref,
+    left_out_ref,
+    inverse_ref,
+    wide_ref,
     right_ref,
     left_ref,
-    inverse_ref,
-    wide_ref,
 ):
     step = pl.program_id(0)
     y, z = place_ref[4], place_ref[3] // 4
@@ -80,14 +95,23 @@
                 wide_ref[:, spans(side * 4 + (y + away) % 4)] = ref[side]
         wide_ref[:, spans((y + 2) % 4)] = far_first_ref[...]
         wide_ref[:, spans(4 + (y + 2) % 4)] = far_second_ref[...]
-        inverse_product(wide_ref, inverse_ref, left_ref)
+        inverse_product(wide_ref, inverse_ref, left_out_ref)
+        left_ref[:1024, :] = left_out_ref[...]
 
     @pl.when(step == 2)
     def _():
         for ref, side in ((below_mine_ref, z), (below_other_ref, 1 - z)):
             for index, away in enumerate((0, 3, 1, 2)):
                 wide_ref[:, spans(side * 4 + (y + away) % 4)] = ref[index]
-        inverse_product(wide_ref, inverse_ref, left_ref)
+        inverse_product(wide_ref, inverse_ref, left_out_ref)
+        left_ref[1024:, :] = left_out_ref[...]
+
+    @pl.when(step > 2)
+    def _():
+        at = pl.multiple_of((step - 3) * 256, 256)
+        subtract_product(
+            left_ref, right_ref[pl.ds(at, 256), :], (front_even_ref, front_odd_ref), out_ref
+        )
 
 
 FOUR_PANELS = pl.BlockSpec((4, 1024, 128), lambda i, s: (0, 0, 0))
@@ -95,35 +119,50 @@
 SQUARE = (1024, 1024)
 
 
-def lower_first(place, rows, mine, other):
+def schur_first(place, rows, mine, other, front):
     def part(i):
-        return jnp.maximum(i - 1, 0)
+        return jnp.clip(i - 1, 0, 1)
+
+    def late(i):
+        return jnp.maximum(i - 3, 0)
 
     pair = pl.BlockSpec((2, 1024, 128), lambda i, s: (0, 0, 0))
     single = pl.BlockSpec((1024, 128), lambda i, s: (0, 0))
     grid_spec = pltpu.PrefetchScalarGridSpec(
         num_scalar_prefetch=1,
-        grid=(3,),
-        in_specs=[pair] * 3 + [single] * 2 + [FOUR_PANELS] * 4 + [FOUR_INVERSES] * 2,
+        grid=(7,),
+        in_specs=[pair] * 3
+        + [single] * 2
+        + [FOUR_PANELS] * 4
+        + [FOUR_INVERSES] * 2
+        + [
+            pl.BlockSpec((2048, 128), lambda i, s: (0, 4 * late(i))),
+            pl.BlockSpec((2048, 128), lambda i, s: (0, 4 * late(i) + 2)),
+        ],
         out_specs=[
-            pl.BlockSpec(SQUARE, lambda i, s: (0, 0)),
+            pl.BlockSpec((16, 2, 128, 128), lambda i, s: (0, late(i), 0, 0)),
             pl.BlockSpec(SQUARE, lambda i, s: (part(i), 0)),
         ],
-        scratch_shapes=[pltpu.VMEM(SQUARE, BF16), pltpu.VMEM(SQUARE, BF16)],
+        scratch_shapes=[
+            pltpu.VMEM(SQUARE, BF16),
+            pltpu.VMEM(SQUARE, BF16),
+            pltpu.VMEM(SQUARE, BF16),
+            pltpu.VMEM((2048, 1024), BF16),
+        ],
     )
     return pl.pallas_call(
         first_kernel,
         grid_spec=grid_spec,
         out_shape=[
-            jax.ShapeDtypeStruct(SQUARE, BF16),
+            jax.ShapeDtypeStruct((16, 8, 128, 128), BF16),
             jax.ShapeDtypeStruct((2048, 1024), BF16),
         ],
         compiler_params=pltpu.CompilerParams(vmem_limit_bytes=VMEM_LIMIT),
         cost_estimate=pl.CostEstimate(
-            flops=4 << 30, bytes_accessed=14 << 20, transcendentals=0
+            flops=8 << 30, bytes_accessed=20 << 20, transcendentals=0
         ),
-        name="lower_first",
-    )(place, *rows, mine, other, mine, other)
+        name="schur_first",
+    )(place, *rows, mine, other, mine, other, front, front)
 
 
 def right_kernel(
@@ -162,27 +201,18 @@
 
 
 def schur_kernel(left_ref, right_ref, front_even_ref, front_odd_ref, out_ref):
-    product = lax.dot_general(
-        left_ref[...], right_ref[...], ROWS_AXIS, preferred_element_type=F32
-    )
-    for which, front_ref in enumerate((front_even_ref, front_odd_ref)):
-        lanes = slice(which * 128, (which + 1) * 128)
-        for k in range(16):
-            rows = slice(k * 128, (k + 1) * 128)
-            out_ref[k, which] = (
-                front_ref[rows, :].astype(F32) - product[rows, lanes]
-            ).astype(BF16)
-
-
-def schur_parcels(b, left, right, front):
+    subtract_product(left_ref, right_ref[...], (front_even_ref, front_odd_ref), out_ref)
+
+
+def schur_second(left, right, front):
     return pl.pallas_call(
         schur_kernel,
         grid=(4,),
         in_specs=[
             pl.BlockSpec((2048, 1024), lambda i: (0, 0)),
             pl.BlockSpec((256, 1024), lambda i: (i, 0)),
-            pl.BlockSpec((2048, 128), lambda i: (0, 4 * i + b)),
-            pl.BlockSpec((2048, 128), lambda i: (0, 4 * i + 2 + b)),
+            pl.BlockSpec((2048, 128), lambda i: (0, 4 * i + 1)),
+            pl.BlockSpec((2048, 128), lambda i: (0, 4 * i + 3)),
         ],
         out_specs=pl.BlockSpec((16, 2, 128, 128), lambda i: (0, i, 0, 0)),
         out_shape=jax.ShapeDtypeStruct((16, 8, 128, 128), BF16),
@@ -190,51 +220,65 @@
         cost_estimate=pl.CostEstimate(
             flops=4 << 30, bytes_accessed=14 << 20, transcendentals=0
         ),
-        name="schur",
+        name="schur_second",
     )(left, right, front, front)
+
+
+OUT_ROWS = 512
 
 
 def place_kernel(
     b, place_ref, schur_in_ref, row_map_ref, col_map_ref, base_ref, *refs
 ):
-    out_ref, schur_ref = refs[-2:]
-    child = pl.program_id(0)
-    for r in range(8):
-        for c in range(8):
-            schur_ref[r * 128 : (r + 1) * 128, c * 128 : (c + 1) * 128] = schur_in_ref[
-                r * 8 + c
-            ]
-    row_ids = lax.broadcasted_iota(jnp.int32, (1024, 1024), 0)
-    col_ids = lax.broadcasted_iota(jnp.int32, (1024, 1024), 1)
-    row_pick = jnp.where(row_map_ref[0] == row_ids, 1.0, 0.0).astype(BF16)
-    col_pick = jnp.where(col_map_ref[0, 0] == col_ids, 1.0, 0.0).astype(BF16)
-    rowed = jnp.dot(row_pick, schur_ref[...], preferred_element_type=F32).astype(BF16)
-    placed = jnp.dot(rowed, col_pick, preferred_element_type=F32)
-
-    @pl.when(child == 0)
-    def _():
-        out_ref[...] = base_ref[...].astype(F32) + placed
-
-    @pl.when(child == 1)
-    def _():
+    out_ref, schur_ref, columns_ref = refs[-3:]
+    step = pl.program_id(0)
+
+    @pl.when(step < 2)
+    def _():
+        for r in range(8):
+            for c in range(8):
+                schur_ref[r * 128 : (r + 1) * 128, c * 128 : (c + 1) * 128] = schur_in_ref[
+                    r * 8 + c
+                ]
+        ids = lax.broadcasted_iota(jnp.int32, SQUARE, 1)
+        pick = jnp.where(col_map_ref[0, 0] == ids, 1.0, 0.0).astype(BF16)
+        columns_ref[pl.ds(pl.multiple_of(step * 1024, 1024), 1024), :] = jnp.dot(
+            schur_ref[...], pick, preferred_element_type=F32
+        ).astype(BF16)
+
+    @pl.when(step >= 2)
+    def _():
+        first = (step - 2) * OUT_ROWS
+        shape = (OUT_ROWS, 1024)
+        row_ids = lax.broadcasted_iota(jnp.int32, shape, 0) + first
+        total = base_ref[...].astype(F32)
+        for child in range(2):
+            pick = jnp.where(row_map_ref[child] == row_ids, 1.0, 0.0).astype(BF16)
+            total += jnp.dot(
+                pick,
+                columns_ref[child * 1024 : (child + 1) * 1024, :],
+                preferred_element_type=F32,
+            )
         rows = row_ids + place_ref[2] * 1024
-        cols = col_ids + (place_ref[3] * 2048 + b * 1024)
-        out_ref[...] = jnp.where(rows >= cols, out_ref[...] + placed, 0.0)
+        cols = lax.broadcasted_iota(jnp.int32, shape, 1) + (
+            place_ref[3] * 2048 + b * 1024
+        )
+        out_ref[...] = jnp.where(rows >= cols, total, 0.0)
 
 
 def place_children(b, place, arrived, row_maps, col_maps, base, half_done=None):
     grid_spec = pltpu.PrefetchScalarGridSpec(
         num_scalar_prefetch=1,
-        grid=(2,),
+        grid=(4,),
         in_specs=[
-            pl.BlockSpec((64, 128, 128), lambda c, s: (c, 0, 0)),
-            pl.BlockSpec((1, 1, 1024), lambda c, s: (c, 0, 0)),
-            pl.BlockSpec((1, 1, 1024, 1), lambda c, s: (c, b, 0, 0)),
-            pl.BlockSpec((1024, 1024), lambda c, s: (0, b)),
+            pl.BlockSpec((64, 128, 128), lambda i, s: (jnp.minimum(i, 1), 0, 0)),
+            pl.BlockSpec((2, 1, 1024), lambda i, s: (0, 0, 0)),
+            pl.BlockSpec((1, 1, 1024, 1), lambda i, s: (jnp.minimum(i, 1), b, 0, 0)),
+            pl.BlockSpec((OUT_ROWS, 1024), lambda i, s: (jnp.maximum(i - 2, 0), b)),
         ]
         + ([] if half_done is None else [pl.BlockSpec(memory_space=pl.ANY)]),
-        out_specs=pl.BlockSpec((1024, 1024), lambda c, s: (0, b)),
-        scratch_shapes=[pltpu.VMEM((1024, 1024), BF16)],
+        out_specs=pl.BlockSpec((OUT_ROWS, 1024), lambda i, s: (jnp.maximum(i - 2, 0), b)),
+        scratch_shapes=[pltpu.VMEM(SQUARE, BF16), pltpu.VMEM((2048, 1024), BF16)],
     )
     return pl.pallas_call(
         functools.partial(place_kernel, b),
@@ -325,7 +369,7 @@
     other = swap_core(mine)
     odd_other = swap_core(odd_mine)
     rows = (pair, behind, ahead, far_first, far_second, below_mine, below_other)
-    right_even, left = lower_first(place, rows, mine, other)
+    parcels, left = schur_first(place, rows, mine, other, front[0])
 
     maps = child_maps.reshape(2, 8, 16, 128)
     row_maps = (
@@ -342,11 +386,10 @@
     def placed(b, arrived, done=None):
         return place_children(b, place, arrived, row_maps, col_maps, root_front, done)
 
-    parcels = schur_parcels(0, left, right_even, front[0])
     parcels, odd_mine, odd_other = lax.optimization_barrier((parcels, odd_mine, odd_other))
     arrived = exchange(parcels)
     right_odd = lower_right(place, odd_mine, odd_other, mine, other)
-    arrived_odd = exchange(schur_parcels(1, left, right_odd, front[0]))
+    arrived_odd = exchange(schur_second(left, right_odd, front[0]))
     return placed(1, arrived_odd, placed(0, arrived))
 
 

time: 240 us -> 235 us (0.979)
  Pallas kernels: 70.9 us -> 64.2 us
    pallas_call x3 -> x2, Pallas kernels: 33.1 us -> 29.4 us  [the longest x1 19.7 us: schur_first(): pl.pallas_call(first_kernel, grid_spec=grid_spec, out_shape=[jax.ShapeDty...]
    pallas_call x2, Pallas kernels: 30.7 us -> 27.7 us  [place_children(): pl.pallas_call(functools.partial(place_kernel, b), grid_spec=grid_spec, o...]
  transfers between devices with their start and end apart: 18 -> 18, of which waited for: 14 -> 14; matrix products, arithmetic and copies ran while one was open for 3% -> 3% of each run, Pallas kernels for 23% -> 21%
where the time goes in v7:
time: 235 us; the launch traced here: 234 us
  waiting for transfers between devices  109 us (46%)
  Pallas kernels  64.2 us (27%)
  starting transfers between devices  51.9 us (22%)
  local copies, waits for them, and re-layouts  5.42 us (2%)
  other arithmetic  3.37 us (1%)
    all_to_all x2, waiting for transfers between devices, exchange(): return lax.all_to_all(parcels.reshape(128, 128, 128), ALL, 0, 0, tiled=True)  70.1 us
    ppermute x16, waiting for transfers between devices, shift(): return lax.ppermute(array, ALL, pairs)  39 us
    ppermute x16, starting transfers between devices, shift(): return lax.ppermute(array, ALL, pairs)  37.6 us
    pallas_call x2, Pallas kernels, place_children(): pl.pallas_call(functools.partial(place_kernel, b), grid_spec=grid_spec, o...  27.7 us
    pallas_call x1, Pallas kernels, schur_first(): pl.pallas_call(first_kernel, grid_spec=grid_spec, out_shape=[jax.ShapeDty...  19.7 us
    all_to_all x2, starting transfers between devices, exchange(): return lax.all_to_all(parcels.reshape(128, 128, 128), ALL, 0, 0, tiled=True)  14.3 us
    pallas_call x1, Pallas kernels, schur_second(): pl.pallas_call(schur_kernel, grid=(4,), in_specs=[pl.BlockSpec((2048, 102...  9.69 us
    pallas_call x1, Pallas kernels, lower_right(): pl.pallas_call(right_kernel, grid_spec=grid_spec, out_shape=jax.ShapeDtyp...  7.09 us
  transfers between devices with their start and end apart: 18, of which 14 were waited for; matrix products, arithmetic and copies ran while one was open for 3% of the time, Pallas kernels for 21%

profile of v7, /device:TPU:1, one launch (start us, length us, event | category | flops | bytes accessed | tf_op | source)
XLA Modules:
  0.0 234.2 jit_solution(14923110872482556051)
XLA Ops:
  0.0 1.1 fusion.3
  1.1 1.0 pad_maximum_fusion.3
  2.1 4.6 %collective-permute-start = (bf16[3072,128]{1,0:T(8,128)(2,1)S(1)}, bf16[3072,128]{1,0:T(8,128)(2,1)S(1)}, u32[]{:S(2)}, u32[]{:S(2)}) collective-permute-start(bf16[3072,128]{1,0:T(8,128)(2,1)S(1)} %pad_maximum_fusion.3), channel_id=1, source_target_pairs={{0,0},{1,8},{2,16},{3,24},{4,32},{5,40},{6,48},{7,56},{8,1},{9,9},... | collective-permute-start | bytes 2359304 | tf_op jit(solution)/shard_map/ppermute | solution.py:24
  6.8 0.1 fusion.2
  6.8 3.7 %collective-permute-start.1 = (bf16[1024,128]{1,0:T(8,128)(2,1)S(1)}, bf16[1024,128]{1,0:T(8,128)(2,1)S(1)}, u32[]{:S(2)}, u32[]{:S(2)}) collective-permute-start(bf16[1024,128]{1,0:T(8,128)(2,1)S(1)} %get-tuple-element.47), channel_id=1, source_target_pairs={{0,4},{1,5},{2,6},{3,7},{4,0},{5,1},{6,2},{7,3},{8,12},{9,13},{10,... | collective-permute-start | bytes 786440 | tf_op jit(solution)/shard_map/ppermute | solution.py:24
  10.6 1.5 collective-permute-start.4
  12.1 0.6 collective-permute-start.3
  12.7 0.9 collective-permute-start.2
  13.6 3.4 %collective-permute-done.1 = bf16[1024,128]{1,0:T(8,128)(2,1)S(1)} collective-permute-done((bf16[1024,128]{1,0:T(8,128)(2,1)S(1)}, bf16[1024,128]{1,0:T(8,128)(2,1)S(1)}, u32[]{:S(2)}, u32[]{:S(2)}) %collective-permute-start.1) | collective-permute-done | bytes 262176 | tf_op jit(solution)/shard_map/ppermute | solution.py:24
  17.0 8.9 %collective-permute-done.4 = bf16[1024,128]{1,0:T(8,128)(2,1)S(1)} collective-permute-done((bf16[1024,128]{1,0:T(8,128)(2,1)S(1)}, bf16[1024,128]{1,0:T(8,128)(2,1)S(1)}, u32[]{:S(2)}, u32[]{:S(2)}) %collective-permute-start.4) | collective-permute-done | bytes 262176 | tf_op jit(solution)/shard_map/ppermute | solution.py:24
  25.9 1.1 collective-permute-done.2
  26.9 15.5 %collective-permute-start.6 = (bf16[3072,128]{1,0:T(8,128)(2,1)S(1)}, bf16[3072,128]{1,0:T(8,128)(2,1)S(1)}, u32[]{:S(2)}, u32[]{:S(2)}) collective-permute-start(bf16[3072,128]{1,0:T(8,128)(2,1)S(1)} %collective-permute-done), channel_id=1, source_target_pairs={{0,48},{1,49},{2,50},{3,51},{4,52},{5,53},{6,54},{7,55},{8,56},{9,... | collective-permute-start | bytes 2359304 | tf_op jit(solution)/shard_map/ppermute | solution.py:24
  42.5 0.1 pad_maximum_fusion.5.near_ref
  42.6 1.2 collective-permute-start.8
  43.8 0.4 collective-permute-start.7
  44.1 1.2 pad_maximum_fusion.1.below_mine_ref
  45.3 1.8 collective-permute-start.13
  47.1 8.2 %collective-permute-done.8.ahead_ref = bf16[2,1024,128]{2,1,0:T(8,128)(2,1)S(1)} collective-permute-done((bf16[2,1024,128]{2,1,0:T(8,128)(2,1)S(1)}, bf16[2,1024,128]{2,1,0:T(8,128)(2,1)S(1)}, u32[]{:S(2)}, u32[]{:S(2)}) %collective-permute-start.8) | collective-permute-done | bytes 524320 | tf_op jit(solution)/shard_map/ppermute | solution.py:24
  55.4 2.9 %collective-permute-done.7.behind_ref = bf16[2,1024,128]{2,1,0:T(8,128)(2,1)S(1)} collective-permute-done((bf16[2,1024,128]{2,1,0:T(8,128)(2,1)S(1)}, bf16[2,1024,128]{2,1,0:T(8,128)(2,1)S(1)}, u32[]{:S(2)}, u32[]{:S(2)}) %collective-permute-start.7) | collective-permute-done | bytes 524320 | tf_op jit(solution)/shard_map/ppermute | solution.py:24
  58.2 0.7 collective-permute-done.6
  58.9 3.1 %collective-permute-done.5 = bf16[3072,128]{1,0:T(8,128)(2,1)S(1)} collective-permute-done((bf16[3072,128]{1,0:T(8,128)(2,1)S(1)}, bf16[3072,128]{1,0:T(8,128)(2,1)S(1)}, u32[]{:S(2)}, u32[]{:S(2)}) %collective-permute-start.5) | collective-permute-done | bytes 786464 | tf_op jit(solution)/shard_map/ppermute | solution.py:24
  62.0 2.1 collective-permute-start.10
  64.1 0.1 collective-permute-start.9
  64.3 0.3 collective-permute-start.12
  64.6 1.3 collective-permute-start.11
  65.8 0.1 slice_bitcast_fusion
  65.9 3.1 %collective-permute-done.10.far_second_ref = bf16[1024,128]{1,0:T(8,128)(2,1)S(1)} collective-permute-done((bf16[1024,128]{1,0:T(8,128)(2,1)S(1)}, bf16[1024,128]{1,0:T(8,128)(2,1)S(1)}, u32[]{:S(2)}, u32[]{:S(2)}) %collective-permute-start.10) | collective-permute-done | bytes 262176 | tf_op jit(solution)/shard_map/ppermute | solution.py:24
  69.0 3.2 %collective-permute-done.9.far_first_ref = bf16[1024,128]{1,0:T(8,128)(2,1)S(1)} collective-permute-done((bf16[1024,128]{1,0:T(8,128)(2,1)S(1)}, bf16[1024,128]{1,0:T(8,128)(2,1)S(1)}, u32[]{:S(2)}, u32[]{:S(2)}) %collective-permute-start.9) | collective-permute-done | bytes 262176 | tf_op jit(solution)/shard_map/ppermute | solution.py:24
  72.2 1.1 collective-permute-done.12
  73.3 1.3 collective-permute-done.11
  74.7 0.3 pad_maximum_fusion.mine_ref.inverse_mine_ref
  75.0 2.7 %collective-permute-start.14 = (bf16[4,2048,128]{2,1,0:T(8,128)(2,1)S(1)}, bf16[4,2048,128]{2,1,0:T(8,128)(2,1)}, u32[]{:S(2)}, u32[]{:S(2)}) collective-permute-start(bf16[4,2048,128]{2,1,0:T(8,128)(2,1)S(1)} %pad_maximum_fusion.mine_ref.inverse_mine_ref), channel_id=1, source_target_pairs={{0,8},{1,9},{2,10},{3,11},{4,12},{5,13},{6,14},{7,15},{8,0},{9,1},... | collective-permute-start | bytes 6291464 | tf_op jit(solution)/shard_map/ppermute | solution.py:24
  77.8 0.1 pad_maximum_fusion.2.mine_ref
  78.0 1.0 collective-permute-start.15
  79.0 0.6 stack.74.place_ref
  79.6 2.0 collective-permute-done.14.other_ref.inverse_other_ref
  81.7 19.7 %schur_first.1 = (bf16[16,8,128,128]{3,2,1,0:T(8,128)(2,1)}, bf16[2048,1024]{1,0:T(8,128)(2,1)}) custom-call(s32[5]{0:T(128)} %stack.74.place_ref, bf16[2,1024,128]{2,1,0:T(8,128)(2,1)} %copy-done.4, bf16[2,1024,128]{2,1,0:T(8,128)(2,1)} %copy-done.6, bf16[2,1024,128]{2,1,0:T(8,128)(2,1)} %copy-done.5, bf16[1024,128]{1,0:T(8,128)(2,1)} %copy-done.10, ...), custom_call_target="tpu_custom_call" | custom-call | flops 8589934592 | bytes 20971520 | tf_op jit(solution)/shard_map/schur_first/pallas_call | solution.py:153
  101.3 7.8 %all-to-all-start.1 = ((bf16[128,128,128]{2,1,0:T(8,128)(2,1)}), bf16[128,128,128]{2,1,0:T(8,128)(2,1)}, u32[]{:S(2)}, u32[]{:S(2)}) async-start(bf16[128,128,128]{2,1,0:T(8,128)(2,1)} %bitcast.65), calls=%async_computation.1 | async-start | bytes 8388608 | tf_op jit(solution)/shard_map/all_to_all | solution.py:384
  109.1 7.1 %lower_right.1.right_ref = bf16[1024,1024]{1,0:T(8,128)(2,1)} custom-call(s32[5]{0:T(128)} %stack.74.place_ref, bf16[4,1024,128]{2,1,0:T(8,128)(2,1)} %copy-done.1, bf16[4,1024,128]{2,1,0:T(8,128)(2,1)} %collective-permute-done.15.other_ref, bf16[4,2048,128]{2,1,0:T(8,128)(2,1)} %copy-done, ...), custom_call_target="tpu_custom_call" | custom-call | flops 1610612736 | bytes 6291456 | tf_op jit(solution)/shard_map/lower_right/pallas_call | solution.py:191
  116.2 9.7 %schur_second.1 = bf16[16,8,128,128]{3,2,1,0:T(8,128)(2,1)} custom-call(bf16[2048,1024]{1,0:T(8,128)(2,1)} %get-tuple-element.38.left_ref, bf16[1024,1024]{1,0:T(8,128)(2,1)} %lower_right.1.right_ref, bf16[2048,2048]{1,0:T(8,128)(2,1)} %bitcast.62, bf16[2048,2048]{1,0:T(8,128)(2,1)} %bitcast.63), custom_call_target="tpu_custom_call" | custom-call | flops 4294967296 | bytes 14680064 | tf_op jit(solution)/shard_map/schur_second/pallas_call | solution.py:208
  125.9 35.6 %all-to-all-done.1.schur_in_ref = bf16[128,128,128]{2,1,0:T(8,128)(2,1)} async-done(((bf16[128,128,128]{2,1,0:T(8,128)(2,1)}), bf16[128,128,128]{2,1,0:T(8,128)(2,1)}, u32[]{:S(2)}, u32[]{:S(2)}) %all-to-all-start.1) | async-done | bytes 4194336 | tf_op jit(solution)/shard_map/all_to_all | solution.py:384
  161.5 6.5 %all-to-all-start = ((bf16[128,128,128]{2,1,0:T(8,128)(2,1)}), bf16[128,128,128]{2,1,0:T(8,128)(2,1)}, u32[]{:S(2)}, u32[]{:S(2)}) async-start(bf16[128,128,128]{2,1,0:T(8,128)(2,1)} %bitcast.64), calls=%async_computation | async-start | bytes 8388608 | tf_op jit(solution)/shard_map/all_to_all | solution.py:384
  168.1 0.1 fusion.1
  168.2 3.3 %reshape.38.col_map_ref = s32[2,2,1024,1]{3,2,1,0:T(8,128)} reshape(s32[2,2,8,128]{3,2,1,0:T(8,128)S(1)} %fusion.1) | data formatting | bytes 32768 | tf_op jit(solution)/shard_map/reshape | solution.py:381
  171.4 0.6 broadcast_subtract_fusion
  172.0 13.8 %place.2.refs_0_ = f32[1024,2048]{1,0:T(8,128)} custom-call(s32[5]{0:T(128)} %stack.74.place_ref, bf16[128,128,128]{2,1,0:T(8,128)(2,1)} %all-to-all-done.1.schur_in_ref, s32[2,1,1024]{2,1,0:T(1,128)} %bitcast.75, s32[2,2,1024,1]{3,2,1,0:T(8,128)} %reshape.38.col_map_ref, bf16[1024,2048]{1,0:T(8,128)(2,1)} %base_ref.3), custom_call_target="tpu_custom_call" | custom-call | flops 8589934592 | bytes 10485760 | tf_op jit(solution)/shard_map/place/pallas_call | solution.py:283
  185.9 34.5 %all-to-all-done.schur_in_ref = bf16[128,128,128]{2,1,0:T(8,128)(2,1)} async-done(((bf16[128,128,128]{2,1,0:T(8,128)(2,1)}), bf16[128,128,128]{2,1,0:T(8,128)(2,1)}, u32[]{:S(2)}, u32[]{:S(2)}) %all-to-all-start) | async-done | bytes 4194336 | tf_op jit(solution)/shard_map/all_to_all | solution.py:384
  220.4 13.9 %place.3 = f32[1024,2048]{1,0:T(8,128)} custom-call(s32[5]{0:T(128)} %stack.74.place_ref, bf16[128,128,128]{2,1,0:T(8,128)(2,1)} %all-to-all-done.schur_in_ref, s32[2,1,1024]{2,1,0:T(1,128)} %bitcast.76, s32[2,2,1024,1]{3,2,1,0:T(8,128)} %reshape.38.col_map_ref, bf16[1024,2048]{1,0:T(8,128)(2,1)} %base_ref.3, ...), custom_call_target="tpu_custom_call", output_to_operand_aliasing={{}: (5, {})} | custom-call | flops 8589934592 | bytes 10485760 | tf_op jit(solution)/shard_map/place/pallas_call | solution.py:283
  (41 shorter events, 0.4 us)
Async XLA Ops:
  0.0 6.7 %copy-start.2 = (bf16[1,2048,128]{2,1,0:T(8,128)(2,1)S(1)}, bf16[1,2048,128]{2,1,0:T(8,128)(2,1)}, u32[]{:S(2)}) copy-start(bf16[1,2048,128]{2,1,0:T(8,128)(2,1)} %param.6) | copy-start | bytes 1572868
  2.1 24.8 %collective-permute-start = (bf16[3072,128]{1,0:T(8,128)(2,1)S(1)}, bf16[3072,128]{1,0:T(8,128)(2,1)S(1)}, u32[]{:S(2)}, u32[]{:S(2)}) collective-permute-start(bf16[3072,128]{1,0:T(8,128)(2,1)S(1)} %pad_maximum_fusion.3), channel_id=1, source_target_pairs={{0,0},{1,8},{2,16},{3,24},{4,32},{5,40},{6,48},{7,56},{8,1},{9,9},... | collective-permute-start | bytes 2359304 | tf_op jit(solution)/shard_map/ppermute | solution.py:24
  6.8 10.2 %collective-permute-start.1 = (bf16[1024,128]{1,0:T(8,128)(2,1)S(1)}, bf16[1024,128]{1,0:T(8,128)(2,1)S(1)}, u32[]{:S(2)}, u32[]{:S(2)}) collective-permute-start(bf16[1024,128]{1,0:T(8,128)(2,1)S(1)} %get-tuple-element.47), channel_id=1, source_target_pairs={{0,4},{1,5},{2,6},{3,7},{4,0},{5,1},{6,2},{7,3},{8,12},{9,13},{10,... | collective-permute-start | bytes 786440 | tf_op jit(solution)/shard_map/ppermute | solution.py:24
  10.6 15.3 %collective-permute-start.4 = (bf16[1024,128]{1,0:T(8,128)(2,1)S(1)}, bf16[1024,128]{1,0:T(8,128)(2,1)S(1)}, u32[]{:S(2)}, u32[]{:S(2)}) collective-permute-start(bf16[1024,128]{1,0:T(8,128)(2,1)S(1)} %get-tuple-element.46), channel_id=1, source_target_pairs={{0,2},{1,3},{2,0},{3,1},{4,6},{5,7},{6,4},{7,5},{8,10},{9,11},{10,... | collective-permute-start | bytes 786440 | tf_op jit(solution)/shard_map/ppermute | solution.py:24
  12.1 13.8 %collective-permute-start.3 = (bf16[1024,128]{1,0:T(8,128)(2,1)S(1)}, bf16[1024,128]{1,0:T(8,128)(2,1)}, u32[]{:S(2)}, u32[]{:S(2)}) collective-permute-start(bf16[1024,128]{1,0:T(8,128)(2,1)S(1)} %get-tuple-element.46), channel_id=1, source_target_pairs={{0,3},{1,0},{2,1},{3,2},{4,7},{5,4},{6,5},{7,6},{8,11},{9,8},{10,9... | collective-permute-start | bytes 786440 | tf_op jit(solution)/shard_map/ppermute | solution.py:24
  12.7 14.2 %collective-permute-start.2 = (bf16[1024,128]{1,0:T(8,128)(2,1)S(1)}, bf16[1024,128]{1,0:T(8,128)(2,1)}, u32[]{:S(2)}, u32[]{:S(2)}) collective-permute-start(bf16[1024,128]{1,0:T(8,128)(2,1)S(1)} %get-tuple-element.46), channel_id=1, source_target_pairs={{0,1},{1,2},{2,3},{3,0},{4,5},{5,6},{6,7},{7,4},{8,9},{9,10},{10,1... | collective-permute-start | bytes 786440 | tf_op jit(solution)/shard_map/ppermute | solution.py:24
  26.9 32.0 %collective-permute-start.6 = (bf16[3072,128]{1,0:T(8,128)(2,1)S(1)}, bf16[3072,128]{1,0:T(8,128)(2,1)S(1)}, u32[]{:S(2)}, u32[]{:S(2)}) collective-permute-start(bf16[3072,128]{1,0:T(8,128)(2,1)S(1)} %collective-permute-done), channel_id=1, source_target_pairs={{0,48},{1,49},{2,50},{3,51},{4,52},{5,53},{6,54},{7,55},{8,56},{9,... | collective-permute-start | bytes 2359304 | tf_op jit(solution)/shard_map/ppermute | solution.py:24
  42.5 19.5 %collective-permute-start.5 = (bf16[3072,128]{1,0:T(8,128)(2,1)S(1)}, bf16[3072,128]{1,0:T(8,128)(2,1)S(1)}, u32[]{:S(2)}, u32[]{:S(2)}) collective-permute-start(bf16[3072,128]{1,0:T(8,128)(2,1)S(1)} %collective-permute-done), channel_id=1, source_target_pairs={{0,16},{1,17},{2,18},{3,19},{4,20},{5,21},{6,22},{7,23},{8,24},{9,... | collective-permute-start | bytes 2359304 | tf_op jit(solution)/shard_map/ppermute | solution.py:24
  42.6 21.5 %copy-start.4 = (bf16[2,1024,128]{2,1,0:T(8,128)(2,1)}, bf16[2,1024,128]{2,1,0:T(8,128)(2,1)S(1)}, u32[]{:S(2)}) copy-start(bf16[2,1024,128]{2,1,0:T(8,128)(2,1)S(1)} %pad_maximum_fusion.5.near_ref) | copy-start | bytes 1572868
  42.6 12.8 %collective-permute-start.8 = (bf16[2,1024,128]{2,1,0:T(8,128)(2,1)S(1)}, bf16[2,1024,128]{2,1,0:T(8,128)(2,1)S(1)}, u32[]{:S(2)}, u32[]{:S(2)}) collective-permute-start(bf16[2,1024,128]{2,1,0:T(8,128)(2,1)S(1)} %pad_maximum_fusion.5.near_ref), channel_id=1, source_target_pairs={{0,3},{1,0},{2,1},{3,2},{4,7},{5,4},{6,5},{7,6},{8,11},{9,8},{10,9... | collective-permute-start | bytes 1572872 | tf_op jit(solution)/shard_map/ppermute | solution.py:24
  43.8 14.5 %collective-permute-start.7 = (bf16[2,1024,128]{2,1,0:T(8,128)(2,1)S(1)}, bf16[2,1024,128]{2,1,0:T(8,128)(2,1)S(1)}, u32[]{:S(2)}, u32[]{:S(2)}) collective-permute-start(bf16[2,1024,128]{2,1,0:T(8,128)(2,1)S(1)} %pad_maximum_fusion.5.near_ref), channel_id=1, source_target_pairs={{0,1},{1,2},{2,3},{3,0},{4,5},{5,6},{6,7},{7,4},{8,9},{9,10},{10,1... | collective-permute-start | bytes 1572872 | tf_op jit(solution)/shard_map/ppermute | solution.py:24
  45.3 20.6 %copy-start.3 = (bf16[4,1024,128]{2,1,0:T(8,128)(2,1)}, bf16[4,1024,128]{2,1,0:T(8,128)(2,1)S(1)}, u32[]{:S(2)}) copy-start(bf16[4,1024,128]{2,1,0:T(8,128)(2,1)S(1)} %pad_maximum_fusion.1.below_mine_ref) | copy-start | bytes 3145732
  45.3 26.9 %collective-permute-start.13 = (bf16[4,1024,128]{2,1,0:T(8,128)(2,1)S(1)}, bf16[4,1024,128]{2,1,0:T(8,128)(2,1)S(1)}, u32[]{:S(2)}, u32[]{:S(2)}) collective-permute-start(bf16[4,1024,128]{2,1,0:T(8,128)(2,1)S(1)} %pad_maximum_fusion.1.below_mine_ref), channel_id=1, source_target_pairs={{0,4},{1,5},{2,6},{3,7},{4,0},{5,1},{6,2},{7,3},{8,12},{9,13},{10,... | collective-permute-start | bytes 3145736 | tf_op jit(solution)/shard_map/ppermute | solution.py:24
  55.4 6.7 %copy-start.5 = (bf16[2,1024,128]{2,1,0:T(8,128)(2,1)}, bf16[2,1024,128]{2,1,0:T(8,128)(2,1)S(1)}, u32[]{:S(2)}) copy-start(bf16[2,1024,128]{2,1,0:T(8,128)(2,1)S(1)} %collective-permute-done.8.ahead_ref) | copy-start | bytes 1572868
  58.2 5.9 %copy-start.6 = (bf16[2,1024,128]{2,1,0:T(8,128)(2,1)}, bf16[2,1024,128]{2,1,0:T(8,128)(2,1)S(1)}, u32[]{:S(2)}) copy-start(bf16[2,1024,128]{2,1,0:T(8,128)(2,1)S(1)} %collective-permute-done.7.behind_ref) | copy-start | bytes 1572868
  62.0 6.9 %collective-permute-start.10 = (bf16[1024,128]{1,0:T(8,128)(2,1)S(1)}, bf16[1024,128]{1,0:T(8,128)(2,1)S(1)}, u32[]{:S(2)}, u32[]{:S(2)}) collective-permute-start(bf16[1024,128]{1,0:T(8,128)(2,1)S(1)} %slice_bitcast_fusion.7), channel_id=1, source_target_pairs={{0,3},{1,0},{2,1},{3,2},{4,7},{5,4},{6,5},{7,6},{8,11},{9,8},{10,9... | collective-permute-start | bytes 786440 | tf_op jit(solution)/shard_map/ppermute | solution.py:24
  64.1 8.0 %collective-permute-start.9 = (bf16[1024,128]{1,0:T(8,128)(2,1)S(1)}, bf16[1024,128]{1,0:T(8,128)(2,1)S(1)}, u32[]{:S(2)}, u32[]{:S(2)}) collective-permute-start(bf16[1024,128]{1,0:T(8,128)(2,1)S(1)} %slice_bitcast_fusion.8), channel_id=1, source_target_pairs={{0,1},{1,2},{2,3},{3,0},{4,5},{5,6},{6,7},{7,4},{8,9},{9,10},{10,1... | collective-permute-start | bytes 786440 | tf_op jit(solution)/shard_map/ppermute | solution.py:24
  64.3 9.0 %collective-permute-start.12 = (bf16[1536,128]{1,0:T(8,128)(2,1)S(1)}, bf16[1536,128]{1,0:T(8,128)(2,1)S(1)}, u32[]{:S(2)}, u32[]{:S(2)}) collective-permute-start(bf16[1536,128]{1,0:T(8,128)(2,1)S(1)} %slice.55), channel_id=1, source_target_pairs={{0,48},{1,49},{2,50},{3,51},{4,52},{5,53},{6,54},{7,55},{8,56},{9,... | collective-permute-start | bytes 1179656 | tf_op jit(solution)/shard_map/ppermute | solution.py:24
  64.6 10.1 %collective-permute-start.11 = (bf16[1536,128]{1,0:T(8,128)(2,1)S(1)}, bf16[1536,128]{1,0:T(8,128)(2,1)S(1)}, u32[]{:S(2)}, u32[]{:S(2)}) collective-permute-start(bf16[1536,128]{1,0:T(8,128)(2,1)S(1)} %slice.54), channel_id=1, source_target_pairs={{0,16},{1,17},{2,18},{3,19},{4,20},{5,21},{6,22},{7,23},{8,24},{9,... | collective-permute-start | bytes 1179656 | tf_op jit(solution)/shard_map/ppermute | solution.py:24
  69.0 6.0 %copy-start.9 = (bf16[1024,128]{1,0:T(8,128)(2,1)}, bf16[1024,128]{1,0:T(8,128)(2,1)S(1)}, u32[]{:S(2)}) copy-start(bf16[1024,128]{1,0:T(8,128)(2,1)S(1)} %collective-permute-done.10.far_second_ref) | copy-start | bytes 786436
  72.2 2.5 %copy-start.10 = (bf16[1024,128]{1,0:T(8,128)(2,1)}, bf16[1024,128]{1,0:T(8,128)(2,1)S(1)}, u32[]{:S(2)}) copy-start(bf16[1024,128]{1,0:T(8,128)(2,1)S(1)} %collective-permute-done.9.far_first_ref) | copy-start | bytes 786436
  72.2 2.5 %copy-start.8 = (bf16[4,1024,128]{2,1,0:T(8,128)(2,1)}, bf16[4,1024,128]{2,1,0:T(8,128)(2,1)S(1)}, u32[]{:S(2)}) copy-start(bf16[4,1024,128]{2,1,0:T(8,128)(2,1)S(1)} %collective-permute-done.13.below_other_ref) | copy-start | bytes 3145732
  75.0 3.0 %copy-start = (bf16[4,2048,128]{2,1,0:T(8,128)(2,1)}, bf16[4,2048,128]{2,1,0:T(8,128)(2,1)S(1)}, u32[]{:S(2)}) copy-start(bf16[4,2048,128]{2,1,0:T(8,128)(2,1)S(1)} %pad_maximum_fusion.mine_ref.inverse_mine_ref) | copy-start | bytes 6291460
  75.0 6.7 %collective-permute-start.14 = (bf16[4,2048,128]{2,1,0:T(8,128)(2,1)S(1)}, bf16[4,2048,128]{2,1,0:T(8,128)(2,1)}, u32[]{:S(2)}, u32[]{:S(2)}) collective-permute-start(bf16[4,2048,128]{2,1,0:T(8,128)(2,1)S(1)} %pad_maximum_fusion.mine_ref.inverse_mine_ref), channel_id=1, source_target_pairs={{0,8},{1,9},{2,10},{3,11},{4,12},{5,13},{6,14},{7,15},{8,0},{9,1},... | collective-permute-start | bytes 6291464 | tf_op jit(solution)/shard_map/ppermute | solution.py:24
  78.0 23.4 %copy-start.1 = (bf16[4,1024,128]{2,1,0:T(8,128)(2,1)}, bf16[4,1024,128]{2,1,0:T(8,128)(2,1)S(1)}, u32[]{:S(2)}) copy-start(bf16[4,1024,128]{2,1,0:T(8,128)(2,1)S(1)} %pad_maximum_fusion.2.mine_ref) | copy-start | bytes 3145732
  78.0 23.4 %collective-permute-start.15 = (bf16[4,1024,128]{2,1,0:T(8,128)(2,1)S(1)}, bf16[4,1024,128]{2,1,0:T(8,128)(2,1)}, u32[]{:S(2)}, u32[]{:S(2)}) collective-permute-start(bf16[4,1024,128]{2,1,0:T(8,128)(2,1)S(1)} %pad_maximum_fusion.2.mine_ref), channel_id=1, source_target_pairs={{0,8},{1,9},{2,10},{3,11},{4,12},{5,13},{6,14},{7,15},{8,0},{9,1},... | collective-permute-start | bytes 3145736 | tf_op jit(solution)/shard_map/ppermute | solution.py:24
  101.3 60.2 %all-to-all-start.1 = ((bf16[128,128,128]{2,1,0:T(8,128)(2,1)}), bf16[128,128,128]{2,1,0:T(8,128)(2,1)}, u32[]{:S(2)}, u32[]{:S(2)}) async-start(bf16[128,128,128]{2,1,0:T(8,128)(2,1)} %bitcast.65), calls=%async_computation.1 | async-start | bytes 8388608 | tf_op jit(solution)/shard_map/all_to_all | solution.py:384
  161.5 6.5 %copy-start.7 = (s32[2,16384]{1,0:T(2,128)S(1)}, s32[2,16384]{1,0:T(2,128)}, u32[]{:S(2)}) copy-start(s32[2,16384]{1,0:T(2,128)} %param.8) | copy-start | bytes 393220
  161.5 58.9 %all-to-all-start = ((bf16[128,128,128]{2,1,0:T(8,128)(2,1)}), bf16[128,128,128]{2,1,0:T(8,128)(2,1)}, u32[]{:S(2)}, u32[]{:S(2)}) async-start(bf16[128,128,128]{2,1,0:T(8,128)(2,1)} %bitcast.64), calls=%async_computation | async-start | bytes 8388608 | tf_op jit(solution)/shard_map/all_to_all | solution.py:384

commit v8 on v7

--- a/solution.py
+++ b/solution.py
@@ -32,7 +32,8 @@
     turn, core = place_ref[0], place_ref[1]
     for ref, part in ((mine_ref, core), (other_ref, 1 - core)):
         for index, away in enumerate((0, 3, 1, 2)):
-            out_ref[:, spans((turn + away) % 4 * 2 + part)] = ref[index]
+            place = (turn + away) % 4
+            out_ref[:, spans(place // 2 * 4 + part * 2 + place % 2)] = ref[index]
 
 
 def inverse_product(wide_ref, inverse_ref, out_ref):
@@ -309,7 +310,9 @@
     place = jnp.stack([(x + 4 - col // 2) % 4, core, target, col, col % 4]).astype(jnp.int32)
 
     def spread(array):
-        return shift(array, lambda h, r, c: (h, (c // 2 + r // 2) % 4 * 2 + c % 2, r))
+        return shift(
+            array, lambda h, r, c: (h, (c // 4 * 2 + c % 2 + r // 2) % 4 * 2 + c % 4 // 2, r)
+        )
 
     def ahead_x(array):
         return shift(array, lambda h, r, c: (h, (r + 2) % 8, c))

time: 235 us -> 227 us (0.966)
  starting transfers between devices: 51.9 us -> 36.5 us
  waiting for transfers between devices: 109 us -> 117 us
    ppermute x16, starting transfers between devices: 37.6 us -> 23.9 us  [shift(): return lax.ppermute(array, ALL, pairs)]
    ppermute x16, waiting for transfers between devices: 39 us -> 46.8 us  [shift(): return lax.ppermute(array, ALL, pairs)]
  transfers between devices with their start and end apart: 18 -> 18, of which waited for: 14 -> 14; matrix products, arithmetic and copies ran while one was open for 3% -> 3% of each run, Pallas kernels for 21% -> 22%
where the time goes in v8:
time: 227 us
  waiting for transfers between devices  117 us (52%)
  Pallas kernels  64.2 us (28%)
  starting transfers between devices  36.5 us (16%)
  local copies, waits for them, and re-layouts  5.42 us (2%)
  other arithmetic  3.37 us (1%)
    all_to_all x2, waiting for transfers between devices, exchange(): return lax.all_to_all(parcels.reshape(128, 128, 128), ALL, 0, 0, tiled=True)  70.1 us
    ppermute x16, waiting for transfers between devices, shift(): return lax.ppermute(array, ALL, pairs)  46.8 us
    pallas_call x2, Pallas kernels, place_children(): pl.pallas_call(functools.partial(place_kernel, b), grid_spec=grid_spec, o...  27.7 us
    ppermute x16, starting transfers between devices, shift(): return lax.ppermute(array, ALL, pairs)  23.9 us
    pallas_call x1, Pallas kernels, schur_first(): pl.pallas_call(first_kernel, grid_spec=grid_spec, out_shape=[jax.ShapeDty...  19.7 us
    all_to_all x2, starting transfers between devices, exchange(): return lax.all_to_all(parcels.reshape(128, 128, 128), ALL, 0, 0, tiled=True)  12.6 us
    pallas_call x1, Pallas kernels, schur_second(): pl.pallas_call(schur_kernel, grid=(4,), in_specs=[pl.BlockSpec((2048, 102...  9.68 us
    pallas_call x1, Pallas kernels, lower_right(): pl.pallas_call(right_kernel, grid_spec=grid_spec, out_shape=jax.ShapeDtyp...  7.13 us
  transfers between devices with their start and end apart: 18, of which 14 were waited for; matrix products, arithmetic and copies ran while one was open for 3% of the time, Pallas kernels for 22%

profile of v8, /device:TPU:1, one launch (start us, length us, event | category | flops | bytes accessed | tf_op | source)
XLA Modules:
  0.0 226.7 jit_solution(13043365894551822332)
XLA Ops:
  0.0 1.1 fusion.3
  1.1 1.0 pad_maximum_fusion.3
  2.1 4.6 %collective-permute-start = (bf16[3072,128]{1,0:T(8,128)(2,1)S(1)}, bf16[3072,128]{1,0:T(8,128)(2,1)S(1)}, u32[]{:S(2)}, u32[]{:S(2)}) collective-permute-start(bf16[3072,128]{1,0:T(8,128)(2,1)S(1)} %pad_maximum_fusion.3), channel_id=1, source_target_pairs={{0,0},{1,16},{2,8},{3,24},{4,32},{5,48},{6,40},{7,56},{8,1},{9,17}... | collective-permute-start | bytes 2359304 | tf_op jit(solution)/shard_map/ppermute | solution.py:24
  6.8 0.1 fusion.2
  6.8 3.7 %collective-permute-start.1 = (bf16[1024,128]{1,0:T(8,128)(2,1)S(1)}, bf16[1024,128]{1,0:T(8,128)(2,1)S(1)}, u32[]{:S(2)}, u32[]{:S(2)}) collective-permute-start(bf16[1024,128]{1,0:T(8,128)(2,1)S(1)} %get-tuple-element.47), channel_id=1, source_target_pairs={{0,4},{1,5},{2,6},{3,7},{4,0},{5,1},{6,2},{7,3},{8,12},{9,13},{10,... | collective-permute-start | bytes 786440 | tf_op jit(solution)/shard_map/ppermute | solution.py:24
  10.6 1.2 collective-permute-start.4
  11.8 1.2 collective-permute-start.3
  13.0 0.3 collective-permute-start.2
  13.3 3.4 %collective-permute-done.1 = bf16[1024,128]{1,0:T(8,128)(2,1)S(1)} collective-permute-done((bf16[1024,128]{1,0:T(8,128)(2,1)S(1)}, bf16[1024,128]{1,0:T(8,128)(2,1)S(1)}, u32[]{:S(2)}, u32[]{:S(2)}) %collective-permute-start.1) | collective-permute-done | bytes 262176 | tf_op jit(solution)/shard_map/ppermute | solution.py:24
  16.7 6.9 %collective-permute-done.4 = bf16[1024,128]{1,0:T(8,128)(2,1)S(1)} collective-permute-done((bf16[1024,128]{1,0:T(8,128)(2,1)S(1)}, bf16[1024,128]{1,0:T(8,128)(2,1)S(1)}, u32[]{:S(2)}, u32[]{:S(2)}) %collective-permute-start.4) | collective-permute-done | bytes 262176 | tf_op jit(solution)/shard_map/ppermute | solution.py:24
  23.6 9.8 %collective-permute-done.3 = bf16[1024,128]{1,0:T(8,128)(2,1)} collective-permute-done((bf16[1024,128]{1,0:T(8,128)(2,1)S(1)}, bf16[1024,128]{1,0:T(8,128)(2,1)}, u32[]{:S(2)}, u32[]{:S(2)}) %collective-permute-start.3) | collective-permute-done | bytes 262176 | tf_op jit(solution)/shard_map/ppermute | solution.py:24
  33.4 3.5 %collective-permute-start.6 = (bf16[3072,128]{1,0:T(8,128)(2,1)S(1)}, bf16[3072,128]{1,0:T(8,128)(2,1)S(1)}, u32[]{:S(2)}, u32[]{:S(2)}) collective-permute-start(bf16[3072,128]{1,0:T(8,128)(2,1)S(1)} %collective-permute-done), channel_id=1, source_target_pairs={{0,48},{1,49},{2,50},{3,51},{4,52},{5,53},{6,54},{7,55},{8,56},{9,... | collective-permute-start | bytes 2359304 | tf_op jit(solution)/shard_map/ppermute | solution.py:24
  37.0 0.1 pad_maximum_fusion.5.near_ref
  37.1 0.4 collective-permute-start.8
  37.4 1.2 collective-permute-start.7
  38.6 1.2 pad_maximum_fusion.1.below_mine_ref
  39.8 0.5 collective-permute-start.13
  40.3 9.5 %collective-permute-done.8.ahead_ref = bf16[2,1024,128]{2,1,0:T(8,128)(2,1)S(1)} collective-permute-done((bf16[2,1024,128]{2,1,0:T(8,128)(2,1)S(1)}, bf16[2,1024,128]{2,1,0:T(8,128)(2,1)S(1)}, u32[]{:S(2)}, u32[]{:S(2)}) %collective-permute-start.8) | collective-permute-done | bytes 524320 | tf_op jit(solution)/shard_map/ppermute | solution.py:24
  49.8 0.9 collective-permute-done.7.behind_ref
  50.7 2.7 %collective-permute-done.6 = bf16[3072,128]{1,0:T(8,128)(2,1)S(1)} collective-permute-done((bf16[3072,128]{1,0:T(8,128)(2,1)S(1)}, bf16[3072,128]{1,0:T(8,128)(2,1)S(1)}, u32[]{:S(2)}, u32[]{:S(2)}) %collective-permute-start.6) | collective-permute-done | bytes 786464 | tf_op jit(solution)/shard_map/ppermute | solution.py:24
  53.4 3.1 %collective-permute-done.5 = bf16[3072,128]{1,0:T(8,128)(2,1)S(1)} collective-permute-done((bf16[3072,128]{1,0:T(8,128)(2,1)S(1)}, bf16[3072,128]{1,0:T(8,128)(2,1)S(1)}, u32[]{:S(2)}, u32[]{:S(2)}) %collective-permute-start.5) | collective-permute-done | bytes 786464 | tf_op jit(solution)/shard_map/ppermute | solution.py:24
  56.5 0.1 collective-permute-start.10
  56.6 1.5 collective-permute-start.9
  58.2 0.4 collective-permute-start.12
  58.6 1.1 collective-permute-start.11
  59.7 0.1 slice_bitcast_fusion
  59.8 2.9 %collective-permute-done.10.far_second_ref = bf16[1024,128]{1,0:T(8,128)(2,1)S(1)} collective-permute-done((bf16[1024,128]{1,0:T(8,128)(2,1)S(1)}, bf16[1024,128]{1,0:T(8,128)(2,1)S(1)}, u32[]{:S(2)}, u32[]{:S(2)}) %collective-permute-start.10) | collective-permute-done | bytes 262176 | tf_op jit(solution)/shard_map/ppermute | solution.py:24
  62.7 1.3 collective-permute-done.9.far_first_ref
  64.0 2.6 %collective-permute-done.12 = bf16[1536,128]{1,0:T(8,128)(2,1)S(1)} collective-permute-done((bf16[1536,128]{1,0:T(8,128)(2,1)S(1)}, bf16[1536,128]{1,0:T(8,128)(2,1)S(1)}, u32[]{:S(2)}, u32[]{:S(2)}) %collective-permute-start.12) | collective-permute-done | bytes 393248 | tf_op jit(solution)/shard_map/ppermute | solution.py:24
  66.7 1.6 collective-permute-done.11
  68.3 0.3 pad_maximum_fusion.mine_ref.inverse_mine_ref
  68.6 3.2 %collective-permute-start.14 = (bf16[4,2048,128]{2,1,0:T(8,128)(2,1)S(1)}, bf16[4,2048,128]{2,1,0:T(8,128)(2,1)}, u32[]{:S(2)}, u32[]{:S(2)}) collective-permute-start(bf16[4,2048,128]{2,1,0:T(8,128)(2,1)S(1)} %pad_maximum_fusion.mine_ref.inverse_mine_ref), channel_id=1, source_target_pairs={{0,8},{1,9},{2,10},{3,11},{4,12},{5,13},{6,14},{7,15},{8,0},{9,1},... | collective-permute-start | bytes 6291464 | tf_op jit(solution)/shard_map/ppermute | solution.py:24
  71.9 0.1 pad_maximum_fusion.2.mine_ref
  72.0 1.0 collective-permute-start.15
  73.1 0.6 stack.74.place_ref
  73.6 2.0 collective-permute-done.14.other_ref.inverse_other_ref
  75.7 19.7 %schur_first.1 = (bf16[16,8,128,128]{3,2,1,0:T(8,128)(2,1)}, bf16[2048,1024]{1,0:T(8,128)(2,1)}) custom-call(s32[5]{0:T(128)} %stack.74.place_ref, bf16[2,1024,128]{2,1,0:T(8,128)(2,1)} %copy-done.4, bf16[2,1024,128]{2,1,0:T(8,128)(2,1)} %copy-done.6, bf16[2,1024,128]{2,1,0:T(8,128)(2,1)} %copy-done.5, bf16[1024,128]{1,0:T(8,128)(2,1)} %copy-done.10, ...), custom_call_target="tpu_custom_call" | custom-call | flops 8589934592 | bytes 20971520 | tf_op jit(solution)/shard_map/schur_first/pallas_call | solution.py:154
  95.4 6.2 %all-to-all-start.1 = ((bf16[128,128,128]{2,1,0:T(8,128)(2,1)}), bf16[128,128,128]{2,1,0:T(8,128)(2,1)}, u32[]{:S(2)}, u32[]{:S(2)}) async-start(bf16[128,128,128]{2,1,0:T(8,128)(2,1)} %bitcast.65), calls=%async_computation.1 | async-start | bytes 8388608 | tf_op jit(solution)/shard_map/all_to_all | solution.py:387
  101.6 7.1 %lower_right.1.right_ref = bf16[1024,1024]{1,0:T(8,128)(2,1)} custom-call(s32[5]{0:T(128)} %stack.74.place_ref, bf16[4,1024,128]{2,1,0:T(8,128)(2,1)} %copy-done.1, bf16[4,1024,128]{2,1,0:T(8,128)(2,1)} %collective-permute-done.15.other_ref, bf16[4,2048,128]{2,1,0:T(8,128)(2,1)} %copy-done, ...), custom_call_target="tpu_custom_call" | custom-call | flops 1610612736 | bytes 6291456 | tf_op jit(solution)/shard_map/lower_right/pallas_call | solution.py:192
  108.7 9.7 %schur_second.1 = bf16[16,8,128,128]{3,2,1,0:T(8,128)(2,1)} custom-call(bf16[2048,1024]{1,0:T(8,128)(2,1)} %get-tuple-element.38.left_ref, bf16[1024,1024]{1,0:T(8,128)(2,1)} %lower_right.1.right_ref, bf16[2048,2048]{1,0:T(8,128)(2,1)} %bitcast.62, bf16[2048,2048]{1,0:T(8,128)(2,1)} %bitcast.63), custom_call_target="tpu_custom_call" | custom-call | flops 4294967296 | bytes 14680064 | tf_op jit(solution)/shard_map/schur_second/pallas_call | solution.py:209
  118.4 35.6 %all-to-all-done.1.schur_in_ref = bf16[128,128,128]{2,1,0:T(8,128)(2,1)} async-done(((bf16[128,128,128]{2,1,0:T(8,128)(2,1)}), bf16[128,128,128]{2,1,0:T(8,128)(2,1)}, u32[]{:S(2)}, u32[]{:S(2)}) %all-to-all-start.1) | async-done | bytes 4194336 | tf_op jit(solution)/shard_map/all_to_all | solution.py:387
  154.0 6.5 %all-to-all-start = ((bf16[128,128,128]{2,1,0:T(8,128)(2,1)}), bf16[128,128,128]{2,1,0:T(8,128)(2,1)}, u32[]{:S(2)}, u32[]{:S(2)}) async-start(bf16[128,128,128]{2,1,0:T(8,128)(2,1)} %bitcast.64), calls=%async_computation | async-start | bytes 8388608 | tf_op jit(solution)/shard_map/all_to_all | solution.py:387
  160.5 0.1 fusion.1
  160.6 3.3 %reshape.38.col_map_ref = s32[2,2,1024,1]{3,2,1,0:T(8,128)} reshape(s32[2,2,8,128]{3,2,1,0:T(8,128)S(1)} %fusion.1) | data formatting | bytes 32768 | tf_op jit(solution)/shard_map/reshape | solution.py:384
  163.9 0.6 broadcast_subtract_fusion
  164.5 13.8 %place.2.refs_0_ = f32[1024,2048]{1,0:T(8,128)} custom-call(s32[5]{0:T(128)} %stack.74.place_ref, bf16[128,128,128]{2,1,0:T(8,128)(2,1)} %all-to-all-done.1.schur_in_ref, s32[2,1,1024]{2,1,0:T(1,128)} %bitcast.75, s32[2,2,1024,1]{3,2,1,0:T(8,128)} %reshape.38.col_map_ref, bf16[1024,2048]{1,0:T(8,128)(2,1)} %base_ref.3), custom_call_target="tpu_custom_call" | custom-call | flops 8589934592 | bytes 10485760 | tf_op jit(solution)/shard_map/place/pallas_call | solution.py:284
  178.3 34.5 %all-to-all-done.schur_in_ref = bf16[128,128,128]{2,1,0:T(8,128)(2,1)} async-done(((bf16[128,128,128]{2,1,0:T(8,128)(2,1)}), bf16[128,128,128]{2,1,0:T(8,128)(2,1)}, u32[]{:S(2)}, u32[]{:S(2)}) %all-to-all-start) | async-done | bytes 4194336 | tf_op jit(solution)/shard_map/all_to_all | solution.py:387
  212.8 13.9 %place.3 = f32[1024,2048]{1,0:T(8,128)} custom-call(s32[5]{0:T(128)} %stack.74.place_ref, bf16[128,128,128]{2,1,0:T(8,128)(2,1)} %all-to-all-done.schur_in_ref, s32[2,1,1024]{2,1,0:T(1,128)} %bitcast.76, s32[2,2,1024,1]{3,2,1,0:T(8,128)} %reshape.38.col_map_ref, bf16[1024,2048]{1,0:T(8,128)(2,1)} %base_ref.3, ...), custom_call_target="tpu_custom_call", output_to_operand_aliasing={{}: (5, {})} | custom-call | flops 8589934592 | bytes 10485760 | tf_op jit(solution)/shard_map/place/pallas_call | solution.py:284
  (41 shorter events, 0.4 us)
Async XLA Ops:
  0.0 6.7 %copy-start.2 = (bf16[1,2048,128]{2,1,0:T(8,128)(2,1)S(1)}, bf16[1,2048,128]{2,1,0:T(8,128)(2,1)}, u32[]{:S(2)}) copy-start(bf16[1,2048,128]{2,1,0:T(8,128)(2,1)} %param.6) | copy-start | bytes 1572868
  2.1 31.3 %collective-permute-start = (bf16[3072,128]{1,0:T(8,128)(2,1)S(1)}, bf16[3072,128]{1,0:T(8,128)(2,1)S(1)}, u32[]{:S(2)}, u32[]{:S(2)}) collective-permute-start(bf16[3072,128]{1,0:T(8,128)(2,1)S(1)} %pad_maximum_fusion.3), channel_id=1, source_target_pairs={{0,0},{1,16},{2,8},{3,24},{4,32},{5,48},{6,40},{7,56},{8,1},{9,17}... | collective-permute-start | bytes 2359304 | tf_op jit(solution)/shard_map/ppermute | solution.py:24
  6.8 9.9 %collective-permute-start.1 = (bf16[1024,128]{1,0:T(8,128)(2,1)S(1)}, bf16[1024,128]{1,0:T(8,128)(2,1)S(1)}, u32[]{:S(2)}, u32[]{:S(2)}) collective-permute-start(bf16[1024,128]{1,0:T(8,128)(2,1)S(1)} %get-tuple-element.47), channel_id=1, source_target_pairs={{0,4},{1,5},{2,6},{3,7},{4,0},{5,1},{6,2},{7,3},{8,12},{9,13},{10,... | collective-permute-start | bytes 786440 | tf_op jit(solution)/shard_map/ppermute | solution.py:24
  10.6 13.1 %collective-permute-start.4 = (bf16[1024,128]{1,0:T(8,128)(2,1)S(1)}, bf16[1024,128]{1,0:T(8,128)(2,1)S(1)}, u32[]{:S(2)}, u32[]{:S(2)}) collective-permute-start(bf16[1024,128]{1,0:T(8,128)(2,1)S(1)} %get-tuple-element.46), channel_id=1, source_target_pairs={{0,2},{1,3},{2,0},{3,1},{4,6},{5,7},{6,4},{7,5},{8,10},{9,11},{10,... | collective-permute-start | bytes 786440 | tf_op jit(solution)/shard_map/ppermute | solution.py:24
  11.8 21.6 %collective-permute-start.3 = (bf16[1024,128]{1,0:T(8,128)(2,1)S(1)}, bf16[1024,128]{1,0:T(8,128)(2,1)}, u32[]{:S(2)}, u32[]{:S(2)}) collective-permute-start(bf16[1024,128]{1,0:T(8,128)(2,1)S(1)} %get-tuple-element.46), channel_id=1, source_target_pairs={{0,3},{1,0},{2,1},{3,2},{4,7},{5,4},{6,5},{7,6},{8,11},{9,8},{10,9... | collective-permute-start | bytes 786440 | tf_op jit(solution)/shard_map/ppermute | solution.py:24
  13.0 20.5 %collective-permute-start.2 = (bf16[1024,128]{1,0:T(8,128)(2,1)S(1)}, bf16[1024,128]{1,0:T(8,128)(2,1)}, u32[]{:S(2)}, u32[]{:S(2)}) collective-permute-start(bf16[1024,128]{1,0:T(8,128)(2,1)S(1)} %get-tuple-element.46), channel_id=1, source_target_pairs={{0,1},{1,2},{2,3},{3,0},{4,5},{5,6},{6,7},{7,4},{8,9},{9,10},{10,1... | collective-permute-start | bytes 786440 | tf_op jit(solution)/shard_map/ppermute | solution.py:24
  33.4 19.9 %collective-permute-start.6 = (bf16[3072,128]{1,0:T(8,128)(2,1)S(1)}, bf16[3072,128]{1,0:T(8,128)(2,1)S(1)}, u32[]{:S(2)}, u32[]{:S(2)}) collective-permute-start(bf16[3072,128]{1,0:T(8,128)(2,1)S(1)} %collective-permute-done), channel_id=1, source_target_pairs={{0,48},{1,49},{2,50},{3,51},{4,52},{5,53},{6,54},{7,55},{8,56},{9,... | collective-permute-start | bytes 2359304 | tf_op jit(solution)/shard_map/ppermute | solution.py:24
  36.9 19.5 %collective-permute-start.5 = (bf16[3072,128]{1,0:T(8,128)(2,1)S(1)}, bf16[3072,128]{1,0:T(8,128)(2,1)S(1)}, u32[]{:S(2)}, u32[]{:S(2)}) collective-permute-start(bf16[3072,128]{1,0:T(8,128)(2,1)S(1)} %collective-permute-done), channel_id=1, source_target_pairs={{0,16},{1,17},{2,18},{3,19},{4,20},{5,21},{6,22},{7,23},{8,24},{9,... | collective-permute-start | bytes 2359304 | tf_op jit(solution)/shard_map/ppermute | solution.py:24
  37.1 19.5 %copy-start.4 = (bf16[2,1024,128]{2,1,0:T(8,128)(2,1)}, bf16[2,1024,128]{2,1,0:T(8,128)(2,1)S(1)}, u32[]{:S(2)}) copy-start(bf16[2,1024,128]{2,1,0:T(8,128)(2,1)S(1)} %pad_maximum_fusion.5.near_ref) | copy-start | bytes 1572868
  37.1 12.7 %collective-permute-start.8 = (bf16[2,1024,128]{2,1,0:T(8,128)(2,1)S(1)}, bf16[2,1024,128]{2,1,0:T(8,128)(2,1)S(1)}, u32[]{:S(2)}, u32[]{:S(2)}) collective-permute-start(bf16[2,1024,128]{2,1,0:T(8,128)(2,1)S(1)} %pad_maximum_fusion.5.near_ref), channel_id=1, source_target_pairs={{0,3},{1,0},{2,1},{3,2},{4,7},{5,4},{6,5},{7,6},{8,11},{9,8},{10,9... | collective-permute-start | bytes 1572872 | tf_op jit(solution)/shard_map/ppermute | solution.py:24
  37.4 13.3 %collective-permute-start.7 = (bf16[2,1024,128]{2,1,0:T(8,128)(2,1)S(1)}, bf16[2,1024,128]{2,1,0:T(8,128)(2,1)S(1)}, u32[]{:S(2)}, u32[]{:S(2)}) collective-permute-start(bf16[2,1024,128]{2,1,0:T(8,128)(2,1)S(1)} %pad_maximum_fusion.5.near_ref), channel_id=1, source_target_pairs={{0,1},{1,2},{2,3},{3,0},{4,5},{5,6},{6,7},{7,4},{8,9},{9,10},{10,1... | collective-permute-start | bytes 1572872 | tf_op jit(solution)/shard_map/ppermute | solution.py:24
  39.8 20.0 %copy-start.3 = (bf16[4,1024,128]{2,1,0:T(8,128)(2,1)}, bf16[4,1024,128]{2,1,0:T(8,128)(2,1)S(1)}, u32[]{:S(2)}) copy-start(bf16[4,1024,128]{2,1,0:T(8,128)(2,1)S(1)} %pad_maximum_fusion.1.below_mine_ref) | copy-start | bytes 3145732
  39.8 24.3 %collective-permute-start.13 = (bf16[4,1024,128]{2,1,0:T(8,128)(2,1)S(1)}, bf16[4,1024,128]{2,1,0:T(8,128)(2,1)S(1)}, u32[]{:S(2)}, u32[]{:S(2)}) collective-permute-start(bf16[4,1024,128]{2,1,0:T(8,128)(2,1)S(1)} %pad_maximum_fusion.1.below_mine_ref), channel_id=1, source_target_pairs={{0,4},{1,5},{2,6},{3,7},{4,0},{5,1},{6,2},{7,3},{8,12},{9,13},{10,... | collective-permute-start | bytes 3145736 | tf_op jit(solution)/shard_map/ppermute | solution.py:24
  49.8 6.7 %copy-start.5 = (bf16[2,1024,128]{2,1,0:T(8,128)(2,1)}, bf16[2,1024,128]{2,1,0:T(8,128)(2,1)S(1)}, u32[]{:S(2)}) copy-start(bf16[2,1024,128]{2,1,0:T(8,128)(2,1)S(1)} %collective-permute-done.8.ahead_ref) | copy-start | bytes 1572868
  50.7 5.9 %copy-start.6 = (bf16[2,1024,128]{2,1,0:T(8,128)(2,1)}, bf16[2,1024,128]{2,1,0:T(8,128)(2,1)S(1)}, u32[]{:S(2)}) copy-start(bf16[2,1024,128]{2,1,0:T(8,128)(2,1)S(1)} %collective-permute-done.7.behind_ref) | copy-start | bytes 1572868
  56.5 6.2 %collective-permute-start.10 = (bf16[1024,128]{1,0:T(8,128)(2,1)S(1)}, bf16[1024,128]{1,0:T(8,128)(2,1)S(1)}, u32[]{:S(2)}, u32[]{:S(2)}) collective-permute-start(bf16[1024,128]{1,0:T(8,128)(2,1)S(1)} %slice_bitcast_fusion.7), channel_id=1, source_target_pairs={{0,3},{1,0},{2,1},{3,2},{4,7},{5,4},{6,5},{7,6},{8,11},{9,8},{10,9... | collective-permute-start | bytes 786440 | tf_op jit(solution)/shard_map/ppermute | solution.py:24
  56.6 7.4 %collective-permute-start.9 = (bf16[1024,128]{1,0:T(8,128)(2,1)S(1)}, bf16[1024,128]{1,0:T(8,128)(2,1)S(1)}, u32[]{:S(2)}, u32[]{:S(2)}) collective-permute-start(bf16[1024,128]{1,0:T(8,128)(2,1)S(1)} %slice_bitcast_fusion.8), channel_id=1, source_target_pairs={{0,1},{1,2},{2,3},{3,0},{4,5},{5,6},{6,7},{7,4},{8,9},{9,10},{10,1... | collective-permute-start | bytes 786440 | tf_op jit(solution)/shard_map/ppermute | solution.py:24
  58.2 8.5 %collective-permute-start.12 = (bf16[1536,128]{1,0:T(8,128)(2,1)S(1)}, bf16[1536,128]{1,0:T(8,128)(2,1)S(1)}, u32[]{:S(2)}, u32[]{:S(2)}) collective-permute-start(bf16[1536,128]{1,0:T(8,128)(2,1)S(1)} %slice.55), channel_id=1, source_target_pairs={{0,48},{1,49},{2,50},{3,51},{4,52},{5,53},{6,54},{7,55},{8,56},{9,... | collective-permute-start | bytes 1179656 | tf_op jit(solution)/shard_map/ppermute | solution.py:24
  58.6 9.6 %collective-permute-start.11 = (bf16[1536,128]{1,0:T(8,128)(2,1)S(1)}, bf16[1536,128]{1,0:T(8,128)(2,1)S(1)}, u32[]{:S(2)}, u32[]{:S(2)}) collective-permute-start(bf16[1536,128]{1,0:T(8,128)(2,1)S(1)} %slice.54), channel_id=1, source_target_pairs={{0,16},{1,17},{2,18},{3,19},{4,20},{5,21},{6,22},{7,23},{8,24},{9,... | collective-permute-start | bytes 1179656 | tf_op jit(solution)/shard_map/ppermute | solution.py:24
  62.7 5.9 %copy-start.9 = (bf16[1024,128]{1,0:T(8,128)(2,1)}, bf16[1024,128]{1,0:T(8,128)(2,1)S(1)}, u32[]{:S(2)}) copy-start(bf16[1024,128]{1,0:T(8,128)(2,1)S(1)} %collective-permute-done.10.far_second_ref) | copy-start | bytes 786436
  64.0 4.2 %copy-start.10 = (bf16[1024,128]{1,0:T(8,128)(2,1)}, bf16[1024,128]{1,0:T(8,128)(2,1)S(1)}, u32[]{:S(2)}) copy-start(bf16[1024,128]{1,0:T(8,128)(2,1)S(1)} %collective-permute-done.9.far_first_ref) | copy-start | bytes 786436
  64.0 4.2 %copy-start.8 = (bf16[4,1024,128]{2,1,0:T(8,128)(2,1)}, bf16[4,1024,128]{2,1,0:T(8,128)(2,1)S(1)}, u32[]{:S(2)}) copy-start(bf16[4,1024,128]{2,1,0:T(8,128)(2,1)S(1)} %collective-permute-done.13.below_other_ref) | copy-start | bytes 3145732
  68.6 3.4 %copy-start = (bf16[4,2048,128]{2,1,0:T(8,128)(2,1)}, bf16[4,2048,128]{2,1,0:T(8,128)(2,1)S(1)}, u32[]{:S(2)}) copy-start(bf16[4,2048,128]{2,1,0:T(8,128)(2,1)S(1)} %pad_maximum_fusion.mine_ref.inverse_mine_ref) | copy-start | bytes 6291460
  68.6 7.1 %collective-permute-start.14 = (bf16[4,2048,128]{2,1,0:T(8,128)(2,1)S(1)}, bf16[4,2048,128]{2,1,0:T(8,128)(2,1)}, u32[]{:S(2)}, u32[]{:S(2)}) collective-permute-start(bf16[4,2048,128]{2,1,0:T(8,128)(2,1)S(1)} %pad_maximum_fusion.mine_ref.inverse_mine_ref), channel_id=1, source_target_pairs={{0,8},{1,9},{2,10},{3,11},{4,12},{5,13},{6,14},{7,15},{8,0},{9,1},... | collective-permute-start | bytes 6291464 | tf_op jit(solution)/shard_map/ppermute | solution.py:24
  72.0 23.4 %copy-start.1 = (bf16[4,1024,128]{2,1,0:T(8,128)(2,1)}, bf16[4,1024,128]{2,1,0:T(8,128)(2,1)S(1)}, u32[]{:S(2)}) copy-start(bf16[4,1024,128]{2,1,0:T(8,128)(2,1)S(1)} %pad_maximum_fusion.2.mine_ref) | copy-start | bytes 3145732
  72.0 23.4 %collective-permute-start.15 = (bf16[4,1024,128]{2,1,0:T(8,128)(2,1)S(1)}, bf16[4,1024,128]{2,1,0:T(8,128)(2,1)}, u32[]{:S(2)}, u32[]{:S(2)}) collective-permute-start(bf16[4,1024,128]{2,1,0:T(8,128)(2,1)S(1)} %pad_maximum_fusion.2.mine_ref), channel_id=1, source_target_pairs={{0,8},{1,9},{2,10},{3,11},{4,12},{5,13},{6,14},{7,15},{8,0},{9,1},... | collective-permute-start | bytes 3145736 | tf_op jit(solution)/shard_map/ppermute | solution.py:24
  95.4 58.6 %all-to-all-start.1 = ((bf16[128,128,128]{2,1,0:T(8,128)(2,1)}), bf16[128,128,128]{2,1,0:T(8,128)(2,1)}, u32[]{:S(2)}, u32[]{:S(2)}) async-start(bf16[128,128,128]{2,1,0:T(8,128)(2,1)} %bitcast.65), calls=%async_computation.1 | async-start | bytes 8388608 | tf_op jit(solution)/shard_map/all_to_all | solution.py:387
  154.0 6.5 %copy-start.7 = (s32[2,16384]{1,0:T(2,128)S(1)}, s32[2,16384]{1,0:T(2,128)}, u32[]{:S(2)}) copy-start(s32[2,16384]{1,0:T(2,128)} %param.8) | copy-start | bytes 393220
  154.0 58.9 %all-to-all-start = ((bf16[128,128,128]{2,1,0:T(8,128)(2,1)}), bf16[128,128,128]{2,1,0:T(8,128)(2,1)}, u32[]{:S(2)}, u32[]{:S(2)}) async-start(bf16[128,128,128]{2,1,0:T(8,128)(2,1)} %bitcast.64), calls=%async_computation | async-start | bytes 8388608 | tf_op jit(solution)/shard_map/all_to_all | solution.py:387

commit v9 on v8

--- a/solution.py
+++ b/solution.py
@@ -332,7 +332,8 @@
     def swap_core(array):
         return shift(array, lambda h, r, c: (h, r ^ 1, c))
 
-    runs = panel[0].reshape(8, 2, 128, 128)
+    upper, below, whole = lax.optimization_barrier((panel[0, :1024], panel[0, 1024:], panel[0]))
+    runs = whole.reshape(8, 2, 128, 128)
     turned = spread(
         jnp.concatenate(
             [
@@ -342,10 +343,8 @@
             ]
         )
     )
-    upper, below = panel[0, :1024], panel[0, 1024:]
-    turned, twin, below_one, below_three, below_two = lax.optimization_barrier(
+    twin, below_one, below_three, below_two = lax.optimization_barrier(
         (
-            turned,
             swap_z(upper),
             ahead_y(below),
             behind_y(below),
@@ -354,6 +353,7 @@
     )
     pair = jnp.stack([jnp.where(col < 4, upper, twin), jnp.where(col < 4, twin, upper)])
     below_mine = jnp.stack([below, below_one, below_three, below_two])
+    turned, pair, below_mine = lax.optimization_barrier((turned, pair, below_mine))
     one, three, behind, ahead = lax.optimization_barrier(
         (ahead_x(turned), behind_x(turned), ahead_y(pair), behind_y(pair))
     )

time: 227 us -> 227 us (level)
  transfers between devices with their start and end apart: 18 -> 18, of which waited for: 14 -> 14; matrix products, arithmetic and copies ran while one was open for 3% -> 2% of each run, Pallas kernels for 22% -> 22%
where the time goes in v9:
time: 227 us
  waiting for transfers between devices  118 us (52%)
  Pallas kernels  64.2 us (28%)
  starting transfers between devices  36.4 us (16%)
  local copies, waits for them, and re-layouts  6.39 us (3%)
    all_to_all x2, waiting for transfers between devices, exchange(): return lax.all_to_all(parcels.reshape(128, 128, 128), ALL, 0, 0, tiled=True)  70.1 us
    ppermute x16, waiting for transfers between devices, shift(): return lax.ppermute(array, ALL, pairs)  48.1 us
    pallas_call x2, Pallas kernels, place_children(): pl.pallas_call(functools.partial(place_kernel, b), grid_spec=grid_spec, o...  27.7 us
    ppermute x16, starting transfers between devices, shift(): return lax.ppermute(array, ALL, pairs)  23.9 us
    pallas_call x1, Pallas kernels, schur_first(): pl.pallas_call(first_kernel, grid_spec=grid_spec, out_shape=[jax.ShapeDty...  19.7 us
    all_to_all x2, starting transfers between devices, exchange(): return lax.all_to_all(parcels.reshape(128, 128, 128), ALL, 0, 0, tiled=True)  12.5 us
    pallas_call x1, Pallas kernels, schur_second(): pl.pallas_call(schur_kernel, grid=(4,), in_specs=[pl.BlockSpec((2048, 102...  9.69 us
    pallas_call x1, Pallas kernels, lower_right(): pl.pallas_call(right_kernel, grid_spec=grid_spec, out_shape=jax.ShapeDtyp...  7.13 us
  transfers between devices with their start and end apart: 18, of which 14 were waited for; matrix products, arithmetic and copies ran while one was open for 2% of the time, Pallas kernels for 22%

profile of v9, /device:TPU:1, one launch (start us, length us, event | category | flops | bytes accessed | tf_op | source)
XLA Modules:
  0.0 226.9 jit_solution(5850053861989800501)
XLA Ops:
  0.0 1.1 slice_bitcast_fusion.9
  1.1 1.1 fusion.2
  2.2 0.1 pad_maximum_fusion.3
  2.3 4.6 %collective-permute-start = (bf16[3072,128]{1,0:T(8,128)(2,1)S(1)}, bf16[3072,128]{1,0:T(8,128)(2,1)S(1)}, u32[]{:S(2)}, u32[]{:S(2)}) collective-permute-start(bf16[3072,128]{1,0:T(8,128)(2,1)S(1)} %pad_maximum_fusion.3), channel_id=1, source_target_pairs={{0,0},{1,16},{2,8},{3,24},{4,32},{5,48},{6,40},{7,56},{8,1},{9,17}... | collective-permute-start | bytes 2359304 | tf_op jit(solution)/shard_map/ppermute | solution.py:24
  6.9 3.7 %collective-permute-start.1 = (bf16[1024,128]{1,0:T(8,128)(2,1)S(1)}, bf16[1024,128]{1,0:T(8,128)(2,1)S(1)}, u32[]{:S(2)}, u32[]{:S(2)}) collective-permute-start(bf16[1024,128]{1,0:T(8,128)(2,1)S(1)} %get-tuple-element.30), channel_id=1, source_target_pairs={{0,4},{1,5},{2,6},{3,7},{4,0},{5,1},{6,2},{7,3},{8,12},{9,13},{10,... | collective-permute-start | bytes 786440 | tf_op jit(solution)/shard_map/ppermute | solution.py:24
  10.6 1.2 collective-permute-start.4
  11.8 1.2 collective-permute-start.3
  13.0 0.3 collective-permute-start.2
  13.3 3.4 %collective-permute-done.1 = bf16[1024,128]{1,0:T(8,128)(2,1)S(1)} collective-permute-done((bf16[1024,128]{1,0:T(8,128)(2,1)S(1)}, bf16[1024,128]{1,0:T(8,128)(2,1)S(1)}, u32[]{:S(2)}, u32[]{:S(2)}) %collective-permute-start.1) | collective-permute-done | bytes 262176 | tf_op jit(solution)/shard_map/ppermute | solution.py:24
  16.7 7.0 %collective-permute-done.4 = bf16[1024,128]{1,0:T(8,128)(2,1)S(1)} collective-permute-done((bf16[1024,128]{1,0:T(8,128)(2,1)S(1)}, bf16[1024,128]{1,0:T(8,128)(2,1)S(1)}, u32[]{:S(2)}, u32[]{:S(2)}) %collective-permute-start.4) | collective-permute-done | bytes 262176 | tf_op jit(solution)/shard_map/ppermute | solution.py:24
  23.8 9.7 %collective-permute-done.3 = bf16[1024,128]{1,0:T(8,128)(2,1)S(1)} collective-permute-done((bf16[1024,128]{1,0:T(8,128)(2,1)S(1)}, bf16[1024,128]{1,0:T(8,128)(2,1)S(1)}, u32[]{:S(2)}, u32[]{:S(2)}) %collective-permute-start.3) | collective-permute-done | bytes 262176 | tf_op jit(solution)/shard_map/ppermute | solution.py:24
  33.5 0.1 pad_maximum_fusion.5.near_ref
  33.5 0.1 pad_maximum_fusion.1.below_mine_ref
  33.7 3.6 %collective-permute-start.6 = (bf16[3072,128]{1,0:T(8,128)(2,1)S(1)}, bf16[3072,128]{1,0:T(8,128)(2,1)S(1)}, u32[]{:S(2)}, u32[]{:S(2)}) collective-permute-start(bf16[3072,128]{1,0:T(8,128)(2,1)S(1)} %collective-permute-done), channel_id=1, source_target_pairs={{0,48},{1,49},{2,50},{3,51},{4,52},{5,53},{6,54},{7,55},{8,56},{9,... | collective-permute-start | bytes 2359304 | tf_op jit(solution)/shard_map/ppermute | solution.py:24
  37.3 0.2 collective-permute-start.8
  37.5 1.2 collective-permute-start.7
  38.8 0.5 collective-permute-start.13
  39.3 10.7 %collective-permute-done.8.ahead_ref = bf16[2,1024,128]{2,1,0:T(8,128)(2,1)S(1)} collective-permute-done((bf16[2,1024,128]{2,1,0:T(8,128)(2,1)S(1)}, bf16[2,1024,128]{2,1,0:T(8,128)(2,1)S(1)}, u32[]{:S(2)}, u32[]{:S(2)}) %collective-permute-start.8) | collective-permute-done | bytes 524320 | tf_op jit(solution)/shard_map/ppermute | solution.py:24
  50.0 0.9 collective-permute-done.7.behind_ref
  50.8 2.8 %collective-permute-done.6 = bf16[3072,128]{1,0:T(8,128)(2,1)S(1)} collective-permute-done((bf16[3072,128]{1,0:T(8,128)(2,1)S(1)}, bf16[3072,128]{1,0:T(8,128)(2,1)S(1)}, u32[]{:S(2)}, u32[]{:S(2)}) %collective-permute-start.6) | collective-permute-done | bytes 786464 | tf_op jit(solution)/shard_map/ppermute | solution.py:24
  53.7 3.1 %collective-permute-done.5 = bf16[3072,128]{1,0:T(8,128)(2,1)S(1)} collective-permute-done((bf16[3072,128]{1,0:T(8,128)(2,1)S(1)}, bf16[3072,128]{1,0:T(8,128)(2,1)S(1)}, u32[]{:S(2)}, u32[]{:S(2)}) %collective-permute-start.5) | collective-permute-done | bytes 786464 | tf_op jit(solution)/shard_map/ppermute | solution.py:24
  56.8 0.1 collective-permute-start.10
  56.9 1.5 collective-permute-start.9
  58.5 0.4 collective-permute-start.12
  58.9 1.1 collective-permute-start.11
  60.0 0.1 slice_bitcast_fusion
  60.1 2.9 %collective-permute-done.10.far_second_ref = bf16[1024,128]{1,0:T(8,128)(2,1)S(1)} collective-permute-done((bf16[1024,128]{1,0:T(8,128)(2,1)S(1)}, bf16[1024,128]{1,0:T(8,128)(2,1)S(1)}, u32[]{:S(2)}, u32[]{:S(2)}) %collective-permute-start.10) | collective-permute-done | bytes 262176 | tf_op jit(solution)/shard_map/ppermute | solution.py:24
  63.0 1.3 collective-permute-done.9.far_first_ref
  64.3 2.6 %collective-permute-done.12 = bf16[1536,128]{1,0:T(8,128)(2,1)S(1)} collective-permute-done((bf16[1536,128]{1,0:T(8,128)(2,1)S(1)}, bf16[1536,128]{1,0:T(8,128)(2,1)S(1)}, u32[]{:S(2)}, u32[]{:S(2)}) %collective-permute-start.12) | collective-permute-done | bytes 393248 | tf_op jit(solution)/shard_map/ppermute | solution.py:24
  66.9 1.6 collective-permute-done.11
  68.6 0.3 pad_maximum_fusion.mine_ref.inverse_mine_ref
  68.9 3.2 %collective-permute-start.14 = (bf16[4,2048,128]{2,1,0:T(8,128)(2,1)S(1)}, bf16[4,2048,128]{2,1,0:T(8,128)(2,1)}, u32[]{:S(2)}, u32[]{:S(2)}) collective-permute-start(bf16[4,2048,128]{2,1,0:T(8,128)(2,1)S(1)} %pad_maximum_fusion.mine_ref.inverse_mine_ref), channel_id=1, source_target_pairs={{0,8},{1,9},{2,10},{3,11},{4,12},{5,13},{6,14},{7,15},{8,0},{9,1},... | collective-permute-start | bytes 6291464 | tf_op jit(solution)/shard_map/ppermute | solution.py:24
  72.2 0.1 pad_maximum_fusion.2.mine_ref
  72.3 1.0 collective-permute-start.15
  73.4 0.6 stack.77.place_ref
  74.0 2.0 collective-permute-done.14.other_ref.inverse_other_ref
  76.0 19.7 %schur_first.1 = (bf16[16,8,128,128]{3,2,1,0:T(8,128)(2,1)}, bf16[2048,1024]{1,0:T(8,128)(2,1)}) custom-call(s32[5]{0:T(128)} %stack.77.place_ref, bf16[2,1024,128]{2,1,0:T(8,128)(2,1)} %copy-done.3, bf16[2,1024,128]{2,1,0:T(8,128)(2,1)} %copy-done.6, bf16[2,1024,128]{2,1,0:T(8,128)(2,1)} %copy-done.5, bf16[1024,128]{1,0:T(8,128)(2,1)} %copy-done.10, ...), custom_call_target="tpu_custom_call" | custom-call | flops 8589934592 | bytes 20971520 | tf_op jit(solution)/shard_map/schur_first/pallas_call | solution.py:154
  95.7 6.1 %all-to-all-start.1 = ((bf16[128,128,128]{2,1,0:T(8,128)(2,1)}), bf16[128,128,128]{2,1,0:T(8,128)(2,1)}, u32[]{:S(2)}, u32[]{:S(2)}) async-start(bf16[128,128,128]{2,1,0:T(8,128)(2,1)} %bitcast.63), calls=%async_computation.1 | async-start | bytes 8388608 | tf_op jit(solution)/shard_map/all_to_all | solution.py:387
  101.8 7.1 %lower_right.1.right_ref = bf16[1024,1024]{1,0:T(8,128)(2,1)} custom-call(s32[5]{0:T(128)} %stack.77.place_ref, bf16[4,1024,128]{2,1,0:T(8,128)(2,1)} %copy-done.1, bf16[4,1024,128]{2,1,0:T(8,128)(2,1)} %collective-permute-done.15.other_ref, bf16[4,2048,128]{2,1,0:T(8,128)(2,1)} %copy-done, ...), custom_call_target="tpu_custom_call" | custom-call | flops 1610612736 | bytes 6291456 | tf_op jit(solution)/shard_map/lower_right/pallas_call | solution.py:192
  108.9 9.7 %schur_second.1 = bf16[16,8,128,128]{3,2,1,0:T(8,128)(2,1)} custom-call(bf16[2048,1024]{1,0:T(8,128)(2,1)} %get-tuple-element.48.left_ref, bf16[1024,1024]{1,0:T(8,128)(2,1)} %lower_right.1.right_ref, bf16[2048,2048]{1,0:T(8,128)(2,1)} %bitcast.60, bf16[2048,2048]{1,0:T(8,128)(2,1)} %bitcast.61), custom_call_target="tpu_custom_call" | custom-call | flops 4294967296 | bytes 14680064 | tf_op jit(solution)/shard_map/schur_second/pallas_call | solution.py:209
  118.6 35.6 %all-to-all-done.1.schur_in_ref = bf16[128,128,128]{2,1,0:T(8,128)(2,1)} async-done(((bf16[128,128,128]{2,1,0:T(8,128)(2,1)}), bf16[128,128,128]{2,1,0:T(8,128)(2,1)}, u32[]{:S(2)}, u32[]{:S(2)}) %all-to-all-start.1) | async-done | bytes 4194336 | tf_op jit(solution)/shard_map/all_to_all | solution.py:387
  154.2 6.5 %all-to-all-start = ((bf16[128,128,128]{2,1,0:T(8,128)(2,1)}), bf16[128,128,128]{2,1,0:T(8,128)(2,1)}, u32[]{:S(2)}, u32[]{:S(2)}) async-start(bf16[128,128,128]{2,1,0:T(8,128)(2,1)} %bitcast.62), calls=%async_computation | async-start | bytes 8388608 | tf_op jit(solution)/shard_map/all_to_all | solution.py:387
  160.7 0.1 fusion.1
  160.8 3.3 %reshape.42.col_map_ref = s32[2,2,1024,1]{3,2,1,0:T(8,128)} reshape(s32[2,2,8,128]{3,2,1,0:T(8,128)S(1)} %fusion.1) | data formatting | bytes 32768 | tf_op jit(solution)/shard_map/reshape | solution.py:384
  164.1 0.6 broadcast_subtract_fusion
  164.7 13.8 %place.2.refs_0_ = f32[1024,2048]{1,0:T(8,128)} custom-call(s32[5]{0:T(128)} %stack.77.place_ref, bf16[128,128,128]{2,1,0:T(8,128)(2,1)} %all-to-all-done.1.schur_in_ref, s32[2,1,1024]{2,1,0:T(1,128)} %bitcast.76, s32[2,2,1024,1]{3,2,1,0:T(8,128)} %reshape.42.col_map_ref, bf16[1024,2048]{1,0:T(8,128)(2,1)} %base_ref.3), custom_call_target="tpu_custom_call" | custom-call | flops 8589934592 | bytes 10485760 | tf_op jit(solution)/shard_map/place/pallas_call | solution.py:284
  178.5 34.5 %all-to-all-done.schur_in_ref = bf16[128,128,128]{2,1,0:T(8,128)(2,1)} async-done(((bf16[128,128,128]{2,1,0:T(8,128)(2,1)}), bf16[128,128,128]{2,1,0:T(8,128)(2,1)}, u32[]{:S(2)}, u32[]{:S(2)}) %all-to-all-start) | async-done | bytes 4194336 | tf_op jit(solution)/shard_map/all_to_all | solution.py:387
  213.0 13.9 %place.3 = f32[1024,2048]{1,0:T(8,128)} custom-call(s32[5]{0:T(128)} %stack.77.place_ref, bf16[128,128,128]{2,1,0:T(8,128)(2,1)} %all-to-all-done.schur_in_ref, s32[2,1,1024]{2,1,0:T(1,128)} %bitcast.77, s32[2,2,1024,1]{3,2,1,0:T(8,128)} %reshape.42.col_map_ref, bf16[1024,2048]{1,0:T(8,128)(2,1)} %base_ref.3, ...), custom_call_target="tpu_custom_call", output_to_operand_aliasing={{}: (5, {})} | custom-call | flops 8589934592 | bytes 10485760 | tf_op jit(solution)/shard_map/place/pallas_call | solution.py:284
  (41 shorter events, 0.4 us)
Async XLA Ops:
  0.0 2.2 copy-start.4
  2.3 31.4 %collective-permute-start = (bf16[3072,128]{1,0:T(8,128)(2,1)S(1)}, bf16[3072,128]{1,0:T(8,128)(2,1)S(1)}, u32[]{:S(2)}, u32[]{:S(2)}) collective-permute-start(bf16[3072,128]{1,0:T(8,128)(2,1)S(1)} %pad_maximum_fusion.3), channel_id=1, source_target_pairs={{0,0},{1,16},{2,8},{3,24},{4,32},{5,48},{6,40},{7,56},{8,1},{9,17}... | collective-permute-start | bytes 2359304 | tf_op jit(solution)/shard_map/ppermute | solution.py:24
  6.9 9.9 %collective-permute-start.1 = (bf16[1024,128]{1,0:T(8,128)(2,1)S(1)}, bf16[1024,128]{1,0:T(8,128)(2,1)S(1)}, u32[]{:S(2)}, u32[]{:S(2)}) collective-permute-start(bf16[1024,128]{1,0:T(8,128)(2,1)S(1)} %get-tuple-element.30), channel_id=1, source_target_pairs={{0,4},{1,5},{2,6},{3,7},{4,0},{5,1},{6,2},{7,3},{8,12},{9,13},{10,... | collective-permute-start | bytes 786440 | tf_op jit(solution)/shard_map/ppermute | solution.py:24
  10.6 13.2 %collective-permute-start.4 = (bf16[1024,128]{1,0:T(8,128)(2,1)S(1)}, bf16[1024,128]{1,0:T(8,128)(2,1)S(1)}, u32[]{:S(2)}, u32[]{:S(2)}) collective-permute-start(bf16[1024,128]{1,0:T(8,128)(2,1)S(1)} %get-tuple-element.31), channel_id=1, source_target_pairs={{0,2},{1,3},{2,0},{3,1},{4,6},{5,7},{6,4},{7,5},{8,10},{9,11},{10,... | collective-permute-start | bytes 786440 | tf_op jit(solution)/shard_map/ppermute | solution.py:24
  11.8 21.6 %collective-permute-start.3 = (bf16[1024,128]{1,0:T(8,128)(2,1)S(1)}, bf16[1024,128]{1,0:T(8,128)(2,1)S(1)}, u32[]{:S(2)}, u32[]{:S(2)}) collective-permute-start(bf16[1024,128]{1,0:T(8,128)(2,1)S(1)} %get-tuple-element.31), channel_id=1, source_target_pairs={{0,3},{1,0},{2,1},{3,2},{4,7},{5,4},{6,5},{7,6},{8,11},{9,8},{10,9... | collective-permute-start | bytes 786440 | tf_op jit(solution)/shard_map/ppermute | solution.py:24
  13.0 20.4 %collective-permute-start.2 = (bf16[1024,128]{1,0:T(8,128)(2,1)S(1)}, bf16[1024,128]{1,0:T(8,128)(2,1)S(1)}, u32[]{:S(2)}, u32[]{:S(2)}) collective-permute-start(bf16[1024,128]{1,0:T(8,128)(2,1)S(1)} %get-tuple-element.31), channel_id=1, source_target_pairs={{0,1},{1,2},{2,3},{3,0},{4,5},{5,6},{6,7},{7,4},{8,9},{9,10},{10,1... | collective-permute-start | bytes 786440 | tf_op jit(solution)/shard_map/ppermute | solution.py:24
  33.5 23.4 %copy-start.3 = (bf16[2,1024,128]{2,1,0:T(8,128)(2,1)}, bf16[2,1024,128]{2,1,0:T(8,128)(2,1)S(1)}, u32[]{:S(2)}) copy-start(bf16[2,1024,128]{2,1,0:T(8,128)(2,1)S(1)} %pad_maximum_fusion.5.near_ref) | copy-start | bytes 1572868
  33.7 26.5 %copy-start.2 = (bf16[4,1024,128]{2,1,0:T(8,128)(2,1)}, bf16[4,1024,128]{2,1,0:T(8,128)(2,1)S(1)}, u32[]{:S(2)}) copy-start(bf16[4,1024,128]{2,1,0:T(8,128)(2,1)S(1)} %pad_maximum_fusion.1.below_mine_ref) | copy-start | bytes 3145732
  33.7 20.0 %collective-permute-start.6 = (bf16[3072,128]{1,0:T(8,128)(2,1)S(1)}, bf16[3072,128]{1,0:T(8,128)(2,1)S(1)}, u32[]{:S(2)}, u32[]{:S(2)}) collective-permute-start(bf16[3072,128]{1,0:T(8,128)(2,1)S(1)} %collective-permute-done), channel_id=1, source_target_pairs={{0,48},{1,49},{2,50},{3,51},{4,52},{5,53},{6,54},{7,55},{8,56},{9,... | collective-permute-start | bytes 2359304 | tf_op jit(solution)/shard_map/ppermute | solution.py:24
  37.3 19.5 %collective-permute-start.5 = (bf16[3072,128]{1,0:T(8,128)(2,1)S(1)}, bf16[3072,128]{1,0:T(8,128)(2,1)S(1)}, u32[]{:S(2)}, u32[]{:S(2)}) collective-permute-start(bf16[3072,128]{1,0:T(8,128)(2,1)S(1)} %collective-permute-done), channel_id=1, source_target_pairs={{0,16},{1,17},{2,18},{3,19},{4,20},{5,21},{6,22},{7,23},{8,24},{9,... | collective-permute-start | bytes 2359304 | tf_op jit(solution)/shard_map/ppermute | solution.py:24
  37.3 12.7 %collective-permute-start.8 = (bf16[2,1024,128]{2,1,0:T(8,128)(2,1)S(1)}, bf16[2,1024,128]{2,1,0:T(8,128)(2,1)S(1)}, u32[]{:S(2)}, u32[]{:S(2)}) collective-permute-start(bf16[2,1024,128]{2,1,0:T(8,128)(2,1)S(1)} %pad_maximum_fusion.5.near_ref), channel_id=1, source_target_pairs={{0,3},{1,0},{2,1},{3,2},{4,7},{5,4},{6,5},{7,6},{8,11},{9,8},{10,9... | collective-permute-start | bytes 1572872 | tf_op jit(solution)/shard_map/ppermute | solution.py:24
  37.5 13.3 %collective-permute-start.7 = (bf16[2,1024,128]{2,1,0:T(8,128)(2,1)S(1)}, bf16[2,1024,128]{2,1,0:T(8,128)(2,1)S(1)}, u32[]{:S(2)}, u32[]{:S(2)}) collective-permute-start(bf16[2,1024,128]{2,1,0:T(8,128)(2,1)S(1)} %pad_maximum_fusion.5.near_ref), channel_id=1, source_target_pairs={{0,1},{1,2},{2,3},{3,0},{4,5},{5,6},{6,7},{7,4},{8,9},{9,10},{10,1... | collective-permute-start | bytes 1572872 | tf_op jit(solution)/shard_map/ppermute | solution.py:24
  38.8 25.6 %collective-permute-start.13 = (bf16[4,1024,128]{2,1,0:T(8,128)(2,1)S(1)}, bf16[4,1024,128]{2,1,0:T(8,128)(2,1)S(1)}, u32[]{:S(2)}, u32[]{:S(2)}) collective-permute-start(bf16[4,1024,128]{2,1,0:T(8,128)(2,1)S(1)} %pad_maximum_fusion.1.below_mine_ref), channel_id=1, source_target_pairs={{0,4},{1,5},{2,6},{3,7},{4,0},{5,1},{6,2},{7,3},{8,12},{9,13},{10,... | collective-permute-start | bytes 3145736 | tf_op jit(solution)/shard_map/ppermute | solution.py:24
  50.0 7.0 %copy-start.5 = (bf16[2,1024,128]{2,1,0:T(8,128)(2,1)}, bf16[2,1024,128]{2,1,0:T(8,128)(2,1)S(1)}, u32[]{:S(2)}) copy-start(bf16[2,1024,128]{2,1,0:T(8,128)(2,1)S(1)} %collective-permute-done.8.ahead_ref) | copy-start | bytes 1572868
  50.8 7.6 %copy-start.6 = (bf16[2,1024,128]{2,1,0:T(8,128)(2,1)}, bf16[2,1024,128]{2,1,0:T(8,128)(2,1)S(1)}, u32[]{:S(2)}) copy-start(bf16[2,1024,128]{2,1,0:T(8,128)(2,1)S(1)} %collective-permute-done.7.behind_ref) | copy-start | bytes 1572868
  56.8 6.2 %collective-permute-start.10 = (bf16[1024,128]{1,0:T(8,128)(2,1)S(1)}, bf16[1024,128]{1,0:T(8,128)(2,1)S(1)}, u32[]{:S(2)}, u32[]{:S(2)}) collective-permute-start(bf16[1024,128]{1,0:T(8,128)(2,1)S(1)} %slice_bitcast_fusion.7), channel_id=1, source_target_pairs={{0,3},{1,0},{2,1},{3,2},{4,7},{5,4},{6,5},{7,6},{8,11},{9,8},{10,9... | collective-permute-start | bytes 786440 | tf_op jit(solution)/shard_map/ppermute | solution.py:24
  56.9 7.4 %collective-permute-start.9 = (bf16[1024,128]{1,0:T(8,128)(2,1)S(1)}, bf16[1024,128]{1,0:T(8,128)(2,1)S(1)}, u32[]{:S(2)}, u32[]{:S(2)}) collective-permute-start(bf16[1024,128]{1,0:T(8,128)(2,1)S(1)} %slice_bitcast_fusion.8), channel_id=1, source_target_pairs={{0,1},{1,2},{2,3},{3,0},{4,5},{5,6},{6,7},{7,4},{8,9},{9,10},{10,1... | collective-permute-start | bytes 786440 | tf_op jit(solution)/shard_map/ppermute | solution.py:24
  58.5 8.4 %collective-permute-start.12 = (bf16[1536,128]{1,0:T(8,128)(2,1)S(1)}, bf16[1536,128]{1,0:T(8,128)(2,1)S(1)}, u32[]{:S(2)}, u32[]{:S(2)}) collective-permute-start(bf16[1536,128]{1,0:T(8,128)(2,1)S(1)} %slice.55), channel_id=1, source_target_pairs={{0,48},{1,49},{2,50},{3,51},{4,52},{5,53},{6,54},{7,55},{8,56},{9,... | collective-permute-start | bytes 1179656 | tf_op jit(solution)/shard_map/ppermute | solution.py:24
  58.9 9.6 %collective-permute-start.11 = (bf16[1536,128]{1,0:T(8,128)(2,1)S(1)}, bf16[1536,128]{1,0:T(8,128)(2,1)S(1)}, u32[]{:S(2)}, u32[]{:S(2)}) collective-permute-start(bf16[1536,128]{1,0:T(8,128)(2,1)S(1)} %slice.54), channel_id=1, source_target_pairs={{0,16},{1,17},{2,18},{3,19},{4,20},{5,21},{6,22},{7,23},{8,24},{9,... | collective-permute-start | bytes 1179656 | tf_op jit(solution)/shard_map/ppermute | solution.py:24
  63.0 5.9 %copy-start.9 = (bf16[1024,128]{1,0:T(8,128)(2,1)}, bf16[1024,128]{1,0:T(8,128)(2,1)S(1)}, u32[]{:S(2)}) copy-start(bf16[1024,128]{1,0:T(8,128)(2,1)S(1)} %collective-permute-done.10.far_second_ref) | copy-start | bytes 786436
  64.3 7.8 %copy-start.10 = (bf16[1024,128]{1,0:T(8,128)(2,1)}, bf16[1024,128]{1,0:T(8,128)(2,1)S(1)}, u32[]{:S(2)}) copy-start(bf16[1024,128]{1,0:T(8,128)(2,1)S(1)} %collective-permute-done.9.far_first_ref) | copy-start | bytes 786436
  64.3 4.2 %copy-start.8 = (bf16[4,1024,128]{2,1,0:T(8,128)(2,1)}, bf16[4,1024,128]{2,1,0:T(8,128)(2,1)S(1)}, u32[]{:S(2)}) copy-start(bf16[4,1024,128]{2,1,0:T(8,128)(2,1)S(1)} %collective-permute-done.13.below_other_ref) | copy-start | bytes 3145732
  68.8 3.5 %copy-start = (bf16[4,2048,128]{2,1,0:T(8,128)(2,1)}, bf16[4,2048,128]{2,1,0:T(8,128)(2,1)S(1)}, u32[]{:S(2)}) copy-start(bf16[4,2048,128]{2,1,0:T(8,128)(2,1)S(1)} %pad_maximum_fusion.mine_ref.inverse_mine_ref) | copy-start | bytes 6291460
  68.9 7.1 %collective-permute-start.14 = (bf16[4,2048,128]{2,1,0:T(8,128)(2,1)S(1)}, bf16[4,2048,128]{2,1,0:T(8,128)(2,1)}, u32[]{:S(2)}, u32[]{:S(2)}) collective-permute-start(bf16[4,2048,128]{2,1,0:T(8,128)(2,1)S(1)} %pad_maximum_fusion.mine_ref.inverse_mine_ref), channel_id=1, source_target_pairs={{0,8},{1,9},{2,10},{3,11},{4,12},{5,13},{6,14},{7,15},{8,0},{9,1},... | collective-permute-start | bytes 6291464 | tf_op jit(solution)/shard_map/ppermute | solution.py:24
  72.3 23.4 %copy-start.1 = (bf16[4,1024,128]{2,1,0:T(8,128)(2,1)}, bf16[4,1024,128]{2,1,0:T(8,128)(2,1)S(1)}, u32[]{:S(2)}) copy-start(bf16[4,1024,128]{2,1,0:T(8,128)(2,1)S(1)} %pad_maximum_fusion.2.mine_ref) | copy-start | bytes 3145732
  72.3 23.4 %collective-permute-start.15 = (bf16[4,1024,128]{2,1,0:T(8,128)(2,1)S(1)}, bf16[4,1024,128]{2,1,0:T(8,128)(2,1)}, u32[]{:S(2)}, u32[]{:S(2)}) collective-permute-start(bf16[4,1024,128]{2,1,0:T(8,128)(2,1)S(1)} %pad_maximum_fusion.2.mine_ref), channel_id=1, source_target_pairs={{0,8},{1,9},{2,10},{3,11},{4,12},{5,13},{6,14},{7,15},{8,0},{9,1},... | collective-permute-start | bytes 3145736 | tf_op jit(solution)/shard_map/ppermute | solution.py:24
  95.7 58.5 %all-to-all-start.1 = ((bf16[128,128,128]{2,1,0:T(8,128)(2,1)}), bf16[128,128,128]{2,1,0:T(8,128)(2,1)}, u32[]{:S(2)}, u32[]{:S(2)}) async-start(bf16[128,128,128]{2,1,0:T(8,128)(2,1)} %bitcast.63), calls=%async_computation.1 | async-start | bytes 8388608 | tf_op jit(solution)/shard_map/all_to_all | solution.py:387
  154.2 6.5 %copy-start.7 = (s32[2,16384]{1,0:T(2,128)S(1)}, s32[2,16384]{1,0:T(2,128)}, u32[]{:S(2)}) copy-start(s32[2,16384]{1,0:T(2,128)} %param.8) | copy-start | bytes 393220
  154.2 58.9 %all-to-all-start = ((bf16[128,128,128]{2,1,0:T(8,128)(2,1)}), bf16[128,128,128]{2,1,0:T(8,128)(2,1)}, u32[]{:S(2)}, u32[]{:S(2)}) async-start(bf16[128,128,128]{2,1,0:T(8,128)(2,1)} %bitcast.62), calls=%async_computation | async-start | bytes 8388608 | tf_op jit(solution)/shard_map/all_to_all | solution.py:387
